TPU v7x, 128 devices: a whole 4x4x4 slice. The times are simulated.
128 devices in a mesh: group: 8 (over x, z_lo), seq: 16 (over z_hi, y, core).
Axes of the slice: x: 4, y: 4, z: 4 (z_hi: 2, z_lo: 2; z = z_hi * 2 + z_lo), core: 2. Of those that a mesh axis runs over, the one named last changes fastest.
Arguments:
- queries: bfloat16 [576, 24576], P(None, 'seq'), may hold values from -13 to 13
- prefix_latent: bfloat16 [8192, 576], P(('group', 'seq')), may hold values from -6 to 6
- tail_latent: bfloat16 [576, 256, 576], P('group', 'seq'), may hold values from -6 to 6
- tail_length: int32 [576], P('group'), may hold values from 1 to 256, 73728 in all
- slot_request: int32 [576], P('group'), may hold values from 0 to 575, each once
- key_absorb: bfloat16 [128, 128, 512], P('seq'), may hold values from -0.5 to 0.5
- value_up: bfloat16 [128, 512, 128], P('seq'), may hold values from -0.25 to 0.25
- out_proj: bfloat16 [16384, 7168], P('seq'), may hold values from -0.75 to 0.75
Outputs:
- mixed: bfloat16 [576, 7168], P('group', 'seq')
All inputs are finite; a program needn't handle non-finite values. No bound on the sum of `tail_length` on one device may be relied on, other than what follows from the above.
Results may differ from a plain program's by a relative error of at most 0.02.
Values may be sent and summed in bfloat16 or wider, within the bound.
No kernel may reach another device: no remote copies, remote signals or barrier semaphores. Data moves between devices by JAX's collectives and lax.ppermute only.
A program may use at most 192 MiB of HBM per device.

v0:
```python
import math

import jax
import jax.numpy as jnp
from jax import lax
from jax.sharding import PartitionSpec as P

masked_fill = -1e30


def fold_step(running, scores, usable, latent, einsum_form):
    highest, weight_sum, context_sum = running
    masked = jnp.where(usable, scores, masked_fill)
    new_highest = jnp.maximum(highest, jnp.max(masked, axis=2))
    weights = jnp.where(usable, jnp.exp(masked - new_highest[:, :, None]), 0.0)
    increment = jnp.einsum(
        einsum_form, weights.astype(jnp.bfloat16), latent, preferred_element_type=jnp.float32
    )
    return (new_highest, jnp.sum(weights, axis=2), increment)


def join_parts(former, latter):
    highest = jnp.maximum(former[0], latter[0])
    former_scale = jnp.exp(former[0] - highest)
    latter_scale = jnp.exp(latter[0] - highest)
    return (
        highest,
        former[1] * former_scale + latter[1] * latter_scale,
        former[2] * former_scale[:, :, None] + latter[2] * latter_scale[:, :, None],
    )


def empty_running(req_rows, head_count, latent_width):
    return (
        jnp.full((req_rows, head_count), masked_fill, jnp.float32),
        jnp.zeros((req_rows, head_count), jnp.float32),
        jnp.zeros((req_rows, head_count, latent_width), jnp.float32),
    )


def on_device(
    queries, prefix_latent, tail_latent, tail_length, slot_request, key_absorb, value_up, out_proj
):
    heads_here, nope_width, latent_width = key_absorb.shape
    value_width = value_up.shape[2]
    req_rows = slot_request.shape[0]
    rope_width = prefix_latent.shape[1] - latent_width
    score_scale = 1.0 / math.sqrt(nope_width + rope_width)
    picked = jnp.take(queries, slot_request, axis=0).reshape(
        req_rows, heads_here, nope_width + rope_width
    )
    query_latent = jnp.einsum(
        "rhn,hnl->rhl", picked[:, :, :nope_width], key_absorb, preferred_element_type=jnp.float32
    ).astype(jnp.bfloat16)
    query_full = jnp.concatenate([query_latent, picked[:, :, nope_width:]], axis=2)
    start_state = empty_running(req_rows, heads_here, latent_width)
    shard_keys = lax.all_gather(prefix_latent, ("group", "seq"), axis=0, tiled=True)
    scores = (
        jnp.einsum("rhc,kc->rhk", query_full, shard_keys, preferred_element_type=jnp.float32)
        * score_scale
    )
    prefix_part = fold_step(start_state, scores, True, shard_keys[:, :latent_width], "rhk,kl->rhl")
    shard_keys = lax.all_gather(tail_latent, "seq", axis=1, tiled=True)
    scores = (
        jnp.einsum("rhc,rkc->rhk", query_full, shard_keys, preferred_element_type=jnp.float32)
        * score_scale
    )
    position = jnp.arange(shard_keys.shape[1], dtype=jnp.int32)
    usable = (position[None, :] < tail_length[:, None])[:, None, :]
    tail_part = fold_step(
        start_state, scores, usable, shard_keys[:, :, :latent_width], "rhk,rkl->rhl"
    )
    highest, weight_sum, context_sum = join_parts(prefix_part, tail_part)
    context = (context_sum / weight_sum[:, :, None]).astype(jnp.bfloat16)
    head_out = jnp.einsum(
        "rhl,hlv->rhv", context, value_up, preferred_element_type=jnp.float32
    ).astype(jnp.bfloat16)
    head_out = head_out.reshape(req_rows, heads_here * value_width)
    partial_value = jnp.dot(head_out, out_proj, preferred_element_type=jnp.float32)
    return lax.psum_scatter(
        partial_value.astype(jnp.bfloat16), "seq", scatter_dimension=1, tiled=True
    )


def solution(mesh):
    placed = (
        P(None, "seq"),
        P(("group", "seq"), None),
        P("group", "seq", None),
        P("group"),
        P("group"),
        P("seq", None, None),
        P("seq", None, None),
        P("seq", None),
    )
    return jax.shard_map(
        on_device, mesh=mesh, in_specs=placed, out_specs=P("group", "seq"), check_vma=False
    )
```

profile of v0, /device:TPU:0, one launch (start us, length us, event | category | flops | bytes accessed | tf_op | source)
XLA Modules:
  0.0 476.8 jit_solution(7657145339572840276)
XLA Ops:
  6.5 0.7 all-gather.3.cloned.1.call-update
  7.3 0.7 all-gather.5.cloned.1.call-update
  8.0 0.0 reduce-scatter.4.cloned.1.call-start
  8.1 0.7 compare_select_fusion
  8.7 0.7 gather_fusion
  9.5 0.2 gather.7
  9.7 0.7 compare_and_fusion
  10.4 0.1 copy_select_fusion
  10.5 1.5 fusion.19
  12.1 0.1 pad_maximum_fusion
  12.1 1.3 iota_compare_fusion
  13.5 204.9 %all-gather.3.cloned.1.call-done = bf16[8192,576]{1,0:T(8,128)(2,1)} async-done(((bf16[64,576]{1,0:T(8,128)(2,1)}), bf16[8192,576]{1,0:T(8,128)(2,1)}) %all-gather.3.cloned.1.call-update) | async-done | bytes 9437200 | tf_op jit(solution)/shard_map/all_gather | solution.py:57
  218.4 17.9 %multiply_reduce_fusion = (f32[72,8]{1,0:T(8,128)S(1)}, f32[72,8,8192]{2,1,0:T(8,128)}) fusion(bf16[8192,576]{1,0:T(8,128)(2,1)} %all-gather.3.cloned.1.call-done, bf16[72,8,576]{2,0,1:T(8,128)(2,1)S(1)} %pad_maximum_fusion), kind=kOutput, calls=%fused_computation.4 | convolution fusion | flops 5445254656 | bytes 28977408 | tf_op jit(solution)/shard_map/rhc,kc->rhk/dot_general | solution.py:59
  236.2 9.7 %fusion.2 = f32[72,8]{1,0:T(8,128)S(1)} fusion(f32[72,8,8192]{2,1,0:T(8,128)} %get-tuple-element.9, f32[72,8]{1,0:T(8,128)S(1)} %broadcast_maximum_fusion.1), kind=kLoop, calls=%fused_computation.5 | loop fusion | flops 14155200 | bytes 18878976 | tf_op jit(solution)/shard_map/reduce_sum | solution.py:19
  245.9 114.2 %all-gather.5.cloned.1.call-done = bf16[72,256,576]{2,1,0:T(8,128)(2,1)} async-done(((bf16[72,16,576]{2,1,0:T(8,128)(2,1)}), bf16[72,256,576]{2,1,0:T(8,128)(2,1)}) %all-gather.5.cloned.1.call-update) | async-done | bytes 21233680 | tf_op jit(solution)/shard_map/all_gather | solution.py:63
  360.2 10.9 %fusion.42 = (f32[72,8]{1,0:T(8,128)S(1)}, f32[72,8,256]{2,1,0:T(8,128)S(1)}) fusion(bf16[72,256,576]{2,1,0:T(8,128)(2,1)} %all-gather.5.cloned.1.call-done, bf16[72,8,576]{2,0,1:T(8,128)(2,1)S(1)} %pad_maximum_fusion, pred[72,256]{1,0:T(8,128)(4,1)S(1)} %copy-done.3), kind=kOutput, calls=%fused_computation.51 | convolution fusion | flops 170311104 | bytes 22507776 | tf_op jit(solution)/shard_map/rhc,rkc->rhk/dot_general | solution.py:65
  371.1 0.3 fusion.27
  371.4 11.4 %fusion.10 = f32[72,8,512]{2,1,0:T(8,128)S(1)} fusion(bf16[8192,576]{1,0:T(8,128)(2,1)} %all-gather.3.cloned.1.call-done, f32[72,8,8192]{2,1,0:T(8,128)} %get-tuple-element.9, f32[72,8]{1,0:T(8,128)S(1)} %broadcast_maximum_fusion.1, f32[72,8]{1,0:T(8,128)S(1)} %get-tuple-element.7), kind=kOutput, calls=%fused_computation.14 | convolution fusion | flops 4846288896 | bytes 28447232 | tf_op jit(solution)/shard_map/rhk,kl->rhl/dot_general | solution.py:16
  382.9 8.0 %divide_convert_fusion = bf16[72,8,512]{2,1,0:T(8,128)(2,1)S(1)} fusion(f32[72,8,512]{2,1,0:T(8,128)S(1)} %fusion.10, bf16[72,256,576]{2,1,0:T(8,128)(2,1)} %all-gather.5.cloned.1.call-done, f32[72,8]{1,0:T(8,128)S(1)} %get-tuple-element.5, f32[72,8]{1,0:T(8,128)S(1)} %get-tuple-element.6, f32[72,8,256]{2,1,0:T(8,128)S(1)} %get-tuple-element.11, ...), kind=kOutput, calls=%fused_computation.21 | convolution fusion | flops 152616960 | bytes 21259008 | tf_op jit(solution)/shard_map/rhk,rkl->rhl/dot_general | solution.py:16
  390.9 0.4 fusion.21
  391.4 7.9 %convolution_convert_fusion = bf16[72,7168]{1,0:T(8,128)(2,1)S(1)} fusion(bf16[1024,7168]{1,0:T(8,128)(2,1)} %param.15, bf16[8,9,8,128]{3,2,1,0:T(8,128)(2,1)S(1)} %fusion.21), kind=kOutput, calls=%fused_computation.13 | convolution fusion | flops 1057480704 | bytes 15859712 | tf_op jit(solution)/shard_map/dot_general | solution.py:79
  399.3 1.7 copy.26
  401.0 67.6 %reduce-scatter.4.cloned.1.call-done = bf16[448,72]{1,0:T(8,128)(2,1)} async-done(((bf16[7168,72]{1,0:T(8,128)(2,1)}), bf16[448,72]{1,0:T(8,128)(2,1)}) %reduce-scatter.4.cloned.1.call-update) | async-done | bytes 64528
  468.6 1.6 copy.27
  (16 shorter events, 0.2 us)
Async XLA Ops:
  6.5 2.2 copy-start
  6.5 211.8 %all-gather.3.cloned.1.call-start = ((), (), s32[]{:S(2)}) async-start(), calls=%async_computation.1 | async-start | bytes 10567680 | tf_op jit(solution)/shard_map/all_gather | solution.py:57
  7.3 352.9 %all-gather.5.cloned.1.call-start = ((), (), s32[]{:S(2)}) async-start(), calls=%async_computation.2 | async-start | bytes 25067520 | tf_op jit(solution)/shard_map/all_gather | solution.py:63
  8.0 460.6 %reduce-scatter.4.cloned.1.call-start = ((), (), s32[]{:S(2)}) async-start(), calls=%async_computation.3 | async-start | bytes 1949696
  236.2 123.9 %copy-start.3 = (pred[72,256]{1,0:T(8,128)(4,1)S(1)}, pred[72,256]{1,0:T(8,128)(4,1)}, u32[]{:S(2)}) copy-start(pred[72,256]{1,0:T(8,128)(4,1)} %iota_compare_fusion) | copy-start | bytes 55300
  382.9 8.1 %copy-start.2 = (bf16[8,512,128]{2,1,0:T(8,128)(2,1)S(1)}, bf16[8,512,128]{2,1,0:T(8,128)(2,1)}, u32[]{:S(2)}) copy-start(bf16[8,512,128]{2,1,0:T(8,128)(2,1)} %param.14) | copy-start | bytes 3145732
  390.9 79.3 %copy-start.1 = (bf16[576,1536]{1,0:T(8,128)(2,1)S(1)}, bf16[576,1536]{1,0:T(8,128)(2,1)}, u32[]{:S(2)}) copy-start(bf16[576,1536]{1,0:T(8,128)(2,1)} %param.8) | copy-start | bytes 5308420
Sparse Core Ops, SparseCore 0:
  9.1 209.2 all-gather.2
  220.8 139.2 all-gather.4
  401.1 67.4 reduce-scatter.3
where the time goes:
time: 477 us
  waiting for transfers between devices  388 us (81%)
  matrix products  58.2 us (12%)
  between operations  13.2 us (3%)
  other arithmetic  12.9 us (3%)
    all_gather x1, waiting for transfers between devices, on_device(): lax.all_gather(prefix_latent, ('group', 'seq'), axis=0, tiled=True)  205 us
    all_gather x1, waiting for transfers between devices, on_device(): shard_keys = lax.all_gather(tail_latent, 'seq', axis=1, tiled=True)  114 us
    unnamed x4, waiting for transfers between devices  69 us
    dot_general x2, matrix products, fold_step(): jnp.einsum(einsum_form, weights.astype(jnp.bfloat16), latent, preferred_e...  19.5 us
    dot_general x1, matrix products, on_device(): jnp.einsum('rhc,kc->rhk', query_full, shard_keys, preferred_element_type=...  17.9 us
    dot_general x1, matrix products, on_device(): jnp.einsum('rhc,rkc->rhk', query_full, shard_keys, preferred_element_type...  10.9 us
    reduce_sum x2, other arithmetic, fold_step(): return (new_highest, jnp.sum(weights, axis=2), increment)  9.98 us
  transfers between devices with their start and end apart: 3, of which 3 were waited for; matrix products, arithmetic and copies ran while one was open for 7% of the time, Pallas kernels for 0%

commit v1 on v0

v1 whole, which is shorter than its diff:
```python
import functools
import math

import jax
import jax.numpy as jnp
from jax import lax
from jax.experimental import pallas as pl
from jax.experimental.pallas import tpu as pltpu
from jax.sharding import Mesh, PartitionSpec as P

ROW_BLOCK = 192


def attend_kernel(
    first, last, width, exponent_scale, key_count, q_ref, *refs
):
    key_refs = refs[:key_count]
    refs = refs[key_count:]
    q = q_ref[...]
    scores = [
        lax.dot_general(
            q, k_ref[...], (((1,), (1,)), ((), ())), preferred_element_type=jnp.float32
        )
        for k_ref in key_refs
    ]
    highest = functools.reduce(
        jnp.maximum, [jnp.max(s, axis=1, keepdims=True) for s in scores]
    )
    if not first:
        stat_ref, acc_ref = refs[:2]
        refs = refs[2:]
        old_highest = stat_ref[:, 0:1]
        old_sum = stat_ref[:, 128:129]
        highest = jnp.maximum(highest, old_highest)
        fade = jnp.exp2((old_highest - highest) * exponent_scale)
    weight_sum = None
    acc = None
    for s, k_ref in zip(scores, key_refs):
        w = jnp.exp2((s - highest) * exponent_scale)
        part_sum = jnp.sum(w, axis=1, keepdims=True)
        part = jnp.dot(
            w.astype(jnp.bfloat16), k_ref[:, :width], preferred_element_type=jnp.float32
        )
        weight_sum = part_sum if weight_sum is None else weight_sum + part_sum
        acc = part if acc is None else acc + part
    if not first:
        weight_sum = weight_sum + old_sum * fade
        acc = acc + acc_ref[...] * fade
    if not last:
        out_stat_ref, out_acc_ref = refs
        out_stat_ref[:, :128] = jnp.broadcast_to(highest, (q.shape[0], 128))
        out_stat_ref[:, 128:] = jnp.broadcast_to(weight_sum, (q.shape[0], 128))
        out_acc_ref[...] = acc
    else:
        (out_ref,) = refs
        pack_context(out_ref, acc, weight_sum, highest, exponent_scale, width)


def pack_context(out_ref, acc, weight_sum, highest, exponent_scale, width):
    rows = acc.shape[0]
    out_ref[:, :width] = (acc / weight_sum).astype(jnp.bfloat16)
    level = highest * exponent_scale + jnp.log2(weight_sum)
    high = level.astype(jnp.bfloat16)
    rest = level - high.astype(jnp.float32)
    middle = rest.astype(jnp.bfloat16)
    low = rest - middle.astype(jnp.float32)
    lane = lax.broadcasted_iota(jnp.int32, (rows, 128), 1)
    packed = jnp.where(
        lane == 0,
        high.astype(jnp.float32),
        jnp.where(lane == 1, middle.astype(jnp.float32), jnp.where(lane == 2, low, 0.0)),
    )
    out_ref[:, width:] = packed.astype(jnp.bfloat16)


def attend(q, keys, state, last, width, exponent_scale):
    rows, features = q.shape
    first = state is None
    row_map = lambda i: (i, 0)
    all_map = lambda i: (0, 0)
    in_specs = [pl.BlockSpec((ROW_BLOCK, features), row_map)]
    in_specs += [pl.BlockSpec(k.shape, all_map) for k in keys]
    args = [q, *keys]
    if not first:
        in_specs += [
            pl.BlockSpec((ROW_BLOCK, 256), row_map),
            pl.BlockSpec((ROW_BLOCK, width), row_map),
        ]
        args += list(state)
    if last:
        out_shape = jax.ShapeDtypeStruct((rows, width + 128), jnp.bfloat16)
        out_specs = pl.BlockSpec((ROW_BLOCK, width + 128), row_map)
    else:
        out_shape = (
            jax.ShapeDtypeStruct((rows, 256), jnp.float32),
            jax.ShapeDtypeStruct((rows, width), jnp.float32),
        )
        out_specs = (
            pl.BlockSpec((ROW_BLOCK, 256), row_map),
            pl.BlockSpec((ROW_BLOCK, width), row_map),
        )
    key_rows = sum(k.shape[0] for k in keys)
    return pl.pallas_call(
        functools.partial(attend_kernel, first, last, width, exponent_scale, len(keys)),
        grid=(rows // ROW_BLOCK,),
        in_specs=in_specs,
        out_specs=out_specs,
        out_shape=out_shape,
        compiler_params=pltpu.CompilerParams(vmem_limit_bytes=32 * 1024 * 1024),
        cost_estimate=pl.CostEstimate(
            flops=2 * rows * key_rows * (features + width),
            bytes_accessed=2 * rows * features + 2 * key_rows * features,
            transcendentals=rows * key_rows,
        ),
        name="prefix_attend",
    )(*args)


def tail_kernel(width, exponent_scale, length_ref, core_ref, q_ref, own_ref, other_ref, out_ref):
    slot = pl.program_id(0)
    sources, _, heads, features = q_ref.shape
    span = own_ref.shape[2]
    q = q_ref[...].reshape(sources * heads, features)
    length = length_ref[slot]
    core = core_ref[0]
    parts = []
    for ref, side in ((own_ref, core), (other_ref, 1 - core)):
        keys = ref[...].reshape(sources * span, features)
        s = lax.dot_general(
            q, keys, (((1,), (1,)), ((), ())), preferred_element_type=jnp.float32
        )
        t = lax.broadcasted_iota(jnp.int32, s.shape, 1)
        position = (t // span) * (2 * span) + side * span + t % span
        parts.append((jnp.where(position < length, s, -1e30), position < length, keys))
    highest = functools.reduce(
        jnp.maximum, [jnp.max(s, axis=1, keepdims=True) for s, _, _ in parts]
    )
    weight_sum = 0.0
    acc = 0.0
    for s, usable, keys in parts:
        w = jnp.where(usable, jnp.exp2((s - highest) * exponent_scale), 0.0)
        weight_sum = weight_sum + jnp.sum(w, axis=1, keepdims=True)
        acc = acc + jnp.dot(
            w.astype(jnp.bfloat16), keys[:, :width], preferred_element_type=jnp.float32
        )
    pack_tail(out_ref, acc, weight_sum, highest, exponent_scale, width, sources, heads)


def pack_tail(out_ref, acc, weight_sum, highest, exponent_scale, width, sources, heads):
    rows = sources * heads
    context = (acc / weight_sum).astype(jnp.bfloat16)
    level = highest * exponent_scale + jnp.log2(weight_sum)
    high = level.astype(jnp.bfloat16)
    rest = level - high.astype(jnp.float32)
    middle = rest.astype(jnp.bfloat16)
    low = rest - middle.astype(jnp.float32)
    lane = lax.broadcasted_iota(jnp.int32, (rows, 128), 1)
    packed = jnp.where(
        lane == 0,
        high.astype(jnp.float32),
        jnp.where(lane == 1, middle.astype(jnp.float32), jnp.where(lane == 2, low, 0.0)),
    ).astype(jnp.bfloat16)
    out_ref[:, 0, :, :width] = context.reshape(sources, heads, width)
    out_ref[:, 0, :, width:] = packed.reshape(sources, heads, 128)


def attend_tails(q, own, other, length, core, width, exponent_scale):
    sources, slots, heads, features = q.shape
    span = own.shape[2]
    block = lambda last2, last1: pl.BlockSpec(
        (sources, 1, last2, last1), lambda i, *_: (0, i, 0, 0)
    )
    return pl.pallas_call(
        functools.partial(tail_kernel, width, exponent_scale),
        grid_spec=pltpu.PrefetchScalarGridSpec(
            num_scalar_prefetch=2,
            grid=(slots,),
            in_specs=[block(heads, features), block(span, features), block(span, features)],
            out_specs=block(heads, width + 128),
        ),
        out_shape=jax.ShapeDtypeStruct((sources, slots, heads, width + 128), jnp.bfloat16),
        compiler_params=pltpu.CompilerParams(vmem_limit_bytes=32 * 1024 * 1024),
        cost_estimate=pl.CostEstimate(
            flops=2 * slots * sources * heads * sources * 2 * span * (features + width),
            bytes_accessed=2 * (q.size + own.size + other.size),
            transcendentals=slots * sources * heads * sources * 2 * span,
        ),
        name="tail_attend",
    )(length, core, q, own, other)


def on_device(
    queries, prefix_latent, tail_latent, tail_length, slot_request, key_absorb, value_up, out_proj
):
    heads_here, nope_width, latent_width = key_absorb.shape
    value_width = value_up.shape[2]
    req_rows = slot_request.shape[0]
    features = prefix_latent.shape[1]
    rope_width = features - latent_width
    exponent_scale = math.log2(math.e) / math.sqrt(nope_width + rope_width)
    core = lax.axis_index("core")
    chips = lax.axis_size("z_hi") * lax.axis_size("y")
    chip = lax.axis_index("z_hi") * lax.axis_size("y") + lax.axis_index("y")
    slots = req_rows // chips

    def ring(value, axis, by):
        size = lax.axis_size(axis)
        return lax.ppermute(value, axis, [(i, (i + by) % size) for i in range(size)])

    def other_core(value):
        return lax.ppermute(value, "core", [(0, 1), (1, 0)])

    def z_ring(value, by):
        low, high = lax.axis_size("z_lo"), lax.axis_size("z_hi")
        size = low * high
        place = lambda z: (z % low) * high + z // low
        pairs = [(place(z), place((z + by) % size)) for z in range(size)]
        return lax.ppermute(value, ("z_lo", "z_hi"), pairs)

    def exchange(value):
        return lax.all_to_all(value, ("z_hi", "y"), 0, 0, tiled=True)

    held = jnp.concatenate(
        [prefix_latent] + [ring(prefix_latent, "y", by) for by in (1, -1, 2)], axis=0
    )
    held = jnp.concatenate([held] + [z_ring(held, by) for by in (1, -1, 2)], axis=0)

    picked = jnp.take(queries, slot_request, axis=0).reshape(
        req_rows, heads_here, nope_width + rope_width
    )
    query_latent = jnp.einsum(
        "rhn,hnl->rhl", picked[:, :, :nope_width], key_absorb, preferred_element_type=jnp.float32
    ).astype(jnp.bfloat16)
    query_full = jnp.concatenate([query_latent, picked[:, :, nope_width:]], axis=2)

    tail_own = exchange(tail_latent).reshape(chips, slots, *tail_latent.shape[1:])
    tail_query = exchange(query_full).reshape(chips, slots, heads_here, features)
    tail_other = other_core(tail_own)
    length = lax.dynamic_slice_in_dim(tail_length, chip * slots, slots)
    tail_part = attend_tails(
        tail_query, tail_own, tail_other, length, core.reshape(1), latent_width, exponent_scale
    )
    tail_part = exchange(
        tail_part.reshape(chips * slots, heads_here, latent_width + 128)
    )

    query_rows = query_full.reshape(req_rows * heads_here, features)
    both = jnp.concatenate([query_rows, other_core(query_rows)], axis=0)
    half = held.shape[0] // 2
    right, left = ring(held, "x", 1), ring(held, "x", -1)
    far_a, far_b = ring(held[:half], "x", 2), ring(held[half:], "x", 2)
    state = attend(both, [held], None, False, latent_width, exponent_scale)
    state = attend(both, [right, left], state, False, latent_width, exponent_scale)
    packed = attend(both, [far_a, far_b], state, True, latent_width, exponent_scale)
    received = other_core(packed[query_rows.shape[0] :])

    parts = [
        part.reshape(req_rows, heads_here, latent_width + 128)
        for part in (packed[: query_rows.shape[0]], received, tail_part)
    ]
    levels = [
        jnp.sum(part[:, :, latent_width : latent_width + 3].astype(jnp.float32), axis=2)
        for part in parts
    ]
    top = functools.reduce(jnp.maximum, levels)
    shares = [jnp.exp2(level - top) for level in levels]
    total = shares[0] + shares[1] + shares[2]
    context = sum(
        part[:, :, :latent_width].astype(jnp.float32) * (share / total)[:, :, None]
        for part, share in zip(parts, shares)
    ).astype(jnp.bfloat16)
    head_out = jnp.einsum(
        "rhl,hlv->rhv", context, value_up, preferred_element_type=jnp.float32
    ).astype(jnp.bfloat16)
    head_out = head_out.reshape(req_rows, heads_here * value_width)
    mixed = jnp.dot(head_out, out_proj, preferred_element_type=jnp.float32)
    width_here = out_proj.shape[1] // (2 * chips)
    mixed = mixed.astype(jnp.bfloat16).reshape(req_rows, chips, 2, width_here)
    mixed = mixed.transpose(2, 1, 0, 3)
    keep = lax.dynamic_index_in_dim(mixed, core, 0, False)
    give = lax.dynamic_index_in_dim(mixed, 1 - core, 0, False)
    paired = keep.astype(jnp.float32) + other_core(give).astype(jnp.float32)
    gathered = exchange(paired.astype(jnp.bfloat16))
    return jnp.sum(gathered.astype(jnp.float32), axis=0).astype(jnp.bfloat16)


def solution(mesh):
    fine = Mesh(
        mesh.devices.reshape(4, 2, 2, 4, 2), ("x", "z_lo", "z_hi", "y", "core")
    )
    group, seq = ("x", "z_lo"), ("z_hi", "y", "core")
    placed = (
        P(None, seq),
        P(group + seq, None),
        P(group, seq, None),
        P(group),
        P(group),
        P(seq, None, None),
        P(seq, None, None),
        P(seq, None),
    )
    return jax.shard_map(
        on_device, mesh=fine, in_specs=placed, out_specs=P(group, seq), check_vma=False
    )
```

time: 477 us -> 200 us (0.42)
  the two profiles are of different devices: /device:TPU:0 before, /device:TPU:32 now
where the time goes in v1:
time: 200 us; the launch traced here: 199 us
  local copies, waits for them, and re-layouts  48.6 us (24%)
  starting transfers between devices  42.3 us (21%)
  waiting for transfers between devices  38.5 us (19%)
  Pallas kernels  33.5 us (17%)
  blocking collectives  15.4 us (8%)
  other arithmetic  10.4 us (5%)
  matrix products  9.56 us (5%)
    pallas_call x3, Pallas kernels, attend(): pl.pallas_call(functools.partial(attend_kernel, first, last, width, expon...  25.6 us
    all_to_all x3, starting transfers between devices, exchange(): return lax.all_to_all(value, ('z_hi', 'y'), 0, 0, tiled=True)  25.2 us
    ppermute x3, waiting for transfers between devices, z_ring(): return lax.ppermute(value, ('z_lo', 'z_hi'), pairs)  21.2 us
    unnamed x45, local copies, waits for them, and re-layouts  20.4 us
    all_to_all x1, blocking collectives, exchange(): return lax.all_to_all(value, ('z_hi', 'y'), 0, 0, tiled=True)  15.4 us
    all_to_all x3, waiting for transfers between devices, exchange(): return lax.all_to_all(value, ('z_hi', 'y'), 0, 0, tiled=True)  13.2 us
    ppermute x7, starting transfers between devices, ring(): lax.ppermute(value, axis, [(i, (i + by) % size) for i in range(size)])  12 us
    ppermute x4, local copies, waits for them, and re-layouts, ring(): lax.ppermute(value, axis, [(i, (i + by) % size) for i in range(size)])  9.12 us
  transfers between devices with their start and end apart: 17, of which 4 were waited for; matrix products, arithmetic and copies ran while one was open for 18% of the time, Pallas kernels for 17%

profile of v1, /device:TPU:32, one launch (start us, length us, event | category | flops | bytes accessed | tf_op | source)
XLA Modules:
  0.0 198.7 jit_solution(3694856895161423907)
XLA Ops:
  14.6 3.1 %collective-permute-start.7 = (bf16[256,576]{1,0:T(8,128)(2,1)}, bf16[256,576]{1,0:T(8,128)(2,1)}, u32[]{:S(2)}, u32[]{:S(2)}) collective-permute-start(bf16[256,576]{1,0:T(8,128)(2,1)} %get-tuple-element.23), channel_id=1, source_target_pairs={{0,8},{16,24},{8,0},{24,16},{1,9},{17,25},{9,1},{25,17},{2,10},{18... | collective-permute-start | bytes 884744 | tf_op jit(solution)/shard_map/ppermute | solution.py:218
  18.7 3.6 %all-to-all-start.1 = ((bf16[72,16,576]{2,1,0:T(8,128)(2,1)}), bf16[72,16,576]{2,1,0:T(8,128)(2,1)S(1)}, u32[]{:S(2)}, u32[]{:S(2)}) async-start(bf16[72,16,576]{2,1,0:T(8,128)(2,1)} %param.10), calls=%async_computation.1 | async-start | bytes 2949120 | tf_op jit(solution)/shard_map/all_to_all | solution.py:221
  22.3 21.2 %collective-permute-done.4 = bf16[256,576]{1,0:T(8,128)(2,1)} collective-permute-done((bf16[256,576]{1,0:T(8,128)(2,1)}, bf16[256,576]{1,0:T(8,128)(2,1)}, u32[]{:S(2)}, u32[]{:S(2)}) %collective-permute-start.4) | collective-permute-done | bytes 294944 | tf_op jit(solution)/shard_map/ppermute | solution.py:218
  48.8 2.4 %copy.65 = bf16[1024,576]{0,1:T(8,128)(2,1)} copy(bf16[1024,576]{1,0:T(8,128)(2,1)} %constant_dynamic-update-slice_fusion.9.refs_0_) | data formatting | bytes 2359296 | tf_op jit(solution)/shard_map/concatenate | solution.py:226
  56.4 2.1 %copy.64 = bf16[512,576]{0,1:T(8,128)(2,1)} copy(bf16[512,576]{1,0:T(8,128)(2,1)} %pad_maximum_fusion.2) | data formatting | bytes 1179648 | tf_op jit(solution)/shard_map/concatenate | solution.py:226
  60.4 2.1 %copy.63 = bf16[512,576]{0,1:T(8,128)(2,1)} copy(bf16[512,576]{1,0:T(8,128)(2,1)} %get-tuple-element.20) | data formatting | bytes 1179648 | tf_op jit(solution)/shard_map/concatenate | solution.py:226
  64.2 2.6 %pad_maximum_fusion.q_ref = bf16[1152,576]{1,0:T(8,128)(2,1)} fusion(bf16[576,576]{1,0:T(8,128)(2,1)} %collective-permute-done, bf16[576,576]{1,0:T(8,128)(2,1)} %bitcast.31), kind=kLoop, calls=%fused_computation.2 | loop fusion | flops 2654208 | bytes 2654208 | tf_op jit(solution)/shard_map/concatenate | solution.py:248
  66.8 6.1 %all-to-all-start = ((bf16[72,8,576]{2,1,0:T(8,128)(2,1)}), bf16[72,8,576]{2,1,0:T(8,128)(2,1)}, u32[]{:S(2)}, u32[]{:S(2)}) async-start(bf16[72,8,576]{2,1,0:T(8,128)(2,1)} %copy.100), calls=%async_computation | async-start | bytes 1474560 | tf_op jit(solution)/shard_map/all_to_all | solution.py:221
  74.3 7.5 %prefix_attend.3 = (f32[1152,256]{1,0:T(8,128)S(1)}, f32[1152,512]{1,0:T(8,128)S(1)}) custom-call(bf16[1152,576]{1,0:T(8,128)(2,1)S(1)} %copy-done.2, bf16[1024,576]{1,0:T(8,128)(2,1)} %constant_dynamic-update-slice_fusion.9.refs_0_), custom_call_target="tpu_custom_call" | custom-call | flops 2566914048 | bytes 2506752 | tf_op jit(solution)/shard_map/prefix_attend/pallas_call | solution.py:103
  84.2 2.1 %copy.70.refs_1_ = bf16[512,576]{1,0:T(8,128)(2,1)} copy(bf16[512,576]{0,1:T(8,128)(2,1)} %collective-permute-done.8) | data formatting | bytes 1179648 | tf_op jit(solution)/shard_map/ppermute | solution.py:208
  86.4 2.1 %collective-permute-done.5 = bf16[512,576]{0,1:T(8,128)(2,1)} collective-permute-done((bf16[512,576]{0,1:T(8,128)(2,1)}, bf16[512,576]{0,1:T(8,128)(2,1)}, u32[]{:S(2)}, u32[]{:S(2)}) %collective-permute-start.5) | collective-permute-done | bytes 589856 | tf_op jit(solution)/shard_map/ppermute | solution.py:208
  88.5 2.1 %copy.69.refs_0_ = bf16[512,576]{1,0:T(8,128)(2,1)} copy(bf16[512,576]{0,1:T(8,128)(2,1)} %collective-permute-done.5) | data formatting | bytes 1179648 | tf_op jit(solution)/shard_map/ppermute | solution.py:208
  90.6 2.4 %copy.67.refs_0_ = bf16[1024,576]{1,0:T(8,128)(2,1)} copy(bf16[1024,576]{0,1:T(8,128)(2,1)} %collective-permute-done.9) | data formatting | bytes 2359296 | tf_op jit(solution)/shard_map/ppermute | solution.py:208
  93.0 2.5 %copy.68.refs_1_ = bf16[1024,576]{1,0:T(8,128)(2,1)} copy(bf16[1024,576]{0,1:T(8,128)(2,1)} %collective-permute-done.10) | data formatting | bytes 2359296 | tf_op jit(solution)/shard_map/ppermute | solution.py:208
  102.4 11.4 %prefix_attend.4 = (f32[1152,256]{1,0:T(8,128)S(1)}, f32[1152,512]{1,0:T(8,128)S(1)}) custom-call(bf16[1152,576]{1,0:T(8,128)(2,1)S(1)} %copy-done.3, bf16[1024,576]{1,0:T(8,128)(2,1)S(1)} %copy-done.5, bf16[1024,576]{1,0:T(8,128)(2,1)S(1)} %copy-done.6, f32[1152,256]{1,0:T(8,128)S(1)} %copy-done.12, f32[1152,512]{1,0:T(8,128)S(1)} %copy-done.10), custom_call_target="tpu_custom_call" | custom-call | flops 5133828096 | bytes 3686400 | tf_op jit(solution)/shard_map/prefix_attend/pallas_call | solution.py:103
  113.9 6.7 %prefix_attend.5 = bf16[1152,640]{1,0:T(8,128)(2,1)S(1)} custom-call(bf16[1152,576]{1,0:T(8,128)(2,1)S(1)} %copy-done.4, bf16[512,576]{1,0:T(8,128)(2,1)S(1)} %copy-done.8, bf16[512,576]{1,0:T(8,128)(2,1)S(1)} %copy-done.7, f32[1152,256]{1,0:T(8,128)S(1)} %get-tuple-element.11.refs_2_, f32[1152,512]{1,0:T(8,128)S(1)} %get-tuple-element.12.refs_3_), custom_call_target="tpu_custom_call" | custom-call | flops 2566914048 | bytes 2506752 | tf_op jit(solution)/shard_map/prefix_attend/pallas_call | solution.py:103
  122.0 7.9 %tail_attend.1 = bf16[8,9,8,640]{3,2,1,0:T(8,128)(2,1)S(1)} custom-call(s32[9]{0:T(128)S(1)} %dynamic_slice.10.length_ref, s32[1]{0:T(128)} %bitcast.4.core_ref, bf16[8,9,8,576]{3,2,1,0:T(8,128)(2,1)} %bitcast.5.q_ref, bf16[8,9,16,576]{3,2,1,0:T(8,128)(2,1)S(1)} %bitcast.33, bf16[8,9,16,576]{3,2,1,0:T(8,128)(2,1)} %collective-permute-done.12.other_ref), custom_call_target="tpu_custom_call" | custom-call | flops 320864256 | bytes 3317760 | tf_op jit(solution)/shard_map/tail_attend/pallas_call | solution.py:173
  130.8 15.5 %all-to-all-start.2 = ((bf16[72,8,640]{2,1,0:T(8,128)(2,1)}), bf16[72,8,640]{2,1,0:T(8,128)(2,1)S(1)}, u32[]{:S(2)}, u32[]{:S(2)}) async-start(bf16[72,8,640]{2,1,0:T(8,128)(2,1)} %bitcast.34), calls=%async_computation.2 | async-start | bytes 1474560 | tf_op jit(solution)/shard_map/all_to_all | solution.py:221
  147.6 13.2 %all-to-all-done.2 = bf16[72,8,640]{2,1,0:T(8,128)(2,1)S(1)} async-done(((bf16[72,8,640]{2,1,0:T(8,128)(2,1)}), bf16[72,8,640]{2,1,0:T(8,128)(2,1)S(1)}, u32[]{:S(2)}, u32[]{:S(2)}) %all-to-all-start.2) | async-done | bytes 737312 | tf_op jit(solution)/shard_map/all_to_all | solution.py:221
  163.4 8.8 %convolution_convert_fusion = bf16[72,7168]{1,0:T(8,128)(2,1)} fusion(bf16[1024,7168]{1,0:T(8,128)(2,1)} %param.15, bf16[8,9,8,128]{3,2,1,0:T(8,128)(2,1)S(1)} %fusion.2), kind=kOutput, calls=%fused_computation.1 | convolution fusion | flops 1057480704 | bytes 15859712 | tf_op jit(solution)/shard_map/dot_general | solution.py:276
  172.2 3.8 %reshape.83 = bf16[72,8,2,448]{3,2,1,0:T(2,128)(2,1)S(1)} reshape(bf16[72,7168]{1,0:T(8,128)(2,1)} %convolution_convert_fusion) | data formatting | bytes 2064384 | tf_op jit(solution)/shard_map/reshape | solution.py:278
  176.0 3.1 %constant_dynamic-slice_fusion.1 = (bf16[72,8,1,448]{3,2,1,0:T(2,128)(2,1)S(1)}, bf16[72,8,1,448]{3,2,1,0:T(2,128)(2,1)S(1)}) fusion(bf16[72,8,2,448]{3,2,1,0:T(2,128)(2,1)S(1)} %reshape.83, s32[]{:T(128)S(6)} %select_n.23, s32[]{:T(128)S(6)} %select_n.24), kind=kLoop, calls=%fused_computation.50 | loop fusion | bytes 2064392 | tf_op jit(solution)/shard_map/jit(dynamic_index_in_dim)/dynamic_slice | solution.py:280
  179.9 2.0 %collective-permute-done.13 = bf16[8,72,448]{2,1,0:T(8,128)(2,1)S(1)} collective-permute-done((bf16[8,72,448]{2,1,0:T(8,128)(2,1)S(1)}, bf16[8,72,448]{2,1,0:T(8,128)(2,1)S(1)}, u32[]{:S(2)}, u32[]{:S(2)}) %collective-permute-start.13) | collective-permute-done | bytes 516128 | tf_op jit(solution)/shard_map/ppermute | solution.py:211
  182.6 15.4 %all_to_all.20 = bf16[8,72,448]{2,1,0:T(8,128)(2,1)S(1)} all-to-all(bf16[8,72,448]{2,1,0:T(8,128)(2,1)S(1)} %fusion.1), channel_id=1, replica_groups=mesh['x'=4,'z_lo'=2,'z_hi'=2,'y'=4,'core'=2] {'z_hi','y'}, dimensions={0} | all-to-all | bytes 1032192 | tf_op jit(solution)/shard_map/all_to_all | solution.py:221
  (99 shorter events, 48.6 us)
Async XLA Ops:
  0.0 6.6 %copy-start = (bf16[576,1536]{1,0:T(8,128)(2,1)S(1)}, bf16[576,1536]{1,0:T(8,128)(2,1)}, u32[]{:S(2)}) copy-start(bf16[576,1536]{1,0:T(8,128)(2,1)} %param.8) | copy-start | bytes 5308420
  0.0 8.4 %collective-permute-start.1 = (bf16[64,576]{1,0:T(8,128)(2,1)}, bf16[64,576]{1,0:T(8,128)(2,1)}, u32[]{:S(2)}, u32[]{:S(2)}) collective-permute-start(bf16[64,576]{1,0:T(8,128)(2,1)} %param.9), channel_id=1, source_target_pairs={{0,2},{2,4},{4,6},{6,0},{1,3},{3,5},{5,7},{7,1},{8,10},{10,12},{12... | collective-permute-start | bytes 221192 | tf_op jit(solution)/shard_map/ppermute | solution.py:208
  1.6 8.4 %collective-permute-start.2 = (bf16[64,576]{1,0:T(8,128)(2,1)}, bf16[64,576]{1,0:T(8,128)(2,1)}, u32[]{:S(2)}, u32[]{:S(2)}) collective-permute-start(bf16[64,576]{1,0:T(8,128)(2,1)} %param.9), channel_id=1, source_target_pairs={{0,6},{2,0},{4,2},{6,4},{1,7},{3,1},{5,3},{7,5},{8,14},{10,8},{12,... | collective-permute-start | bytes 221192 | tf_op jit(solution)/shard_map/ppermute | solution.py:208
  3.2 8.3 %collective-permute-start.3 = (bf16[64,576]{1,0:T(8,128)(2,1)}, bf16[64,576]{1,0:T(8,128)(2,1)S(1)}, u32[]{:S(2)}, u32[]{:S(2)}) collective-permute-start(bf16[64,576]{1,0:T(8,128)(2,1)} %param.9), channel_id=1, source_target_pairs={{0,4},{2,6},{4,0},{6,2},{1,5},{3,7},{5,1},{7,3},{8,12},{10,14},{12... | collective-permute-start | bytes 221192 | tf_op jit(solution)/shard_map/ppermute | solution.py:208
  7.3 6.9 %copy-start.14 = (bf16[8,128,512]{2,1,0:T(8,128)(2,1)S(1)}, bf16[8,128,512]{2,1,0:T(8,128)(2,1)}, u32[]{:S(2)}) copy-start(bf16[8,128,512]{2,1,0:T(8,128)(2,1)} %param.13) | copy-start | bytes 3145732
  12.2 1.9 copy-start.16
  12.2 31.2 %collective-permute-start.4 = (bf16[256,576]{1,0:T(8,128)(2,1)}, bf16[256,576]{1,0:T(8,128)(2,1)}, u32[]{:S(2)}, u32[]{:S(2)}) collective-permute-start(bf16[256,576]{1,0:T(8,128)(2,1)} %get-tuple-element.23), channel_id=1, source_target_pairs={{0,16},{16,8},{8,24},{24,0},{1,17},{17,9},{9,25},{25,1},{2,18},{18... | collective-permute-start | bytes 884744 | tf_op jit(solution)/shard_map/ppermute | solution.py:218
  14.1 31.2 %collective-permute-start.6 = (bf16[256,576]{1,0:T(8,128)(2,1)}, bf16[256,576]{1,0:T(8,128)(2,1)}, u32[]{:S(2)}, u32[]{:S(2)}) collective-permute-start(bf16[256,576]{1,0:T(8,128)(2,1)} %get-tuple-element.23), channel_id=1, source_target_pairs={{0,24},{16,0},{8,16},{24,8},{1,25},{17,1},{9,17},{25,9},{2,26},{18... | collective-permute-start | bytes 884744 | tf_op jit(solution)/shard_map/ppermute | solution.py:218
  14.6 32.5 %collective-permute-start.7 = (bf16[256,576]{1,0:T(8,128)(2,1)}, bf16[256,576]{1,0:T(8,128)(2,1)}, u32[]{:S(2)}, u32[]{:S(2)}) collective-permute-start(bf16[256,576]{1,0:T(8,128)(2,1)} %get-tuple-element.23), channel_id=1, source_target_pairs={{0,8},{16,24},{8,0},{24,16},{1,9},{17,25},{9,1},{25,17},{2,10},{18... | collective-permute-start | bytes 884744 | tf_op jit(solution)/shard_map/ppermute | solution.py:218
  18.7 45.5 %collective-permute-start = (bf16[576,576]{1,0:T(8,128)(2,1)}, bf16[576,576]{1,0:T(8,128)(2,1)}, u32[]{:S(2)}, u32[]{:S(2)}) collective-permute-start(bf16[576,576]{1,0:T(8,128)(2,1)} %bitcast.31), channel_id=1, source_target_pairs={{0,1},{1,0},{2,3},{3,2},{4,5},{5,4},{6,7},{7,6},{8,9},{9,8},{10,11... | collective-permute-start | bytes 1990664 | tf_op jit(solution)/shard_map/ppermute | solution.py:211
  18.7 48.2 %all-to-all-start.1 = ((bf16[72,16,576]{2,1,0:T(8,128)(2,1)}), bf16[72,16,576]{2,1,0:T(8,128)(2,1)S(1)}, u32[]{:S(2)}, u32[]{:S(2)}) async-start(bf16[72,16,576]{2,1,0:T(8,128)(2,1)} %param.10), calls=%async_computation.1 | async-start | bytes 2949120 | tf_op jit(solution)/shard_map/all_to_all | solution.py:221
  51.2 39.4 %collective-permute-start.9 = (bf16[1024,576]{0,1:T(8,128)(2,1)}, bf16[1024,576]{0,1:T(8,128)(2,1)}, u32[]{:S(2)}, u32[]{:S(2)}) collective-permute-start(bf16[1024,576]{0,1:T(8,128)(2,1)} %copy.65), channel_id=1, source_target_pairs={{0,32},{32,64},{64,96},{96,0},{1,33},{33,65},{65,97},{97,1},{2,34}... | collective-permute-start | bytes 3538952 | tf_op jit(solution)/shard_map/ppermute | solution.py:208
  52.7 40.3 %collective-permute-start.10 = (bf16[1024,576]{0,1:T(8,128)(2,1)}, bf16[1024,576]{0,1:T(8,128)(2,1)}, u32[]{:S(2)}, u32[]{:S(2)}) collective-permute-start(bf16[1024,576]{0,1:T(8,128)(2,1)} %copy.65), channel_id=1, source_target_pairs={{0,96},{32,0},{64,32},{96,64},{1,97},{33,1},{65,33},{97,65},{2,98}... | collective-permute-start | bytes 3538952 | tf_op jit(solution)/shard_map/ppermute | solution.py:208
  58.5 25.7 %collective-permute-start.8 = (bf16[512,576]{0,1:T(8,128)(2,1)}, bf16[512,576]{0,1:T(8,128)(2,1)}, u32[]{:S(2)}, u32[]{:S(2)}) collective-permute-start(bf16[512,576]{0,1:T(8,128)(2,1)} %copy.64), channel_id=1, source_target_pairs={{0,64},{32,96},{64,0},{96,32},{1,65},{33,97},{65,1},{97,33},{2,66}... | collective-permute-start | bytes 1769480 | tf_op jit(solution)/shard_map/ppermute | solution.py:208
  62.5 26.0 %collective-permute-start.5 = (bf16[512,576]{0,1:T(8,128)(2,1)}, bf16[512,576]{0,1:T(8,128)(2,1)}, u32[]{:S(2)}, u32[]{:S(2)}) collective-permute-start(bf16[512,576]{0,1:T(8,128)(2,1)} %copy.63), channel_id=1, source_target_pairs={{0,64},{32,96},{64,0},{96,32},{1,65},{33,97},{65,1},{97,33},{2,66}... | collective-permute-start | bytes 1769480 | tf_op jit(solution)/shard_map/ppermute | solution.py:208
  66.8 55.1 %all-to-all-start = ((bf16[72,8,576]{2,1,0:T(8,128)(2,1)}), bf16[72,8,576]{2,1,0:T(8,128)(2,1)}, u32[]{:S(2)}, u32[]{:S(2)}) async-start(bf16[72,8,576]{2,1,0:T(8,128)(2,1)} %copy.100), calls=%async_computation | async-start | bytes 1474560 | tf_op jit(solution)/shard_map/all_to_all | solution.py:221
  72.9 49.1 %collective-permute-start.12 = (bf16[8,9,16,576]{3,2,1,0:T(8,128)(2,1)S(1)}, bf16[8,9,16,576]{3,2,1,0:T(8,128)(2,1)}, u32[]{:S(2)}, u32[]{:S(2)}) collective-permute-start(bf16[8,9,16,576]{3,2,1,0:T(8,128)(2,1)S(1)} %bitcast.32), channel_id=1, source_target_pairs={{0,1},{1,0},{2,3},{3,2},{4,5},{5,4},{6,7},{7,6},{8,9},{9,8},{10,11... | collective-permute-start | bytes 3981320 | tf_op jit(solution)/shard_map/ppermute | solution.py:211
  102.4 11.4 %copy-start.4 = (bf16[1152,576]{1,0:T(8,128)(2,1)S(1)}, bf16[1152,576]{1,0:T(8,128)(2,1)}, u32[]{:S(2)}) copy-start(bf16[1152,576]{1,0:T(8,128)(2,1)} %pad_maximum_fusion.q_ref) | copy-start | bytes 3981316
  102.4 11.4 %copy-start.7 = (bf16[512,576]{1,0:T(8,128)(2,1)S(1)}, bf16[512,576]{1,0:T(8,128)(2,1)}, u32[]{:S(2)}) copy-start(bf16[512,576]{1,0:T(8,128)(2,1)} %copy.70.refs_1_) | copy-start | bytes 1769476
  102.4 11.5 %copy-start.8 = (bf16[512,576]{1,0:T(8,128)(2,1)S(1)}, bf16[512,576]{1,0:T(8,128)(2,1)}, u32[]{:S(2)}) copy-start(bf16[512,576]{1,0:T(8,128)(2,1)} %copy.69.refs_0_) | copy-start | bytes 1769476
  121.9 24.6 %collective-permute-start.11 = (bf16[576,640]{1,0:T(8,128)(2,1)}, bf16[576,640]{1,0:T(8,128)(2,1)}, u32[]{:S(2)}, u32[]{:S(2)}) collective-permute-start(bf16[576,640]{1,0:T(8,128)(2,1)} %get-tuple-element.14), channel_id=1, source_target_pairs={{0,1},{1,0},{2,3},{3,2},{4,5},{5,4},{6,7},{7,6},{8,9},{9,8},{10,11... | collective-permute-start | bytes 2211848 | tf_op jit(solution)/shard_map/ppermute | solution.py:211
  130.7 15.5 %copy-start.13 = (bf16[72,8,640]{2,1,0:T(8,128)(2,1)S(1)}, bf16[72,8,640]{2,1,0:T(8,128)(2,1)}, u32[]{:S(2)}) copy-start(bf16[72,8,640]{2,1,0:T(8,128)(2,1)} %get-tuple-element.13) | copy-start | bytes 2211844
  130.8 30.1 %all-to-all-start.2 = ((bf16[72,8,640]{2,1,0:T(8,128)(2,1)}), bf16[72,8,640]{2,1,0:T(8,128)(2,1)S(1)}, u32[]{:S(2)}, u32[]{:S(2)}) async-start(bf16[72,8,640]{2,1,0:T(8,128)(2,1)} %bitcast.34), calls=%async_computation.2 | async-start | bytes 1474560 | tf_op jit(solution)/shard_map/all_to_all | solution.py:221
  179.8 2.1 %collective-permute-start.13 = (bf16[8,72,448]{2,1,0:T(8,128)(2,1)S(1)}, bf16[8,72,448]{2,1,0:T(8,128)(2,1)S(1)}, u32[]{:S(2)}, u32[]{:S(2)}) collective-permute-start(bf16[8,72,448]{2,1,0:T(8,128)(2,1)S(1)} %bitcast.35), channel_id=1, source_target_pairs={{0,1},{1,0},{2,3},{3,2},{4,5},{5,4},{6,7},{7,6},{8,9},{9,8},{10,11... | collective-permute-start | bytes 1548296 | tf_op jit(solution)/shard_map/ppermute | solution.py:211
  (12 other events, 15.6 us)

commit v2 on v1

v2 whole, which is shorter than its diff:
```python
import functools
import math

import jax
import jax.numpy as jnp
from jax import lax
from jax.experimental import pallas as pl
from jax.experimental.pallas import tpu as pltpu
from jax.sharding import Mesh, PartitionSpec as P

ROW_BLOCK = 288
KEY_BLOCK = 512
SLOT_BLOCK = 3
VMEM = 58 * 1024 * 1024
COST = pl.CostEstimate(flops=1000000, bytes_accessed=1000000, transcendentals=0)


def pack(acc, weight_sum, highest, exponent_scale):
    context = (acc / weight_sum).astype(jnp.bfloat16)
    level = highest * exponent_scale + jnp.log2(weight_sum)
    high = level.astype(jnp.bfloat16).astype(jnp.float32)
    middle = (level - high).astype(jnp.bfloat16).astype(jnp.float32)
    low = level - high - middle
    lane = lax.broadcasted_iota(jnp.int32, (acc.shape[0], 128), 1)
    terms = jnp.where(
        lane == 0, high, jnp.where(lane == 1, middle, jnp.where(lane == 2, low, 0.0))
    )
    return context, terms.astype(jnp.bfloat16)


def attend_kernel(first, last, width, exponent_scale, key_count, q_ref, *refs):
    key_refs = refs[:key_count]
    refs = refs[key_count:]
    q = q_ref[...]
    if first:
        highest = weight_sum = acc = None
    else:
        stat_ref, acc_ref = refs[:2]
        refs = refs[2:]
        highest = stat_ref[:, 0:1]
        weight_sum = stat_ref[:, 128:129]
        acc = acc_ref[...]
    blocks = [
        (k_ref, at) for k_ref in key_refs for at in range(0, k_ref.shape[1], KEY_BLOCK)
    ]

    def scores_of(block):
        k_ref, at = block
        return jnp.dot(
            q, k_ref[:, at : at + KEY_BLOCK], preferred_element_type=jnp.float32
        )

    scores = scores_of(blocks[0])
    for place, (k_ref, at) in enumerate(blocks):
        upcoming = scores_of(blocks[place + 1]) if place + 1 < len(blocks) else None
        block_highest = jnp.max(scores, axis=1, keepdims=True)
        new_highest = (
            block_highest if highest is None else jnp.maximum(highest, block_highest)
        )
        w = jnp.exp2((scores - new_highest) * exponent_scale)
        part_sum = jnp.sum(w, axis=1, keepdims=True)
        part = lax.dot_general(
            w.astype(jnp.bfloat16),
            k_ref[:width, at : at + KEY_BLOCK],
            (((1,), (1,)), ((), ())),
            preferred_element_type=jnp.float32,
        )
        if highest is None:
            weight_sum, acc = part_sum, part
        else:
            fade = jnp.exp2((highest - new_highest) * exponent_scale)
            weight_sum = weight_sum * fade + part_sum
            acc = acc * fade + part
        highest, scores = new_highest, upcoming
    if last:
        (out_ref,) = refs
        out_ref[:, :width], out_ref[:, width:] = pack(acc, weight_sum, highest, exponent_scale)
    else:
        out_stat_ref, out_acc_ref = refs
        out_stat_ref[:, :128] = jnp.broadcast_to(highest, (q.shape[0], 128))
        out_stat_ref[:, 128:] = jnp.broadcast_to(weight_sum, (q.shape[0], 128))
        out_acc_ref[...] = acc


def attend(q, keys, state, last, width, exponent_scale, second=False):
    rows, features = q.shape
    first = state is None
    row_map = lambda i: (i, 0)
    all_map = lambda i: (0, 0)
    in_specs = [pl.BlockSpec((ROW_BLOCK, features), row_map)]
    in_specs += [pl.BlockSpec(k.shape, all_map) for k in keys]
    args = [q, *keys]
    state_specs = (
        pl.BlockSpec((ROW_BLOCK, 256), row_map),
        pl.BlockSpec((ROW_BLOCK, width), row_map),
    )
    skip = rows // ROW_BLOCK if second else 0
    old_map = lambda i: (i + skip, 0)
    if not first:
        in_specs += [
            pl.BlockSpec((ROW_BLOCK, 256), old_map),
            pl.BlockSpec((ROW_BLOCK, width), old_map),
        ]
        args += list(state)
    if last:
        out_shape = jax.ShapeDtypeStruct((rows, width + 128), jnp.bfloat16)
        out_specs = pl.BlockSpec((ROW_BLOCK, width + 128), row_map)
    else:
        out_shape = (
            jax.ShapeDtypeStruct((rows, 256), jnp.float32),
            jax.ShapeDtypeStruct((rows, width), jnp.float32),
        )
        out_specs = state_specs
    return pl.pallas_call(
        functools.partial(attend_kernel, first, last, width, exponent_scale, len(keys)),
        grid=(rows // ROW_BLOCK,),
        in_specs=in_specs,
        out_specs=out_specs,
        out_shape=out_shape,
        compiler_params=pltpu.CompilerParams(vmem_limit_bytes=VMEM),
        cost_estimate=COST,
        name="prefix_attend",
    )(*args)


def tail_kernel(width, exponent_scale, length_ref, core_ref, q_ref, own_ref, other_ref, out_ref):
    first_slot = pl.program_id(0) * SLOT_BLOCK
    sources, _, heads, features = q_ref.shape
    span = own_ref.shape[2]
    core = core_ref[0]
    for at in range(SLOT_BLOCK):
        q = q_ref[:, at].reshape(sources * heads, features)
        length = length_ref[first_slot + at]
        parts = []
        for ref, side in ((own_ref, core), (other_ref, 1 - core)):
            keys = ref[:, at].reshape(sources * span, features)
            s = lax.dot_general(
                q, keys, (((1,), (1,)), ((), ())), preferred_element_type=jnp.float32
            )
            t = lax.broadcasted_iota(jnp.int32, s.shape, 1)
            usable = (t // span) * (2 * span) + side * span + t % span < length
            parts.append((jnp.where(usable, s, -1e30), usable, keys))
        highest = functools.reduce(
            jnp.maximum, [jnp.max(s, axis=1, keepdims=True) for s, _, _ in parts]
        )
        weight_sum = 0.0
        acc = 0.0
        for s, usable, keys in parts:
            w = jnp.where(usable, jnp.exp2((s - highest) * exponent_scale), 0.0)
            weight_sum = weight_sum + jnp.sum(w, axis=1, keepdims=True)
            acc = acc + jnp.dot(
                w.astype(jnp.bfloat16), keys[:, :width], preferred_element_type=jnp.float32
            )
        context, level = pack(acc, weight_sum, highest, exponent_scale)
        out_ref[:, at, :, :width] = context.reshape(sources, heads, width)
        out_ref[:, at, :, width:] = level.reshape(sources, heads, 128)


def attend_tails(q, own, other, length, core, width, exponent_scale):
    sources, slots, heads, features = q.shape
    span = own.shape[2]
    block = lambda last2, last1: pl.BlockSpec(
        (sources, SLOT_BLOCK, last2, last1), lambda i, *_: (0, i, 0, 0)
    )
    return pl.pallas_call(
        functools.partial(tail_kernel, width, exponent_scale),
        grid_spec=pltpu.PrefetchScalarGridSpec(
            num_scalar_prefetch=2,
            grid=(slots // SLOT_BLOCK,),
            in_specs=[block(heads, features), block(span, features), block(span, features)],
            out_specs=block(heads, width + 128),
        ),
        out_shape=jax.ShapeDtypeStruct((sources, slots, heads, width + 128), jnp.bfloat16),
        compiler_params=pltpu.CompilerParams(vmem_limit_bytes=VMEM),
        cost_estimate=COST,
        name="tail_attend",
    )(length, core, q, own, other)


def finish_kernel(
    width, core_ref, own_ref, received_ref, tail_ref, up_ref, proj_ref,
    keep_ref, give_ref, context_ref, head_ref,
):
    heads = up_ref.shape[0]
    value_width = up_ref.shape[2]
    req_rows = head_ref.shape[0]

    @pl.when(pl.program_id(0) == 0)
    def _():
        refs = (own_ref, received_ref, tail_ref)
        levels = [
            jnp.sum(ref[:, width:].astype(jnp.float32), axis=1, keepdims=True) for ref in refs
        ]
        top = functools.reduce(jnp.maximum, levels)
        shares = [jnp.exp2(level - top) for level in levels]
        total = shares[0] + shares[1] + shares[2]
        context = sum(
            ref[:, :width].astype(jnp.float32) * (share / total)
            for ref, share in zip(refs, shares)
        )
        context_ref[...] = context.reshape(req_rows, heads, width)
        for h in range(heads):
            head_ref[:, h * value_width : (h + 1) * value_width] = jnp.dot(
                context_ref[:, h, :].astype(jnp.bfloat16),
                up_ref[h],
                preferred_element_type=jnp.float32,
            ).astype(jnp.bfloat16)

    mixed = jnp.dot(head_ref[...], proj_ref[...], preferred_element_type=jnp.float32)
    mixed = mixed.astype(jnp.bfloat16)
    half = mixed.shape[1] // 2
    early = core_ref[0] == 0
    keep_ref[0] = jnp.where(early, mixed[:, :half], mixed[:, half:])
    give_ref[0] = jnp.where(early, mixed[:, half:], mixed[:, :half])


def finish(own, received, tail, value_up, out_proj, core, chips):
    heads, width, value_width = value_up.shape
    rows, packed_width = own.shape
    req_rows = rows // heads
    depth, columns = out_proj.shape
    block = columns // chips
    half = jax.ShapeDtypeStruct((chips, req_rows, block // 2), jnp.bfloat16)
    half_spec = pl.BlockSpec((1, req_rows, block // 2), lambda i, *_: (i, 0, 0))
    whole = pl.BlockSpec((rows, packed_width), lambda i, *_: (0, 0))
    return pl.pallas_call(
        functools.partial(finish_kernel, width),
        grid_spec=pltpu.PrefetchScalarGridSpec(
            num_scalar_prefetch=1,
            grid=(chips,),
            in_specs=[
                whole,
                whole,
                whole,
                pl.BlockSpec(value_up.shape, lambda i, *_: (0, 0, 0)),
                pl.BlockSpec((depth, block), lambda i, *_: (0, i)),
            ],
            out_specs=(half_spec, half_spec),
            scratch_shapes=[
                pltpu.VMEM((req_rows, heads, width), jnp.float32),
                pltpu.VMEM((req_rows, heads * value_width), jnp.bfloat16),
            ],
        ),
        out_shape=(half, half),
        compiler_params=pltpu.CompilerParams(vmem_limit_bytes=VMEM),
        cost_estimate=COST,
        name="finish",
    )(core, own, received, tail, value_up, out_proj)


def on_device(
    queries, prefix_latent, tail_latent, tail_length, slot_request, key_absorb, value_up, out_proj
):
    heads_here, nope_width, latent_width = key_absorb.shape
    value_width = value_up.shape[2]
    req_rows = slot_request.shape[0]
    features = prefix_latent.shape[1]
    rope_width = features - latent_width
    exponent_scale = math.log2(math.e) / math.sqrt(nope_width + rope_width)
    core = lax.axis_index("core")
    chips = lax.axis_size("z_hi") * lax.axis_size("y")
    chip = lax.axis_index("z_hi") * lax.axis_size("y") + lax.axis_index("y")
    slots = req_rows // chips

    def ring(value, axis, by):
        size = lax.axis_size(axis)
        return lax.ppermute(value, axis, [(i, (i + by) % size) for i in range(size)])

    def other_core(value):
        return lax.ppermute(value, "core", [(0, 1), (1, 0)])

    def z_ring(value, by):
        low, high = lax.axis_size("z_lo"), lax.axis_size("z_hi")
        size = low * high
        place = lambda z: (z % low) * high + z // low
        pairs = [(place(z), place((z + by) % size)) for z in range(size)]
        return lax.ppermute(value, ("z_lo", "z_hi"), pairs)

    def exchange(value):
        return lax.all_to_all(value, ("z_hi", "y"), 0, 0, tiled=True)

    picked = jnp.take(queries, slot_request, axis=0).reshape(
        req_rows, heads_here, nope_width + rope_width
    )
    query_latent = jnp.einsum(
        "rhn,hnl->rhl", picked[:, :, :nope_width], key_absorb, preferred_element_type=jnp.float32
    ).astype(jnp.bfloat16)
    query_full = jnp.concatenate([query_latent, picked[:, :, nope_width:]], axis=2)
    query_rows = query_full.reshape(req_rows * heads_here, features)

    held = jnp.concatenate(
        [prefix_latent] + [ring(prefix_latent, "y", by) for by in (1, -1, 2)], axis=0
    ).T
    shifted = [z_ring(held, by) for by in (1, -1, 2)]
    held = jnp.concatenate([held] + shifted, axis=1)
    tail_query = exchange(query_full).reshape(chips, slots, heads_here, features)
    query_other = other_core(query_rows)
    both = jnp.concatenate([query_rows, query_other], axis=0)
    tail_latent, both, _, tail_query = lax.optimization_barrier(
        (tail_latent, both, held, tail_query)
    )

    half = held.shape[1] // 2
    right, left = ring(held, "x", 1), ring(held, "x", -1)
    far = [ring(held[:, :half], "x", 2), ring(held[:, half:], "x", 2)]

    tail_own = exchange(tail_latent).reshape(chips, slots, *tail_latent.shape[1:])
    length = lax.dynamic_slice_in_dim(tail_length, chip * slots, slots)
    core_at = core.reshape(1)

    go = functools.partial(attend, width=latent_width, exponent_scale=exponent_scale)
    state = go(both, [held], None, False)
    tail_own, state, right, left = lax.optimization_barrier((tail_own, state, right, left))
    tail_other = other_core(tail_own)

    tail_part = attend_tails(
        tail_query, tail_own, tail_other, length, core_at, latent_width, exponent_scale
    )
    tail_part, right, left = lax.optimization_barrier((tail_part, right, left))
    tail_part = exchange(
        tail_part.reshape(chips * slots, heads_here, latent_width + 128)
    ).reshape(req_rows * heads_here, latent_width + 128)

    state = go(both, [right, left], state, False)
    state, far, tail_part = lax.optimization_barrier((state, far, tail_part))
    packed_other = go(query_other, far, state, True, second=True)
    received = other_core(packed_other)
    packed_own = go(query_rows, far, state, True)

    keep, give = finish(
        packed_own, received, tail_part, value_up, out_proj, core_at, chips
    )
    paired = keep.astype(jnp.float32) + other_core(give).astype(jnp.float32)
    gathered = exchange(paired.astype(jnp.bfloat16))
    return jnp.sum(gathered.astype(jnp.float32), axis=0).astype(jnp.bfloat16)


def solution(mesh):
    fine = Mesh(
        mesh.devices.reshape(4, 2, 2, 4, 2), ("x", "z_lo", "z_hi", "y", "core")
    )
    group, seq = ("x", "z_lo"), ("z_hi", "y", "core")
    placed = (
        P(None, seq),
        P(group + seq, None),
        P(group, seq, None),
        P(group),
        P(group),
        P(seq, None, None),
        P(seq, None, None),
        P(seq, None),
    )
    return jax.shard_map(
        on_device, mesh=fine, in_specs=placed, out_specs=P(group, seq), check_vma=False
    )
```

time: 200 us -> 159 us (0.80)
  the two profiles are of different devices: /device:TPU:32 before, /device:TPU:0 now
where the time goes in v2:
time: 159 us; the launch traced here: 158 us
  Pallas kernels  46.7 us (29%)
  waiting for transfers between devices  41.3 us (26%)
  starting transfers between devices  32.9 us (21%)
  blocking collectives  19.6 us (12%)
  other arithmetic  11.7 us (7%)
  local copies, waits for them, and re-layouts  5.58 us (4%)
    pallas_call x4, Pallas kernels, attend(): pl.pallas_call(functools.partial(attend_kernel, first, last, width, expon...  27.2 us
    ppermute x7, waiting for transfers between devices, ring(): lax.ppermute(value, axis, [(i, (i + by) % size) for i in range(size)])  21.2 us
    all_to_all x1, blocking collectives, exchange(): return lax.all_to_all(value, ('z_hi', 'y'), 0, 0, tiled=True)  19.6 us
    ppermute x3, waiting for transfers between devices, z_ring(): return lax.ppermute(value, ('z_lo', 'z_hi'), pairs)  14.4 us
    all_to_all x3, starting transfers between devices, exchange(): return lax.all_to_all(value, ('z_hi', 'y'), 0, 0, tiled=True)  14.3 us
    pallas_call x1, Pallas kernels, finish(): pl.pallas_call(functools.partial(finish_kernel, width), grid_spec=pltpu.P...  12.8 us
    ppermute x7, starting transfers between devices, ring(): lax.ppermute(value, axis, [(i, (i + by) % size) for i in range(size)])  12.1 us
    pallas_call x1, Pallas kernels, attend_tails(): pl.pallas_call(functools.partial(tail_kernel, width, exponent_scale), gri...  6.58 us
  transfers between devices with their start and end apart: 17, of which 9 were waited for; matrix products, arithmetic and copies ran while one was open for 6% of the time, Pallas kernels for 18%

profile of v2, /device:TPU:0, one launch (start us, length us, event | category | flops | bytes accessed | tf_op | source)
XLA Modules:
  0.0 158.2 jit_solution(1611348916882798875)
XLA Ops:
  4.2 3.4 %collective-permute-start.3 = (bf16[64,576]{0,1:T(8,128)(2,1)S(1)}, bf16[64,576]{0,1:T(8,128)(2,1)S(1)}, u32[]{:S(2)}, u32[]{:S(2)}) collective-permute-start(bf16[64,576]{0,1:T(8,128)(2,1)S(1)} %copy.27), channel_id=1, source_target_pairs={{0,4},{2,6},{4,0},{6,2},{1,5},{3,7},{5,1},{7,3},{8,12},{10,14},{12... | collective-permute-start | bytes 221192 | tf_op jit(solution)/shard_map/ppermute | solution.py:267
  9.6 2.8 %collective-permute-done.3 = bf16[64,576]{0,1:T(8,128)(2,1)S(1)} collective-permute-done((bf16[64,576]{0,1:T(8,128)(2,1)S(1)}, bf16[64,576]{0,1:T(8,128)(2,1)S(1)}, u32[]{:S(2)}, u32[]{:S(2)}) %collective-permute-start.3) | collective-permute-done | bytes 73760 | tf_op jit(solution)/shard_map/ppermute | solution.py:267
  12.4 3.2 %collective-permute-done.2 = bf16[64,576]{0,1:T(8,128)(2,1)S(1)} collective-permute-done((bf16[64,576]{0,1:T(8,128)(2,1)S(1)}, bf16[64,576]{0,1:T(8,128)(2,1)S(1)}, u32[]{:S(2)}, u32[]{:S(2)}) %collective-permute-start.2) | collective-permute-done | bytes 73760 | tf_op jit(solution)/shard_map/ppermute | solution.py:267
  15.9 4.0 %collective-permute-start.6 = (bf16[576,256]{1,0:T(8,128)(2,1)S(1)}, bf16[576,256]{1,0:T(8,128)(2,1)}, u32[]{:S(2)}, u32[]{:S(2)}) collective-permute-start(bf16[576,256]{1,0:T(8,128)(2,1)S(1)} %maximum_bitcast_fusion), channel_id=1, source_target_pairs={{0,8},{16,24},{8,0},{24,16},{1,9},{17,25},{9,1},{25,17},{2,10},{18... | collective-permute-start | bytes 884744 | tf_op jit(solution)/shard_map/ppermute | solution.py:277
  21.9 4.6 %all-to-all-start = ((bf16[72,8,576]{2,1,0:T(8,128)(2,1)}), bf16[72,8,576]{2,1,0:T(8,128)(2,1)S(1)}, u32[]{:S(2)}, u32[]{:S(2)}) async-start(bf16[72,8,576]{2,1,0:T(8,128)(2,1)} %copy.32), calls=%async_computation | async-start | bytes 1474560 | tf_op jit(solution)/shard_map/all_to_all | solution.py:280
  27.8 13.0 %collective-permute-done.5 = bf16[576,256]{1,0:T(8,128)(2,1)} collective-permute-done((bf16[576,256]{1,0:T(8,128)(2,1)S(1)}, bf16[576,256]{1,0:T(8,128)(2,1)}, u32[]{:S(2)}, u32[]{:S(2)}) %collective-permute-start.5) | collective-permute-done | bytes 294944 | tf_op jit(solution)/shard_map/ppermute | solution.py:277
  40.9 2.3 %pad_maximum_fusion.1.refs_0_ = bf16[576,1024]{1,0:T(8,128)(2,1)} fusion(bf16[576,256]{1,0:T(8,128)(2,1)} %collective-permute-done.6, bf16[576,256]{1,0:T(8,128)(2,1)} %collective-permute-done.5, bf16[576,256]{1,0:T(8,128)(2,1)} %collective-permute-done.4, bf16[576,256]{1,0:T(8,128)(2,1)S(1)} %maximum_bitcast_fusion), kind=kLoop, calls=%fused_computation.4 | loop fusion | flops 4718592 | bytes 2359296 | tf_op jit(solution)/shard_map/concatenate | solution.py:295
  43.2 2.8 %collective-permute-start.8 = (bf16[576,1024]{1,0:T(8,128)(2,1)}, bf16[576,1024]{1,0:T(8,128)(2,1)}, u32[]{:S(2)}, u32[]{:S(2)}) collective-permute-start(bf16[576,1024]{1,0:T(8,128)(2,1)} %pad_maximum_fusion.1.refs_0_), channel_id=1, source_target_pairs={{0,96},{32,0},{64,32},{96,64},{1,97},{33,1},{65,33},{97,65},{2,98}... | collective-permute-start | bytes 3538952 | tf_op jit(solution)/shard_map/ppermute | solution.py:267
  45.9 2.7 %pad_maximum_fusion.q_ref = bf16[1152,576]{1,0:T(8,128)(2,1)} fusion(bf16[576,576]{1,0:T(8,128)(2,1)S(1)} %collective-permute-done.q_ref, bf16[576,576]{1,0:T(8,128)(2,1)} %bitcast.10.clone.2.q_ref), kind=kLoop, calls=%fused_computation.1 | loop fusion | flops 2654208 | bytes 2654208 | tf_op jit(solution)/shard_map/concatenate | solution.py:298
  49.5 6.2 %all-to-all-start.1 = ((bf16[72,16,576]{2,1,0:T(8,128)(2,1)}), bf16[72,16,576]{2,1,0:T(8,128)(2,1)S(1)}, u32[]{:S(2)}, u32[]{:S(2)}) async-start(bf16[72,16,576]{2,1,0:T(8,128)(2,1)} %param.10), calls=%async_computation.1 | async-start | bytes 2949120 | tf_op jit(solution)/shard_map/all_to_all | solution.py:280
  55.7 6.4 %prefix_attend.4 = (f32[1152,256]{1,0:T(8,128)}, f32[1152,512]{1,0:T(8,128)}) custom-call(bf16[1152,576]{1,0:T(8,128)(2,1)} %pad_maximum_fusion.q_ref, bf16[576,1024]{1,0:T(8,128)(2,1)} %pad_maximum_fusion.1.refs_0_), custom_call_target="tpu_custom_call" | custom-call | flops 1000000 | bytes 1000000 | tf_op jit(solution)/shard_map/prefix_attend/pallas_call | solution.py:114
  62.1 7.9 %collective-permute-done.8.refs_1_ = bf16[576,1024]{1,0:T(8,128)(2,1)} collective-permute-done((bf16[576,1024]{1,0:T(8,128)(2,1)}, bf16[576,1024]{1,0:T(8,128)(2,1)}, u32[]{:S(2)}, u32[]{:S(2)}) %collective-permute-start.8) | collective-permute-done | bytes 1179680 | tf_op jit(solution)/shard_map/ppermute | solution.py:267
  70.0 3.4 %collective-permute-done.7.refs_0_ = bf16[576,1024]{1,0:T(8,128)(2,1)} collective-permute-done((bf16[576,1024]{1,0:T(8,128)(2,1)}, bf16[576,1024]{1,0:T(8,128)(2,1)}, u32[]{:S(2)}, u32[]{:S(2)}) %collective-permute-start.7) | collective-permute-done | bytes 1179680 | tf_op jit(solution)/shard_map/ppermute | solution.py:267
  73.4 3.8 %all-to-all-done.1 = bf16[72,16,576]{2,1,0:T(8,128)(2,1)S(1)} async-done(((bf16[72,16,576]{2,1,0:T(8,128)(2,1)}), bf16[72,16,576]{2,1,0:T(8,128)(2,1)S(1)}, u32[]{:S(2)}, u32[]{:S(2)}) %all-to-all-start.1) | async-done | bytes 1327136 | tf_op jit(solution)/shard_map/all_to_all | solution.py:280
  79.9 2.0 %collective-permute-start.11 = (bf16[576,512]{1,0:T(8,128)(2,1)}, bf16[576,512]{1,0:T(8,128)(2,1)}, u32[]{:S(2)}, u32[]{:S(2)}) collective-permute-start(bf16[576,512]{1,0:T(8,128)(2,1)} %pad_maximum_fusion.4), channel_id=1, source_target_pairs={{0,64},{32,96},{64,0},{96,32},{1,65},{33,97},{65,1},{97,33},{2,66}... | collective-permute-start | bytes 1769480 | tf_op jit(solution)/shard_map/ppermute | solution.py:267
  81.9 6.6 %tail_attend.1 = bf16[8,9,8,640]{3,2,1,0:T(8,128)(2,1)} custom-call(s32[9]{0:T(128)} %dynamic_slice.3.length_ref, s32[1]{0:T(128)} %bitcast.core_ref, bf16[8,9,8,576]{3,2,1,0:T(8,128)(2,1)} %bitcast.14, bf16[8,9,16,576]{3,2,1,0:T(8,128)(2,1)} %bitcast.13, bf16[8,9,16,576]{3,2,1,0:T(8,128)(2,1)} %collective-permute-done.9.other_ref), custom_call_target="tpu_custom_call" | custom-call | flops 1000000 | bytes 1000000 | tf_op jit(solution)/shard_map/tail_attend/pallas_call | solution.py:165
  88.5 3.5 %all-to-all-start.2 = ((bf16[72,8,640]{2,1,0:T(8,128)(2,1)}), bf16[72,8,640]{2,1,0:T(8,128)(2,1)S(1)}, u32[]{:S(2)}, u32[]{:S(2)}) async-start(bf16[72,8,640]{2,1,0:T(8,128)(2,1)} %bitcast.15), calls=%async_computation.2 | async-start | bytes 1474560 | tf_op jit(solution)/shard_map/all_to_all | solution.py:280
  93.1 2.0 %collective-permute-start.10 = (bf16[576,512]{1,0:T(8,128)(2,1)S(1)}, bf16[576,512]{1,0:T(8,128)(2,1)S(1)}, u32[]{:S(2)}, u32[]{:S(2)}) collective-permute-start(bf16[576,512]{1,0:T(8,128)(2,1)S(1)} %pad_maximum_fusion.3), channel_id=1, source_target_pairs={{0,64},{32,96},{64,0},{96,32},{1,65},{33,97},{65,1},{97,33},{2,66}... | collective-permute-start | bytes 1769480 | tf_op jit(solution)/shard_map/ppermute | solution.py:267
  95.1 11.1 %prefix_attend.5 = (f32[1152,256]{1,0:T(8,128)}, f32[1152,512]{1,0:T(8,128)}) custom-call(bf16[1152,576]{1,0:T(8,128)(2,1)} %pad_maximum_fusion.q_ref, bf16[576,1024]{1,0:T(8,128)(2,1)} %collective-permute-done.7.refs_0_, bf16[576,1024]{1,0:T(8,128)(2,1)} %collective-permute-done.8.refs_1_, f32[1152,256]{1,0:T(8,128)} %get-tuple-element.37.refs_2_, ...), custom_call_target="tpu_custom_call" | custom-call | flops 1000000 | bytes 1000000 | tf_op jit(solution)/shard_map/prefix_attend/pallas_call | solution.py:114
  106.2 3.8 %collective-permute-done.10.refs_0_ = bf16[576,512]{1,0:T(8,128)(2,1)S(1)} collective-permute-done((bf16[576,512]{1,0:T(8,128)(2,1)S(1)}, bf16[576,512]{1,0:T(8,128)(2,1)S(1)}, u32[]{:S(2)}, u32[]{:S(2)}) %collective-permute-start.10) | collective-permute-done | bytes 589856 | tf_op jit(solution)/shard_map/ppermute | solution.py:267
  110.8 4.8 %prefix_attend.7 = bf16[576,640]{1,0:T(8,128)(2,1)} custom-call(bf16[576,576]{1,0:T(8,128)(2,1)} %copy-done.2, bf16[576,512]{1,0:T(8,128)(2,1)} %copy-done.5, bf16[576,512]{1,0:T(8,128)(2,1)} %collective-permute-done.11.refs_1_, f32[1152,256]{1,0:T(8,128)} %get-tuple-element.44.refs_2_, f32[1152,512]{1,0:T(8,128)} %get-tuple-element.45.refs_3_), custom_call_target="tpu_custom_call" | custom-call | flops 1000000 | bytes 1000000 | tf_op jit(solution)/shard_map/prefix_attend/pallas_call | solution.py:114
  115.6 4.9 %prefix_attend.6.own_ref = bf16[576,640]{1,0:T(8,128)(2,1)} custom-call(bf16[576,576]{1,0:T(8,128)(2,1)} %bitcast.10.clone.2.q_ref, bf16[576,512]{1,0:T(8,128)(2,1)} %copy-done.5, bf16[576,512]{1,0:T(8,128)(2,1)} %collective-permute-done.11.refs_1_, f32[1152,256]{1,0:T(8,128)} %get-tuple-element.44.refs_2_, f32[1152,512]{1,0:T(8,128)} %get-tuple-element.45.refs_3_), custom_call_target="tpu_custom_call" | custom-call | flops 1000000 | bytes 1000000 | tf_op jit(solution)/shard_map/prefix_attend/pallas_call | solution.py:114
  121.4 12.8 %finish.1 = (bf16[8,72,448]{2,1,0:T(8,128)(2,1)}, bf16[8,72,448]{2,1,0:T(8,128)(2,1)}) custom-call(s32[1]{0:T(128)} %bitcast.core_ref, bf16[576,640]{1,0:T(8,128)(2,1)} %prefix_attend.6.own_ref, bf16[576,640]{1,0:T(8,128)(2,1)} %copy-done.7, bf16[576,640]{1,0:T(8,128)(2,1)} %bitcast.16, bf16[8,512,128]{2,1,0:T(8,128)(2,1)} %up_ref.1, bf16[1024,7168]{1,0:T(8,128)(2,1)} %proj_ref.1), custom_call_target="tpu_custom_call" | custom-call | flops 1000000 | bytes 1000000 | tf_op jit(solution)/shard_map/finish/pallas_call | solution.py:226
  137.8 19.6 %all_to_all.20 = bf16[8,72,448]{2,1,0:T(8,128)(2,1)S(1)} all-to-all(bf16[8,72,448]{2,1,0:T(8,128)(2,1)S(1)} %add_convert_fusion), channel_id=1, replica_groups=mesh['x'=4,'z_lo'=2,'z_hi'=2,'y'=4,'core'=2] {'z_hi','y'}, dimensions={0} | all-to-all | bytes 1032192 | tf_op jit(solution)/shard_map/all_to_all | solution.py:280
  (56 shorter events, 20.4 us)
Async XLA Ops:
  0.0 1.5 copy-start
  1.5 1.2 copy-start.6
  3.0 1.0 copy-start.8
  4.1 41.9 %collective-permute-start = (bf16[576,576]{1,0:T(8,128)(2,1)}, bf16[576,576]{1,0:T(8,128)(2,1)S(1)}, u32[]{:S(2)}, u32[]{:S(2)}) collective-permute-start(bf16[576,576]{1,0:T(8,128)(2,1)} %bitcast.10.clone.2.q_ref), channel_id=1, source_target_pairs={{0,1},{1,0},{2,3},{3,2},{4,5},{5,4},{6,7},{7,6},{8,9},{9,8},{10,11... | collective-permute-start | bytes 1990664 | tf_op jit(solution)/shard_map/ppermute | solution.py:270
  4.2 8.2 %collective-permute-start.3 = (bf16[64,576]{0,1:T(8,128)(2,1)S(1)}, bf16[64,576]{0,1:T(8,128)(2,1)S(1)}, u32[]{:S(2)}, u32[]{:S(2)}) collective-permute-start(bf16[64,576]{0,1:T(8,128)(2,1)S(1)} %copy.27), channel_id=1, source_target_pairs={{0,4},{2,6},{4,0},{6,2},{1,5},{3,7},{5,1},{7,3},{8,12},{10,14},{12... | collective-permute-start | bytes 221192 | tf_op jit(solution)/shard_map/ppermute | solution.py:267
  7.6 8.1 %collective-permute-start.2 = (bf16[64,576]{0,1:T(8,128)(2,1)S(1)}, bf16[64,576]{0,1:T(8,128)(2,1)S(1)}, u32[]{:S(2)}, u32[]{:S(2)}) collective-permute-start(bf16[64,576]{0,1:T(8,128)(2,1)S(1)} %copy.27), channel_id=1, source_target_pairs={{0,6},{2,0},{4,2},{6,4},{1,7},{3,1},{5,3},{7,5},{8,14},{10,8},{12,... | collective-permute-start | bytes 221192 | tf_op jit(solution)/shard_map/ppermute | solution.py:267
  8.6 7.1 %collective-permute-start.1 = (bf16[64,576]{0,1:T(8,128)(2,1)S(1)}, bf16[64,576]{0,1:T(8,128)(2,1)S(1)}, u32[]{:S(2)}, u32[]{:S(2)}) collective-permute-start(bf16[64,576]{0,1:T(8,128)(2,1)S(1)} %copy.27), channel_id=1, source_target_pairs={{0,2},{2,4},{4,6},{6,0},{1,3},{3,5},{5,7},{7,1},{8,10},{10,12},{12... | collective-permute-start | bytes 221192 | tf_op jit(solution)/shard_map/ppermute | solution.py:267
  15.9 12.0 %collective-permute-start.6 = (bf16[576,256]{1,0:T(8,128)(2,1)S(1)}, bf16[576,256]{1,0:T(8,128)(2,1)}, u32[]{:S(2)}, u32[]{:S(2)}) collective-permute-start(bf16[576,256]{1,0:T(8,128)(2,1)S(1)} %maximum_bitcast_fusion), channel_id=1, source_target_pairs={{0,8},{16,24},{8,0},{24,16},{1,9},{17,25},{9,1},{25,17},{2,10},{18... | collective-permute-start | bytes 884744 | tf_op jit(solution)/shard_map/ppermute | solution.py:277
  19.8 21.0 %collective-permute-start.5 = (bf16[576,256]{1,0:T(8,128)(2,1)S(1)}, bf16[576,256]{1,0:T(8,128)(2,1)}, u32[]{:S(2)}, u32[]{:S(2)}) collective-permute-start(bf16[576,256]{1,0:T(8,128)(2,1)S(1)} %maximum_bitcast_fusion), channel_id=1, source_target_pairs={{0,24},{16,0},{8,16},{24,8},{1,25},{17,1},{9,17},{25,9},{2,26},{18... | collective-permute-start | bytes 884744 | tf_op jit(solution)/shard_map/ppermute | solution.py:277
  20.6 20.3 %collective-permute-start.4 = (bf16[576,256]{1,0:T(8,128)(2,1)S(1)}, bf16[576,256]{1,0:T(8,128)(2,1)}, u32[]{:S(2)}, u32[]{:S(2)}) collective-permute-start(bf16[576,256]{1,0:T(8,128)(2,1)S(1)} %maximum_bitcast_fusion), channel_id=1, source_target_pairs={{0,16},{16,8},{8,24},{24,0},{1,17},{17,9},{9,25},{25,1},{2,18},{18... | collective-permute-start | bytes 884744 | tf_op jit(solution)/shard_map/ppermute | solution.py:277
  21.9 26.7 %all-to-all-start = ((bf16[72,8,576]{2,1,0:T(8,128)(2,1)}), bf16[72,8,576]{2,1,0:T(8,128)(2,1)S(1)}, u32[]{:S(2)}, u32[]{:S(2)}) async-start(bf16[72,8,576]{2,1,0:T(8,128)(2,1)} %copy.32), calls=%async_computation | async-start | bytes 1474560 | tf_op jit(solution)/shard_map/all_to_all | solution.py:280
  43.2 26.8 %collective-permute-start.8 = (bf16[576,1024]{1,0:T(8,128)(2,1)}, bf16[576,1024]{1,0:T(8,128)(2,1)}, u32[]{:S(2)}, u32[]{:S(2)}) collective-permute-start(bf16[576,1024]{1,0:T(8,128)(2,1)} %pad_maximum_fusion.1.refs_0_), channel_id=1, source_target_pairs={{0,96},{32,0},{64,32},{96,64},{1,97},{33,1},{65,33},{97,65},{2,98}... | collective-permute-start | bytes 3538952 | tf_op jit(solution)/shard_map/ppermute | solution.py:267
  45.9 27.5 %collective-permute-start.7 = (bf16[576,1024]{1,0:T(8,128)(2,1)}, bf16[576,1024]{1,0:T(8,128)(2,1)}, u32[]{:S(2)}, u32[]{:S(2)}) collective-permute-start(bf16[576,1024]{1,0:T(8,128)(2,1)} %pad_maximum_fusion.1.refs_0_), channel_id=1, source_target_pairs={{0,32},{32,64},{64,96},{96,0},{1,33},{33,65},{65,97},{97,1},{2,34}... | collective-permute-start | bytes 3538952 | tf_op jit(solution)/shard_map/ppermute | solution.py:267
  45.9 2.7 %copy-start.2 = (bf16[576,576]{1,0:T(8,128)(2,1)}, bf16[576,576]{1,0:T(8,128)(2,1)S(1)}, u32[]{:S(2)}) copy-start(bf16[576,576]{1,0:T(8,128)(2,1)S(1)} %collective-permute-done.q_ref) | copy-start | bytes 1990660
  49.5 27.8 %all-to-all-start.1 = ((bf16[72,16,576]{2,1,0:T(8,128)(2,1)}), bf16[72,16,576]{2,1,0:T(8,128)(2,1)S(1)}, u32[]{:S(2)}, u32[]{:S(2)}) async-start(bf16[72,16,576]{2,1,0:T(8,128)(2,1)} %param.10), calls=%async_computation.1 | async-start | bytes 2949120 | tf_op jit(solution)/shard_map/all_to_all | solution.py:280
  55.7 21.6 %copy-start.9 = (s32[72]{0:T(128)S(1)}, s32[72]{0:T(128)}, u32[]{:S(2)}) copy-start(s32[72]{0:T(128)} %param.11) | copy-start | bytes 868
  77.2 4.7 %copy-start.1 = (bf16[72,16,576]{2,1,0:T(8,128)(2,1)}, bf16[72,16,576]{2,1,0:T(8,128)(2,1)S(1)}, u32[]{:S(2)}) copy-start(bf16[72,16,576]{2,1,0:T(8,128)(2,1)S(1)} %all-to-all-done.1) | copy-start | bytes 3981316
  77.2 4.7 %collective-permute-start.9 = (bf16[8,9,16,576]{3,2,1,0:T(8,128)(2,1)S(1)}, bf16[8,9,16,576]{3,2,1,0:T(8,128)(2,1)}, u32[]{:S(2)}, u32[]{:S(2)}) collective-permute-start(bf16[8,9,16,576]{3,2,1,0:T(8,128)(2,1)S(1)} %bitcast.12), channel_id=1, source_target_pairs={{0,1},{1,0},{2,3},{3,2},{4,5},{5,4},{6,7},{7,6},{8,9},{9,8},{10,11... | collective-permute-start | bytes 3981320 | tf_op jit(solution)/shard_map/ppermute | solution.py:270
  79.9 26.3 %collective-permute-start.11 = (bf16[576,512]{1,0:T(8,128)(2,1)}, bf16[576,512]{1,0:T(8,128)(2,1)}, u32[]{:S(2)}, u32[]{:S(2)}) collective-permute-start(bf16[576,512]{1,0:T(8,128)(2,1)} %pad_maximum_fusion.4), channel_id=1, source_target_pairs={{0,64},{32,96},{64,0},{96,32},{1,65},{33,97},{65,1},{97,33},{2,66}... | collective-permute-start | bytes 1769480 | tf_op jit(solution)/shard_map/ppermute | solution.py:267
  88.5 21.5 %all-to-all-start.2 = ((bf16[72,8,640]{2,1,0:T(8,128)(2,1)}), bf16[72,8,640]{2,1,0:T(8,128)(2,1)S(1)}, u32[]{:S(2)}, u32[]{:S(2)}) async-start(bf16[72,8,640]{2,1,0:T(8,128)(2,1)} %bitcast.15), calls=%async_computation.2 | async-start | bytes 1474560 | tf_op jit(solution)/shard_map/all_to_all | solution.py:280
  93.1 16.9 %collective-permute-start.10 = (bf16[576,512]{1,0:T(8,128)(2,1)S(1)}, bf16[576,512]{1,0:T(8,128)(2,1)S(1)}, u32[]{:S(2)}, u32[]{:S(2)}) collective-permute-start(bf16[576,512]{1,0:T(8,128)(2,1)S(1)} %pad_maximum_fusion.3), channel_id=1, source_target_pairs={{0,64},{32,96},{64,0},{96,32},{1,65},{33,97},{65,1},{97,33},{2,66}... | collective-permute-start | bytes 1769480 | tf_op jit(solution)/shard_map/ppermute | solution.py:267
  110.0 5.6 %copy-start.4 = (bf16[72,8,640]{2,1,0:T(8,128)(2,1)}, bf16[72,8,640]{2,1,0:T(8,128)(2,1)S(1)}, u32[]{:S(2)}) copy-start(bf16[72,8,640]{2,1,0:T(8,128)(2,1)S(1)} %all-to-all-done.2) | copy-start | bytes 2211844
  115.6 4.9 %collective-permute-start.12 = (bf16[576,640]{1,0:T(8,128)(2,1)}, bf16[576,640]{1,0:T(8,128)(2,1)S(1)}, u32[]{:S(2)}, u32[]{:S(2)}) collective-permute-start(bf16[576,640]{1,0:T(8,128)(2,1)} %prefix_attend.7), channel_id=1, source_target_pairs={{0,1},{1,0},{2,3},{3,2},{4,5},{5,4},{6,7},{7,6},{8,9},{9,8},{10,11... | collective-permute-start | bytes 2211848 | tf_op jit(solution)/shard_map/ppermute | solution.py:270
  134.3 2.3 %collective-permute-start.13 = (bf16[8,72,448]{2,1,0:T(8,128)(2,1)}, bf16[8,72,448]{2,1,0:T(8,128)(2,1)S(1)}, u32[]{:S(2)}, u32[]{:S(2)}) collective-permute-start(bf16[8,72,448]{2,1,0:T(8,128)(2,1)} %get-tuple-element.48), channel_id=1, source_target_pairs={{0,1},{1,0},{2,3},{3,2},{4,5},{5,4},{6,7},{7,6},{8,9},{9,8},{10,11... | collective-permute-start | bytes 1548296 | tf_op jit(solution)/shard_map/ppermute | solution.py:270
  (3 other events, 2.6 us)

commit v3 on v2

v3 whole, which is shorter than its diff:
```python
import functools
import math

import jax
import jax.numpy as jnp
from jax import lax
from jax.experimental import pallas as pl
from jax.experimental.pallas import tpu as pltpu
from jax.sharding import Mesh, PartitionSpec as P

ROW_BLOCK = 288
KEY_BLOCK = 512
VMEM = 58 * 1024 * 1024
COST = pl.CostEstimate(flops=10**11, bytes_accessed=10**8, transcendentals=0)


def pack(acc, weight_sum, highest, exponent_scale):
    context = (acc / weight_sum).astype(jnp.bfloat16)
    level = highest * exponent_scale + jnp.log2(weight_sum)
    high = level.astype(jnp.bfloat16).astype(jnp.float32)
    middle = (level - high).astype(jnp.bfloat16).astype(jnp.float32)
    low = level - high - middle
    lane = lax.broadcasted_iota(jnp.int32, (acc.shape[0], 128), 1)
    terms = jnp.where(
        lane == 0, high, jnp.where(lane == 1, middle, jnp.where(lane == 2, low, 0.0))
    )
    return context, terms.astype(jnp.bfloat16)


def attend_kernel(first, last, width, exponent_scale, key_count, q_ref, *refs):
    key_refs = refs[:key_count]
    refs = refs[key_count:]
    q = q_ref[...]
    if first:
        highest = weight_sum = acc = None
    else:
        stat_ref, acc_ref = refs[:2]
        refs = refs[2:]
        highest = stat_ref[:, 0:1]
        weight_sum = stat_ref[:, 128:129]
        acc = acc_ref[...]
    blocks = [
        (k_ref, at) for k_ref in key_refs for at in range(0, k_ref.shape[1], KEY_BLOCK)
    ]

    def scores_of(block):
        k_ref, at = block
        return jnp.dot(
            q, k_ref[:, at : at + KEY_BLOCK], preferred_element_type=jnp.float32
        )

    scores = scores_of(blocks[0])
    for place, (k_ref, at) in enumerate(blocks):
        upcoming = scores_of(blocks[place + 1]) if place + 1 < len(blocks) else None
        block_highest = jnp.max(scores, axis=1, keepdims=True)
        new_highest = (
            block_highest if highest is None else jnp.maximum(highest, block_highest)
        )
        w = jnp.exp2((scores - new_highest) * exponent_scale)
        part_sum = jnp.sum(w, axis=1, keepdims=True)
        part = lax.dot_general(
            w.astype(jnp.bfloat16),
            k_ref[:width, at : at + KEY_BLOCK],
            (((1,), (1,)), ((), ())),
            preferred_element_type=jnp.float32,
        )
        if highest is None:
            weight_sum, acc = part_sum, part
        else:
            fade = jnp.exp2((highest - new_highest) * exponent_scale)
            weight_sum = weight_sum * fade + part_sum
            acc = acc * fade + part
        highest, scores = new_highest, upcoming
    if last:
        (out_ref,) = refs
        out_ref[:, :width], out_ref[:, width:] = pack(acc, weight_sum, highest, exponent_scale)
    else:
        out_stat_ref, out_acc_ref = refs
        out_stat_ref[:, :128] = jnp.broadcast_to(highest, (q.shape[0], 128))
        out_stat_ref[:, 128:] = jnp.broadcast_to(weight_sum, (q.shape[0], 128))
        out_acc_ref[...] = acc


def attend(q, keys, state, last, width, exponent_scale, second=False, cost=COST):
    rows, features = q.shape
    first = state is None
    row_map = lambda i: (i, 0)
    all_map = lambda i: (0, 0)
    in_specs = [pl.BlockSpec((ROW_BLOCK, features), row_map)]
    in_specs += [pl.BlockSpec(k.shape, all_map) for k in keys]
    args = [q, *keys]
    state_specs = (
        pl.BlockSpec((ROW_BLOCK, 256), row_map),
        pl.BlockSpec((ROW_BLOCK, width), row_map),
    )
    skip = rows // ROW_BLOCK if second else 0
    old_map = lambda i: (i + skip, 0)
    if not first:
        in_specs += [
            pl.BlockSpec((ROW_BLOCK, 256), old_map),
            pl.BlockSpec((ROW_BLOCK, width), old_map),
        ]
        args += list(state)
    if last:
        out_shape = jax.ShapeDtypeStruct((rows, width + 128), jnp.bfloat16)
        out_specs = pl.BlockSpec((ROW_BLOCK, width + 128), row_map)
    else:
        out_shape = (
            jax.ShapeDtypeStruct((rows, 256), jnp.float32),
            jax.ShapeDtypeStruct((rows, width), jnp.float32),
        )
        out_specs = state_specs
    return pl.pallas_call(
        functools.partial(attend_kernel, first, last, width, exponent_scale, len(keys)),
        grid=(rows // ROW_BLOCK,),
        in_specs=in_specs,
        out_specs=out_specs,
        out_shape=out_shape,
        compiler_params=pltpu.CompilerParams(vmem_limit_bytes=VMEM),
        cost_estimate=cost,
        name="prefix_attend",
    )(*args)


def tail_kernel(span, width, exponent_scale, length_ref, joined_ref, out_ref):
    sources, _, tall, features = joined_ref.shape
    heads = tall - span
    keys = joined_ref[:, 0, :span].reshape(sources * span, features)
    q = joined_ref[:, 0, span:].reshape(sources * heads, features)
    s = lax.dot_general(q, keys, (((1,), (1,)), ((), ())), preferred_element_type=jnp.float32)
    usable = lax.broadcasted_iota(jnp.int32, s.shape, 1) < length_ref[pl.program_id(0)]
    s = jnp.where(usable, s, -1e30)
    highest = jnp.max(s, axis=1, keepdims=True)
    w = jnp.where(usable, jnp.exp2((s - highest) * exponent_scale), 0.0)
    weight_sum = jnp.sum(w, axis=1, keepdims=True)
    acc = jnp.dot(w.astype(jnp.bfloat16), keys[:, :width], preferred_element_type=jnp.float32)
    context, level = pack(acc, weight_sum, highest, exponent_scale)
    out_ref[:, 0, :, :width] = context.reshape(sources, heads, width)
    out_ref[:, 0, :, width:] = level.reshape(sources, heads, 128)


def attend_tails(joined, span, length, width, exponent_scale):
    sources, slots, tall, features = joined.shape
    heads = tall - span
    block = lambda last2, last1: pl.BlockSpec(
        (sources, 1, last2, last1), lambda i, *_: (0, i, 0, 0)
    )
    return pl.pallas_call(
        functools.partial(tail_kernel, span, width, exponent_scale),
        grid_spec=pltpu.PrefetchScalarGridSpec(
            num_scalar_prefetch=1,
            grid=(slots,),
            in_specs=[block(tall, features)],
            out_specs=block(heads, width + 128),
        ),
        out_shape=jax.ShapeDtypeStruct((sources, slots, heads, width + 128), jnp.bfloat16),
        compiler_params=pltpu.CompilerParams(vmem_limit_bytes=VMEM),
        cost_estimate=COST,
        name="tail_attend",
    )(length, joined)


def project(core, order_ref, head, proj_ref, keep_ref, give_ref, block_refs, sems, between):
    columns = block_refs.shape[2]
    copies = [
        pltpu.make_async_copy(
            proj_ref.at[:, pl.ds(pl.multiple_of(order_ref[i] * columns, 128), columns)],
            block_refs.at[i],
            sems.at[i],
        )
        for i in range(block_refs.shape[0])
    ]
    for copy in copies:
        copy.start()
    head = between() if head is None else head
    half = columns // 2
    early = core == 0
    for i, copy in enumerate(copies):
        copy.wait()
        mixed = jnp.dot(head, block_refs[i], preferred_element_type=jnp.float32)
        mixed = mixed.astype(jnp.bfloat16)
        keep_ref[i] = jnp.where(early, mixed[:, :half], mixed[:, half:])
        give_ref[i] = jnp.where(early, mixed[:, half:], mixed[:, :half])


def first_kernel(
    width, core_ref, order_ref, own_ref, received_ref, tail_ref, up_ref, proj_ref,
    keep_ref, give_ref, head_ref, context_ref, block_refs, sems,
):
    heads, _, value_width = up_ref.shape
    req_rows = head_ref.shape[0]

    def make_head():
        refs = (own_ref, received_ref, tail_ref)
        levels = [
            jnp.sum(ref[:, width:].astype(jnp.float32), axis=1, keepdims=True) for ref in refs
        ]
        top = functools.reduce(jnp.maximum, levels)
        shares = [jnp.exp2(level - top) for level in levels]
        total = shares[0] + shares[1] + shares[2]
        context = sum(
            ref[:, :width].astype(jnp.float32) * (share / total)
            for ref, share in zip(refs, shares)
        )
        context_ref[...] = context.reshape(req_rows, heads, width)
        for h in range(heads):
            head_ref[:, h * value_width : (h + 1) * value_width] = jnp.dot(
                context_ref[:, h, :].astype(jnp.bfloat16),
                up_ref[h],
                preferred_element_type=jnp.float32,
            ).astype(jnp.bfloat16)
        return head_ref[...]

    project(
        core_ref[0], order_ref, None, proj_ref, keep_ref, give_ref, block_refs, sems, make_head
    )


def second_kernel(
    core_ref, order_ref, head_ref, proj_ref, keep_ref, give_ref, block_refs, sems
):
    project(
        core_ref[0], order_ref, head_ref[...], proj_ref, keep_ref, give_ref, block_refs, sems, None
    )


def finish(args, head, out_proj, value_up, core, order, chips):
    heads, width, value_width = value_up.shape
    depth, columns = out_proj.shape
    block = columns // chips
    count = order.shape[0]
    vmem = pl.BlockSpec(memory_space=pltpu.VMEM)
    smem = pl.BlockSpec(memory_space=pltpu.SMEM)
    req_rows = (args[0].shape[0] // heads) if head is None else head.shape[0]
    half = jax.ShapeDtypeStruct((count, req_rows, block // 2), jnp.bfloat16)
    scratch = [
        pltpu.VMEM((count, depth, block), jnp.bfloat16),
        pltpu.SemaphoreType.DMA((count,)),
    ]
    common = dict(
        compiler_params=pltpu.CompilerParams(vmem_limit_bytes=VMEM), cost_estimate=COST
    )
    anywhere = pl.BlockSpec(memory_space=pl.ANY)
    if head is None:
        return pl.pallas_call(
            functools.partial(first_kernel, width),
            in_specs=[smem, smem, vmem, vmem, vmem, vmem, anywhere],
            out_specs=(vmem, vmem, vmem),
            out_shape=(
                half,
                half,
                jax.ShapeDtypeStruct((req_rows, heads * value_width), jnp.bfloat16),
            ),
            scratch_shapes=[pltpu.VMEM((req_rows, heads, width), jnp.float32)] + scratch,
            name="finish_first",
            **common,
        )(core, order, *args, value_up, out_proj)
    return pl.pallas_call(
        second_kernel,
        in_specs=[smem, smem, vmem, anywhere],
        out_specs=(vmem, vmem),
        out_shape=(half, half),
        scratch_shapes=scratch,
        name="finish_second",
        **common,
    )(core, order, head, out_proj)


def on_device(
    queries, prefix_latent, tail_latent, tail_length, slot_request, key_absorb, value_up, out_proj
):
    heads_here, nope_width, latent_width = key_absorb.shape
    value_width = value_up.shape[2]
    req_rows = slot_request.shape[0]
    features = prefix_latent.shape[1]
    rope_width = features - latent_width
    exponent_scale = math.log2(math.e) / math.sqrt(nope_width + rope_width)
    core = lax.axis_index("core")
    core_at = core.reshape(1)
    z_high, y_at = lax.axis_index("z_hi"), lax.axis_index("y")
    high_size, y_size = lax.axis_size("z_hi"), lax.axis_size("y")
    chips = high_size * y_size
    devices = chips * 2
    device = (z_high * y_size + y_at) * 2 + core
    slots = -(-req_rows // devices)
    span = tail_latent.shape[1]

    def ring(value, axis, by):
        size = lax.axis_size(axis)
        return lax.ppermute(value, axis, [(i, (i + by) % size) for i in range(size)])

    def other_core(value):
        return lax.ppermute(value, "core", [(0, 1), (1, 0)])

    def z_ring(value, by):
        low, high = lax.axis_size("z_lo"), lax.axis_size("z_hi")
        size = low * high
        place = lambda z: (z % low) * high + z // low
        pairs = [(place(z), place((z + by) % size)) for z in range(size)]
        return lax.ppermute(value, ("z_lo", "z_hi"), pairs)

    def exchange(value):
        return lax.all_to_all(value, ("z_hi", "y", "core"), 0, 0, tiled=True)

    def chip_shift(value, by_high, by_y):
        place = lambda z, y: (z % high_size) * y_size + y % y_size
        pairs = [
            (place(z, y), place(z + by_high, y + by_y))
            for z in range(high_size)
            for y in range(y_size)
        ]
        return lax.ppermute(value, ("z_hi", "y"), pairs)

    picked = jnp.take(queries, slot_request, axis=0).reshape(
        req_rows, heads_here, nope_width + rope_width
    )
    query_latent = jnp.einsum(
        "rhn,hnl->rhl", picked[:, :, :nope_width], key_absorb, preferred_element_type=jnp.float32
    ).astype(jnp.bfloat16)
    query_full = jnp.concatenate([query_latent, picked[:, :, nope_width:]], axis=2)
    query_rows = query_full.reshape(req_rows * heads_here, features)

    held = jnp.concatenate(
        [prefix_latent] + [ring(prefix_latent, "y", by) for by in (1, -1, 2)], axis=0
    ).T
    shifted = [z_ring(held, by) for by in (1, -1, 2)]
    held = [
        jnp.concatenate([held, shifted[0]], axis=1),
        jnp.concatenate([shifted[1], shifted[2]], axis=1),
    ]
    joined = jnp.pad(
        jnp.concatenate([tail_latent, query_full], axis=1),
        ((0, slots * devices - req_rows), (0, 0), (0, 0)),
    )
    query_other = other_core(query_rows)
    both = jnp.concatenate([query_rows, query_other], axis=0)
    both, held, joined = lax.optimization_barrier((both, held, joined))

    right = [ring(half, "x", 1) for half in held]
    left = [ring(half, "x", -1) for half in held]

    joined = exchange(joined).reshape(devices, slots, span + heads_here, features)
    length = lax.dynamic_slice_in_dim(
        jnp.pad(tail_length, (0, slots * devices - req_rows), constant_values=1),
        device * slots,
        slots,
    )

    go = functools.partial(attend, width=latent_width, exponent_scale=exponent_scale)
    far = [ring(right[0], "x", 1), ring(left[1], "x", -1)]
    state = go(both, held, None, False)

    state = go(both, right + left, state, False, cost=None)
    joined, state = lax.optimization_barrier((joined, state))
    tail_part = attend_tails(joined, span, length, latent_width, exponent_scale)
    tail_part, state = lax.optimization_barrier((tail_part, state))
    tail_part = exchange(tail_part.reshape(devices * slots, heads_here, latent_width + 128))
    tail_part = tail_part[:req_rows].reshape(req_rows * heads_here, latent_width + 128)

    packed_other = go(query_other, far, state, True, second=True, cost=None)
    received = other_core(packed_other)
    packed_own = go(query_rows, far, state, True, cost=None)

    moves = [(1, by) for by in range(y_size)] + [(0, by) for by in (1, 2, 3, 0)]
    order = jnp.stack(
        [
            ((z_high + by_high) % high_size) * y_size + (y_at + by_y) % y_size
            for by_high, by_y in moves
        ]
    ).astype(jnp.int32)
    run = functools.partial(
        finish, out_proj=out_proj, value_up=value_up, core=core_at, chips=chips
    )
    keep, give, head = run((packed_own, received, tail_part), None, order=order[:y_size])
    first = (keep, other_core(give))
    keep, give = run((), head, order=order[y_size:])
    second = (keep, other_core(give))
    paired = [
        (mine[i].astype(jnp.float32) + theirs[i].astype(jnp.float32))
        for mine, theirs in (first, second)
        for i in range(y_size)
    ]
    total = paired[-1]
    for (by_high, by_y), value in zip(moves[:-1], paired[:-1]):
        total += chip_shift(value.astype(jnp.bfloat16), by_high, by_y).astype(jnp.float32)
    return total.astype(jnp.bfloat16)


def solution(mesh):
    fine = Mesh(
        mesh.devices.reshape(4, 2, 2, 4, 2), ("x", "z_lo", "z_hi", "y", "core")
    )
    group, seq = ("x", "z_lo"), ("z_hi", "y", "core")
    placed = (
        P(None, seq),
        P(group + seq, None),
        P(group, seq, None),
        P(group),
        P(group),
        P(seq, None, None),
        P(seq, None, None),
        P(seq, None),
    )
    return jax.shard_map(
        on_device, mesh=fine, in_specs=placed, out_specs=P(group, seq), check_vma=False
    )
```

time: 159 us -> 145 us (0.912)
  blocking collectives: 19.6 us -> 0 us
  starting transfers between devices: 32.9 us -> 46.2 us
  waiting for transfers between devices: 41.3 us -> 31.9 us
  other arithmetic: 11.7 us -> 13.5 us
    all_to_all x1 -> x0, blocking collectives: 19.6 us -> none  [exchange(): return lax.all_to_all(value, ('z_hi', 'y'), 0, 0, tiled=True)]
    ppermute x0 -> x7, starting transfers between devices: none -> 14.3 us  [chip_shift(): return lax.ppermute(value, ('z_hi', 'y'), pairs)]
    ppermute x7 -> x9, waiting for transfers between devices: 21.2 us -> 14 us  [ring(): lax.ppermute(value, axis, [(i, (i + by) % size) for i in range(size)])]
    all_to_all x3 -> x2, starting transfers between devices: 14.3 us -> 10.3 us  [exchange(): return lax.all_to_all(value, ('z_hi', 'y', 'core'), 0, 0, tiled=True)]
    ppermute x7 -> x9, starting transfers between devices: 12.1 us -> 15.1 us  [ring(): lax.ppermute(value, axis, [(i, (i + by) % size) for i in range(size)])]
    ppermute x3, waiting for transfers between devices: 14.4 us -> 11.6 us  [z_ring(): return lax.ppermute(value, ('z_lo', 'z_hi'), pairs)]
    ppermute x0 -> x7, waiting for transfers between devices: none -> 1.98 us  [chip_shift(): return lax.ppermute(value, ('z_hi', 'y'), pairs)]
    ppermute x4, waiting for transfers between devices: 1.85 us -> 0.01 us  [other_core(): return lax.ppermute(value, 'core', [(0, 1), (1, 0)])]
  transfers between devices with their start and end apart: 17 -> 25, of which waited for: 9 -> 8; matrix products, arithmetic and copies ran while one was open for 6% -> 9% of each run, Pallas kernels for 18% -> 27%
where the time goes in v3:
time: 145 us; the launch traced here: 143 us
  starting transfers between devices  46.2 us (32%)
  Pallas kernels  45.7 us (32%)
  waiting for transfers between devices  31.9 us (22%)
  other arithmetic  13.5 us (9%)
  local copies, waits for them, and re-layouts  5.72 us (4%)
    pallas_call x4, Pallas kernels, attend(): pl.pallas_call(functools.partial(attend_kernel, first, last, width, expon...  27.2 us
    ppermute x9, starting transfers between devices, ring(): lax.ppermute(value, axis, [(i, (i + by) % size) for i in range(size)])  15.1 us
    ppermute x7, starting transfers between devices, chip_shift(): return lax.ppermute(value, ('z_hi', 'y'), pairs)  14.3 us
    ppermute x9, waiting for transfers between devices, ring(): lax.ppermute(value, axis, [(i, (i + by) % size) for i in range(size)])  14 us
    ppermute x3, waiting for transfers between devices, z_ring(): return lax.ppermute(value, ('z_lo', 'z_hi'), pairs)  11.6 us
    all_to_all x2, starting transfers between devices, exchange(): return lax.all_to_all(value, ('z_hi', 'y', 'core'), 0, 0, tiled=True)  10.3 us
    pallas_call x1, Pallas kernels, finish(): pl.pallas_call(functools.partial(first_kernel, width), in_specs=[smem, sm...  6.86 us
    pallas_call x1, Pallas kernels, attend_tails(): pl.pallas_call(functools.partial(tail_kernel, span, width, exponent_scale...  6.12 us
  transfers between devices with their start and end apart: 25, of which 8 were waited for; matrix products, arithmetic and copies ran while one was open for 9% of the time, Pallas kernels for 27%

profile of v3, /device:TPU:0, one launch (start us, length us, event | category | flops | bytes accessed | tf_op | source)
XLA Modules:
  0.0 143.5 jit_solution(2396845842924336143)
XLA Ops:
  4.5 2.1 %collective-permute-start.3 = (bf16[64,576]{0,1:T(8,128)(2,1)S(1)}, bf16[64,576]{0,1:T(8,128)(2,1)}, u32[]{:S(2)}, u32[]{:S(2)}) collective-permute-start(bf16[64,576]{0,1:T(8,128)(2,1)S(1)} %copy.20), channel_id=1, source_target_pairs={{0,4},{2,6},{4,0},{6,2},{1,5},{3,7},{5,1},{7,3},{8,12},{10,14},{12... | collective-permute-start | bytes 221192 | tf_op jit(solution)/shard_map/ppermute | solution.py:290
  10.7 1.9 %collective-permute-done.3 = bf16[64,576]{0,1:T(8,128)(2,1)} collective-permute-done((bf16[64,576]{0,1:T(8,128)(2,1)S(1)}, bf16[64,576]{0,1:T(8,128)(2,1)}, u32[]{:S(2)}, u32[]{:S(2)}) %collective-permute-start.3) | collective-permute-done | bytes 73760 | tf_op jit(solution)/shard_map/ppermute | solution.py:290
  14.0 4.1 %collective-permute-start.5 = (bf16[576,256]{1,0:T(8,128)(2,1)S(1)}, bf16[576,256]{1,0:T(8,128)(2,1)}, u32[]{:S(2)}, u32[]{:S(2)}) collective-permute-start(bf16[576,256]{1,0:T(8,128)(2,1)S(1)} %maximum_bitcast_fusion), channel_id=1, source_target_pairs={{0,24},{16,0},{8,16},{24,8},{1,25},{17,1},{9,17},{25,9},{2,26},{18... | collective-permute-start | bytes 884744 | tf_op jit(solution)/shard_map/ppermute | solution.py:300
  21.7 11.6 %collective-permute-done.4 = bf16[576,256]{1,0:T(8,128)(2,1)} collective-permute-done((bf16[576,256]{1,0:T(8,128)(2,1)S(1)}, bf16[576,256]{1,0:T(8,128)(2,1)}, u32[]{:S(2)}, u32[]{:S(2)}) %collective-permute-start.4) | collective-permute-done | bytes 294944 | tf_op jit(solution)/shard_map/ppermute | solution.py:300
  33.3 1.8 %pad_maximum_fusion.2.refs_0_ = bf16[576,512]{1,0:T(8,128)(2,1)} fusion(bf16[576,256]{1,0:T(8,128)(2,1)} %collective-permute-done.4, bf16[576,256]{1,0:T(8,128)(2,1)S(1)} %maximum_bitcast_fusion), kind=kLoop, calls=%fused_computation.10 | loop fusion | flops 1179648 | bytes 1179648 | tf_op jit(solution)/shard_map/concatenate | solution.py:328
  35.1 1.9 %pad_maximum_fusion.3.refs_1_ = bf16[576,512]{1,0:T(8,128)(2,1)} fusion(bf16[576,256]{1,0:T(8,128)(2,1)} %collective-permute-done.6, bf16[576,256]{1,0:T(8,128)(2,1)} %collective-permute-done.5), kind=kLoop, calls=%fused_computation.11 | loop fusion | flops 1179648 | bytes 1179648 | tf_op jit(solution)/shard_map/concatenate | solution.py:329
  38.4 2.8 %collective-permute-start.9 = (bf16[576,512]{1,0:T(8,128)(2,1)}, bf16[576,512]{1,0:T(8,128)(2,1)}, u32[]{:S(2)}, u32[]{:S(2)}) collective-permute-start(bf16[576,512]{1,0:T(8,128)(2,1)} %pad_maximum_fusion.3.refs_1_), channel_id=1, source_target_pairs={{0,96},{32,0},{64,32},{96,64},{1,97},{33,1},{65,33},{97,65},{2,98}... | collective-permute-start | bytes 1769480 | tf_op jit(solution)/shard_map/ppermute | solution.py:290
  41.9 2.5 %collective-permute-start.12 = (bf16[576,512]{1,0:T(8,128)(2,1)}, bf16[576,512]{1,0:T(8,128)(2,1)}, u32[]{:S(2)}, u32[]{:S(2)}) collective-permute-start(bf16[576,512]{1,0:T(8,128)(2,1)} %pad_maximum_fusion.2.refs_0_), channel_id=1, source_target_pairs={{0,96},{32,0},{64,32},{96,64},{1,97},{33,1},{65,33},{97,65},{2,98}... | collective-permute-start | bytes 1769480 | tf_op jit(solution)/shard_map/ppermute | solution.py:290
  44.5 4.5 %all-to-all-start = ((bf16[80,24,576]{2,1,0:T(8,128)(2,1)}), bf16[80,24,576]{2,1,0:T(8,128)(2,1)}, u32[]{:S(2)}, u32[]{:S(2)}) async-start(bf16[80,24,576]{2,1,0:T(8,128)(2,1)} %fusion.2), calls=%async_computation | async-start | bytes 4915200 | tf_op jit(solution)/shard_map/all_to_all | solution.py:303
  48.9 6.3 %prefix_attend.4 = (f32[1152,256]{1,0:T(8,128)}, f32[1152,512]{1,0:T(8,128)}) custom-call(bf16[1152,576]{1,0:T(8,128)(2,1)} %pad_maximum_fusion.q_ref, bf16[576,512]{1,0:T(8,128)(2,1)} %pad_maximum_fusion.2.refs_0_, bf16[576,512]{1,0:T(8,128)(2,1)} %pad_maximum_fusion.3.refs_1_), custom_call_target="tpu_custom_call" | custom-call | flops 99999997952 | bytes 100000000 | tf_op jit(solution)/shard_map/prefix_attend/pallas_call | solution.py:113
  55.3 3.7 %collective-permute-start.10 = (bf16[576,512]{1,0:T(8,128)(2,1)}, bf16[576,512]{1,0:T(8,128)(2,1)S(1)}, u32[]{:S(2)}, u32[]{:S(2)}) collective-permute-start(bf16[576,512]{1,0:T(8,128)(2,1)} %collective-permute-done.9.refs_3_), channel_id=1, source_target_pairs={{0,96},{32,0},{64,32},{96,64},{1,97},{33,1},{65,33},{97,65},{2,98}... | collective-permute-start | bytes 1769480 | tf_op jit(solution)/shard_map/ppermute | solution.py:290
  58.9 11.0 %collective-permute-done.7.refs_0_ = bf16[576,512]{1,0:T(8,128)(2,1)} collective-permute-done((bf16[576,512]{1,0:T(8,128)(2,1)}, bf16[576,512]{1,0:T(8,128)(2,1)}, u32[]{:S(2)}, u32[]{:S(2)}) %collective-permute-start.7) | collective-permute-done | bytes 589856 | tf_op jit(solution)/shard_map/ppermute | solution.py:290
  70.0 11.1 %prefix_attend.5 = (f32[1152,256]{1,0:T(8,128)}, f32[1152,512]{1,0:T(8,128)}) custom-call(bf16[1152,576]{1,0:T(8,128)(2,1)} %pad_maximum_fusion.q_ref, bf16[576,512]{1,0:T(8,128)(2,1)} %collective-permute-done.7.refs_0_, bf16[576,512]{1,0:T(8,128)(2,1)} %collective-permute-done.11.refs_1_, bf16[576,512]{1,0:T(8,128)(2,1)} %collective-permute-done.12.refs_2_, ...), custom_call_target="tpu_custom_call" | custom-call | tf_op jit(solution)/shard_map/prefix_attend/pallas_call | solution.py:113
  82.0 6.1 %tail_attend.1 = bf16[16,5,8,640]{3,2,1,0:T(8,128)(2,1)} custom-call(s32[5]{0:T(128)} %pad_dynamic-slice_fusion.length_ref, bf16[16,5,24,576]{3,2,1,0:T(8,128)(2,1)} %bitcast.12.joined_ref), custom_call_target="tpu_custom_call" | custom-call | flops 99999997952 | bytes 100000000 | tf_op jit(solution)/shard_map/tail_attend/pallas_call | solution.py:148
  88.1 5.8 %all-to-all-start.1 = ((bf16[80,8,640]{2,1,0:T(8,128)(2,1)}), bf16[80,8,640]{2,1,0:T(8,128)(2,1)S(1)}, u32[]{:S(2)}, u32[]{:S(2)}) async-start(bf16[80,8,640]{2,1,0:T(8,128)(2,1)} %bitcast.53), calls=%async_computation.1 | async-start | bytes 1638400 | tf_op jit(solution)/shard_map/all_to_all | solution.py:303
  94.9 4.8 %prefix_attend.7 = bf16[576,640]{1,0:T(8,128)(2,1)} custom-call(bf16[576,576]{1,0:T(8,128)(2,1)} %copy-done.2, bf16[576,512]{1,0:T(8,128)(2,1)} %collective-permute-done.8.refs_0_, bf16[576,512]{1,0:T(8,128)(2,1)} %copy-done.3, f32[1152,256]{1,0:T(8,128)} %get-tuple-element.35.refs_2_, f32[1152,512]{1,0:T(8,128)} %get-tuple-element.36.refs_3_), custom_call_target="tpu_custom_call" | custom-call | tf_op jit(solution)/shard_map/prefix_attend/pallas_call | solution.py:113
  101.3 4.9 %prefix_attend.6.own_ref = bf16[576,640]{1,0:T(8,128)(2,1)} custom-call(bf16[576,576]{1,0:T(8,128)(2,1)} %bitcast.52, bf16[576,512]{1,0:T(8,128)(2,1)} %collective-permute-done.8.refs_0_, bf16[576,512]{1,0:T(8,128)(2,1)} %copy-done.3, f32[1152,256]{1,0:T(8,128)} %get-tuple-element.35.refs_2_, f32[1152,512]{1,0:T(8,128)} %get-tuple-element.36.refs_3_), custom_call_target="tpu_custom_call" | custom-call | tf_op jit(solution)/shard_map/prefix_attend/pallas_call | solution.py:113
  106.2 3.3 %all-to-all-done.1 = bf16[80,8,640]{2,1,0:T(8,128)(2,1)S(1)} async-done(((bf16[80,8,640]{2,1,0:T(8,128)(2,1)}), bf16[80,8,640]{2,1,0:T(8,128)(2,1)S(1)}, u32[]{:S(2)}, u32[]{:S(2)}) %all-to-all-start.1) | async-done | bytes 819232 | tf_op jit(solution)/shard_map/all_to_all | solution.py:303
  111.4 6.9 %finish_first.1 = (bf16[4,72,448]{2,1,0:T(8,128)(2,1)}, bf16[4,72,448]{2,1,0:T(8,128)(2,1)}, bf16[72,1024]{1,0:T(8,128)(2,1)}) custom-call(s32[1]{0:T(128)} %bitcast.core_ref, s32[4]{0:T(128)} %pad_add_fusion.1.order_ref, bf16[576,640]{1,0:T(8,128)(2,1)} %prefix_attend.6.own_ref, bf16[576,640]{1,0:T(8,128)(2,1)} %copy-done.8, ...), custom_call_target="tpu_custom_call" | custom-call | flops 99999997952 | bytes 100000000 | tf_op jit(solution)/shard_map/finish_first/pallas_call | solution.py:245
  118.4 5.5 %finish_second.1 = (bf16[4,72,448]{2,1,0:T(8,128)(2,1)}, bf16[4,72,448]{2,1,0:T(8,128)(2,1)}) custom-call(s32[1]{0:T(128)} %bitcast.core_ref, s32[4]{0:T(128)} %pad_add_fusion.order_ref, bf16[72,1024]{1,0:T(8,128)(2,1)} %get-tuple-element.38.head_ref, bf16[1024,7168]{1,0:T(8,128)(2,1)} %proj_ref.3), custom_call_target="tpu_custom_call" | custom-call | flops 99999997952 | bytes 100000000 | tf_op jit(solution)/shard_map/finish_second/pallas_call | solution.py:258
  126.5 4.6 %collective-permute-start.18 = (bf16[72,448]{1,0:T(8,128)(2,1)S(1)}, bf16[72,448]{1,0:T(8,128)(2,1)S(1)}, u32[]{:S(2)}, u32[]{:S(2)}) collective-permute-start(bf16[72,448]{1,0:T(8,128)(2,1)S(1)} %get-tuple-element.47), channel_id=1, source_target_pairs={{0,12},{2,14},{4,8},{6,10},{8,4},{10,6},{12,0},{14,2},{1,13},{3,15... | collective-permute-start | bytes 193544 | tf_op jit(solution)/shard_map/ppermute | solution.py:312
  131.1 1.8 %collective-permute-start.19 = (bf16[72,448]{1,0:T(8,128)(2,1)S(1)}, bf16[72,448]{1,0:T(8,128)(2,1)S(1)}, u32[]{:S(2)}, u32[]{:S(2)}) collective-permute-start(bf16[72,448]{1,0:T(8,128)(2,1)S(1)} %get-tuple-element.46), channel_id=1, source_target_pairs={{0,14},{2,8},{4,10},{6,12},{8,6},{10,0},{12,2},{14,4},{1,15},{3,9}... | collective-permute-start | bytes 193544 | tf_op jit(solution)/shard_map/ppermute | solution.py:312
  134.8 2.6 %collective-permute-start.21 = (bf16[72,448]{1,0:T(8,128)(2,1)S(1)}, bf16[72,448]{1,0:T(8,128)(2,1)S(1)}, u32[]{:S(2)}, u32[]{:S(2)}) collective-permute-start(bf16[72,448]{1,0:T(8,128)(2,1)S(1)} %get-tuple-element.51), channel_id=1, source_target_pairs={{0,4},{2,6},{4,0},{6,2},{8,12},{10,14},{12,8},{14,10},{1,5},{3,7},... | collective-permute-start | bytes 193544 | tf_op jit(solution)/shard_map/ppermute | solution.py:312
  137.4 2.5 %collective-permute-start.22 = (bf16[72,448]{1,0:T(8,128)(2,1)S(1)}, bf16[72,448]{1,0:T(8,128)(2,1)S(1)}, u32[]{:S(2)}, u32[]{:S(2)}) collective-permute-start(bf16[72,448]{1,0:T(8,128)(2,1)S(1)} %get-tuple-element.50), channel_id=1, source_target_pairs={{0,6},{2,0},{4,2},{6,4},{8,14},{10,8},{12,10},{14,12},{1,7},{3,1},... | collective-permute-start | bytes 193544 | tf_op jit(solution)/shard_map/ppermute | solution.py:312
  (76 shorter events, 29.1 us)
Async XLA Ops:
  1.2 8.5 %collective-permute-start.1 = (bf16[64,576]{0,1:T(8,128)(2,1)S(1)}, bf16[64,576]{0,1:T(8,128)(2,1)}, u32[]{:S(2)}, u32[]{:S(2)}) collective-permute-start(bf16[64,576]{0,1:T(8,128)(2,1)S(1)} %copy.20), channel_id=1, source_target_pairs={{0,2},{2,4},{4,6},{6,0},{1,3},{3,5},{5,7},{7,1},{8,10},{10,12},{12... | collective-permute-start | bytes 221192 | tf_op jit(solution)/shard_map/ppermute | solution.py:290
  2.9 7.8 %collective-permute-start.2 = (bf16[64,576]{0,1:T(8,128)(2,1)S(1)}, bf16[64,576]{0,1:T(8,128)(2,1)}, u32[]{:S(2)}, u32[]{:S(2)}) collective-permute-start(bf16[64,576]{0,1:T(8,128)(2,1)S(1)} %copy.20), channel_id=1, source_target_pairs={{0,6},{2,0},{4,2},{6,4},{1,7},{3,1},{5,3},{7,5},{8,14},{10,8},{12,... | collective-permute-start | bytes 221192 | tf_op jit(solution)/shard_map/ppermute | solution.py:290
  4.5 8.2 %collective-permute-start.3 = (bf16[64,576]{0,1:T(8,128)(2,1)S(1)}, bf16[64,576]{0,1:T(8,128)(2,1)}, u32[]{:S(2)}, u32[]{:S(2)}) collective-permute-start(bf16[64,576]{0,1:T(8,128)(2,1)S(1)} %copy.20), channel_id=1, source_target_pairs={{0,4},{2,6},{4,0},{6,2},{1,5},{3,7},{5,1},{7,3},{8,12},{10,14},{12... | collective-permute-start | bytes 221192 | tf_op jit(solution)/shard_map/ppermute | solution.py:290
  9.5 27.5 %collective-permute-start = (bf16[576,576]{1,0:T(8,128)(2,1)S(1)}, bf16[576,576]{1,0:T(8,128)(2,1)S(1)}, u32[]{:S(2)}, u32[]{:S(2)}) collective-permute-start(bf16[576,576]{1,0:T(8,128)(2,1)S(1)} %bitcast.50), channel_id=1, source_target_pairs={{0,1},{1,0},{2,3},{3,2},{4,5},{5,4},{6,7},{7,6},{8,9},{9,8},{10,11... | collective-permute-start | bytes 1990664 | tf_op jit(solution)/shard_map/ppermute | solution.py:293
  14.0 21.2 %collective-permute-start.5 = (bf16[576,256]{1,0:T(8,128)(2,1)S(1)}, bf16[576,256]{1,0:T(8,128)(2,1)}, u32[]{:S(2)}, u32[]{:S(2)}) collective-permute-start(bf16[576,256]{1,0:T(8,128)(2,1)S(1)} %maximum_bitcast_fusion), channel_id=1, source_target_pairs={{0,24},{16,0},{8,16},{24,8},{1,25},{17,1},{9,17},{25,9},{2,26},{18... | collective-permute-start | bytes 884744 | tf_op jit(solution)/shard_map/ppermute | solution.py:300
  18.1 17.1 %collective-permute-start.6 = (bf16[576,256]{1,0:T(8,128)(2,1)S(1)}, bf16[576,256]{1,0:T(8,128)(2,1)}, u32[]{:S(2)}, u32[]{:S(2)}) collective-permute-start(bf16[576,256]{1,0:T(8,128)(2,1)S(1)} %maximum_bitcast_fusion), channel_id=1, source_target_pairs={{0,8},{16,24},{8,0},{24,16},{1,9},{17,25},{9,1},{25,17},{2,10},{18... | collective-permute-start | bytes 884744 | tf_op jit(solution)/shard_map/ppermute | solution.py:300
  18.1 15.2 %collective-permute-start.4 = (bf16[576,256]{1,0:T(8,128)(2,1)S(1)}, bf16[576,256]{1,0:T(8,128)(2,1)}, u32[]{:S(2)}, u32[]{:S(2)}) collective-permute-start(bf16[576,256]{1,0:T(8,128)(2,1)S(1)} %maximum_bitcast_fusion), channel_id=1, source_target_pairs={{0,16},{16,8},{8,24},{24,0},{1,17},{17,9},{9,25},{25,1},{2,18},{18... | collective-permute-start | bytes 884744 | tf_op jit(solution)/shard_map/ppermute | solution.py:300
  38.4 16.8 %collective-permute-start.9 = (bf16[576,512]{1,0:T(8,128)(2,1)}, bf16[576,512]{1,0:T(8,128)(2,1)}, u32[]{:S(2)}, u32[]{:S(2)}) collective-permute-start(bf16[576,512]{1,0:T(8,128)(2,1)} %pad_maximum_fusion.3.refs_1_), channel_id=1, source_target_pairs={{0,96},{32,0},{64,32},{96,64},{1,97},{33,1},{65,33},{97,65},{2,98}... | collective-permute-start | bytes 1769480 | tf_op jit(solution)/shard_map/ppermute | solution.py:290
  41.2 28.8 %collective-permute-start.11 = (bf16[576,512]{1,0:T(8,128)(2,1)}, bf16[576,512]{1,0:T(8,128)(2,1)}, u32[]{:S(2)}, u32[]{:S(2)}) collective-permute-start(bf16[576,512]{1,0:T(8,128)(2,1)} %pad_maximum_fusion.3.refs_1_), channel_id=1, source_target_pairs={{0,32},{32,64},{64,96},{96,0},{1,33},{33,65},{65,97},{97,1},{2,34}... | collective-permute-start | bytes 1769480 | tf_op jit(solution)/shard_map/ppermute | solution.py:290
  41.2 28.8 %collective-permute-start.7 = (bf16[576,512]{1,0:T(8,128)(2,1)}, bf16[576,512]{1,0:T(8,128)(2,1)}, u32[]{:S(2)}, u32[]{:S(2)}) collective-permute-start(bf16[576,512]{1,0:T(8,128)(2,1)} %pad_maximum_fusion.2.refs_0_), channel_id=1, source_target_pairs={{0,32},{32,64},{64,96},{96,0},{1,33},{33,65},{65,97},{97,1},{2,34}... | collective-permute-start | bytes 1769480 | tf_op jit(solution)/shard_map/ppermute | solution.py:290
  41.9 28.0 %collective-permute-start.12 = (bf16[576,512]{1,0:T(8,128)(2,1)}, bf16[576,512]{1,0:T(8,128)(2,1)}, u32[]{:S(2)}, u32[]{:S(2)}) collective-permute-start(bf16[576,512]{1,0:T(8,128)(2,1)} %pad_maximum_fusion.2.refs_0_), channel_id=1, source_target_pairs={{0,96},{32,0},{64,32},{96,64},{1,97},{33,1},{65,33},{97,65},{2,98}... | collective-permute-start | bytes 1769480 | tf_op jit(solution)/shard_map/ppermute | solution.py:290
  44.5 37.6 %all-to-all-start = ((bf16[80,24,576]{2,1,0:T(8,128)(2,1)}), bf16[80,24,576]{2,1,0:T(8,128)(2,1)}, u32[]{:S(2)}, u32[]{:S(2)}) async-start(bf16[80,24,576]{2,1,0:T(8,128)(2,1)} %fusion.2), calls=%async_computation | async-start | bytes 4915200 | tf_op jit(solution)/shard_map/all_to_all | solution.py:303
  55.3 38.7 %collective-permute-start.10 = (bf16[576,512]{1,0:T(8,128)(2,1)}, bf16[576,512]{1,0:T(8,128)(2,1)S(1)}, u32[]{:S(2)}, u32[]{:S(2)}) collective-permute-start(bf16[576,512]{1,0:T(8,128)(2,1)} %collective-permute-done.9.refs_3_), channel_id=1, source_target_pairs={{0,96},{32,0},{64,32},{96,64},{1,97},{33,1},{65,33},{97,65},{2,98}... | collective-permute-start | bytes 1769480 | tf_op jit(solution)/shard_map/ppermute | solution.py:290
  70.0 24.0 %collective-permute-start.8 = (bf16[576,512]{1,0:T(8,128)(2,1)}, bf16[576,512]{1,0:T(8,128)(2,1)}, u32[]{:S(2)}, u32[]{:S(2)}) collective-permute-start(bf16[576,512]{1,0:T(8,128)(2,1)} %collective-permute-done.7.refs_0_), channel_id=1, source_target_pairs={{0,32},{32,64},{64,96},{96,0},{1,33},{33,65},{65,97},{97,1},{2,34}... | collective-permute-start | bytes 1769480 | tf_op jit(solution)/shard_map/ppermute | solution.py:290
  88.1 21.4 %all-to-all-start.1 = ((bf16[80,8,640]{2,1,0:T(8,128)(2,1)}), bf16[80,8,640]{2,1,0:T(8,128)(2,1)S(1)}, u32[]{:S(2)}, u32[]{:S(2)}) async-start(bf16[80,8,640]{2,1,0:T(8,128)(2,1)} %bitcast.53), calls=%async_computation.1 | async-start | bytes 1638400 | tf_op jit(solution)/shard_map/all_to_all | solution.py:303
  99.7 10.9 %collective-permute-start.13 = (bf16[576,640]{1,0:T(8,128)(2,1)}, bf16[576,640]{1,0:T(8,128)(2,1)S(1)}, u32[]{:S(2)}, u32[]{:S(2)}) collective-permute-start(bf16[576,640]{1,0:T(8,128)(2,1)} %prefix_attend.7), channel_id=1, source_target_pairs={{0,1},{1,0},{2,3},{3,2},{4,5},{5,4},{6,7},{7,6},{8,9},{9,8},{10,11... | collective-permute-start | bytes 2211848 | tf_op jit(solution)/shard_map/ppermute | solution.py:293
  118.3 6.2 %collective-permute-start.15 = (bf16[4,72,448]{2,1,0:T(8,128)(2,1)}, bf16[4,72,448]{2,1,0:T(8,128)(2,1)S(1)}, u32[]{:S(2)}, u32[]{:S(2)}) collective-permute-start(bf16[4,72,448]{2,1,0:T(8,128)(2,1)} %get-tuple-element.42), channel_id=1, source_target_pairs={{0,1},{1,0},{2,3},{3,2},{4,5},{5,4},{6,7},{7,6},{8,9},{9,8},{10,11... | collective-permute-start | bytes 774152 | tf_op jit(solution)/shard_map/ppermute | solution.py:293
  123.9 8.9 %collective-permute-start.14 = (bf16[4,72,448]{2,1,0:T(8,128)(2,1)}, bf16[4,72,448]{2,1,0:T(8,128)(2,1)S(1)}, u32[]{:S(2)}, u32[]{:S(2)}) collective-permute-start(bf16[4,72,448]{2,1,0:T(8,128)(2,1)} %get-tuple-element.40), channel_id=1, source_target_pairs={{0,1},{1,0},{2,3},{3,2},{4,5},{5,4},{6,7},{7,6},{8,9},{9,8},{10,11... | collective-permute-start | bytes 774152 | tf_op jit(solution)/shard_map/ppermute | solution.py:293
  124.6 10.2 %collective-permute-start.16 = (bf16[72,448]{1,0:T(8,128)(2,1)S(1)}, bf16[72,448]{1,0:T(8,128)(2,1)S(1)}, u32[]{:S(2)}, u32[]{:S(2)}) collective-permute-start(bf16[72,448]{1,0:T(8,128)(2,1)S(1)} %get-tuple-element.45), channel_id=1, source_target_pairs={{0,8},{2,10},{4,12},{6,14},{8,0},{10,2},{12,4},{14,6},{1,9},{3,11}... | collective-permute-start | bytes 193544 | tf_op jit(solution)/shard_map/ppermute | solution.py:312
  125.2 12.2 %collective-permute-start.17 = (bf16[72,448]{1,0:T(8,128)(2,1)S(1)}, bf16[72,448]{1,0:T(8,128)(2,1)S(1)}, u32[]{:S(2)}, u32[]{:S(2)}) collective-permute-start(bf16[72,448]{1,0:T(8,128)(2,1)S(1)} %get-tuple-element.48), channel_id=1, source_target_pairs={{0,10},{2,12},{4,14},{6,8},{8,2},{10,4},{12,6},{14,0},{1,11},{3,13... | collective-permute-start | bytes 193544 | tf_op jit(solution)/shard_map/ppermute | solution.py:312
  126.5 13.4 %collective-permute-start.18 = (bf16[72,448]{1,0:T(8,128)(2,1)S(1)}, bf16[72,448]{1,0:T(8,128)(2,1)S(1)}, u32[]{:S(2)}, u32[]{:S(2)}) collective-permute-start(bf16[72,448]{1,0:T(8,128)(2,1)S(1)} %get-tuple-element.47), channel_id=1, source_target_pairs={{0,12},{2,14},{4,8},{6,10},{8,4},{10,6},{12,0},{14,2},{1,13},{3,15... | collective-permute-start | bytes 193544 | tf_op jit(solution)/shard_map/ppermute | solution.py:312
  131.1 8.8 %collective-permute-start.19 = (bf16[72,448]{1,0:T(8,128)(2,1)S(1)}, bf16[72,448]{1,0:T(8,128)(2,1)S(1)}, u32[]{:S(2)}, u32[]{:S(2)}) collective-permute-start(bf16[72,448]{1,0:T(8,128)(2,1)S(1)} %get-tuple-element.46), channel_id=1, source_target_pairs={{0,14},{2,8},{4,10},{6,12},{8,6},{10,0},{12,2},{14,4},{1,15},{3,9}... | collective-permute-start | bytes 193544 | tf_op jit(solution)/shard_map/ppermute | solution.py:312
  133.9 6.0 %collective-permute-start.20 = (bf16[72,448]{1,0:T(8,128)(2,1)S(1)}, bf16[72,448]{1,0:T(8,128)(2,1)S(1)}, u32[]{:S(2)}, u32[]{:S(2)}) collective-permute-start(bf16[72,448]{1,0:T(8,128)(2,1)S(1)} %get-tuple-element.49), channel_id=1, source_target_pairs={{0,2},{2,4},{4,6},{6,0},{8,10},{10,12},{12,14},{14,8},{1,3},{3,5},... | collective-permute-start | bytes 193544 | tf_op jit(solution)/shard_map/ppermute | solution.py:312
  134.8 5.9 %collective-permute-start.21 = (bf16[72,448]{1,0:T(8,128)(2,1)S(1)}, bf16[72,448]{1,0:T(8,128)(2,1)S(1)}, u32[]{:S(2)}, u32[]{:S(2)}) collective-permute-start(bf16[72,448]{1,0:T(8,128)(2,1)S(1)} %get-tuple-element.51), channel_id=1, source_target_pairs={{0,4},{2,6},{4,0},{6,2},{8,12},{10,14},{12,8},{14,10},{1,5},{3,7},... | collective-permute-start | bytes 193544 | tf_op jit(solution)/shard_map/ppermute | solution.py:312
  (11 other events, 89.5 us)

commit v4 on v3

--- a/solution.py
+++ b/solution.py
@@ -11,7 +11,7 @@
 ROW_BLOCK = 288
 KEY_BLOCK = 512
 VMEM = 58 * 1024 * 1024
-COST = pl.CostEstimate(flops=10**11, bytes_accessed=10**8, transcendentals=0)
+COST = None
 
 
 def pack(acc, weight_sum, highest, exponent_scale):
@@ -81,7 +81,7 @@
         out_acc_ref[...] = acc
 
 
-def attend(q, keys, state, last, width, exponent_scale, second=False, cost=COST):
+def attend(q, keys, state, last, width, exponent_scale, second=False):
     rows, features = q.shape
     first = state is None
     row_map = lambda i: (i, 0)
@@ -117,7 +117,7 @@
         out_specs=out_specs,
         out_shape=out_shape,
         compiler_params=pltpu.CompilerParams(vmem_limit_bytes=VMEM),
-        cost_estimate=cost,
+        cost_estimate=COST,
         name="prefix_attend",
     )(*args)
 
@@ -160,7 +160,10 @@
     )(length, joined)
 
 
-def project(core, order_ref, head, proj_ref, keep_ref, give_ref, block_refs, sems, between):
+def finish_kernel(
+    width, core_ref, order_ref, own_ref, received_ref, tail_ref, up_ref, proj_ref,
+    keep_ref, give_ref, head_ref, context_ref, block_refs, sems,
+):
     columns = block_refs.shape[2]
     copies = [
         pltpu.make_async_copy(
@@ -172,9 +175,29 @@
     ]
     for copy in copies:
         copy.start()
-    head = between() if head is None else head
-    half = columns // 2
-    early = core == 0
+    heads, _, value_width = up_ref.shape
+    req_rows = head_ref.shape[0]
+    refs = (own_ref, received_ref, tail_ref)
+    levels = [
+        jnp.sum(ref[:, width:].astype(jnp.float32), axis=1, keepdims=True) for ref in refs
+    ]
+    top = functools.reduce(jnp.maximum, levels)
+    shares = [jnp.exp2(level - top) for level in levels]
+    total = shares[0] + shares[1] + shares[2]
+    context = sum(
+        ref[:, :width].astype(jnp.float32) * (share / total)
+        for ref, share in zip(refs, shares)
+    )
+    context_ref[...] = context.reshape(req_rows, heads, width)
+    for h in range(heads):
+        head_ref[:, h * value_width : (h + 1) * value_width] = jnp.dot(
+            context_ref[:, h, :].astype(jnp.bfloat16),
+            up_ref[h],
+            preferred_element_type=jnp.float32,
+        ).astype(jnp.bfloat16)
+    head = head_ref[...]
+    half = keep_ref.shape[2]
+    early = core_ref[0] == 0
     for i, copy in enumerate(copies):
         copy.wait()
         mixed = jnp.dot(head, block_refs[i], preferred_element_type=jnp.float32)
@@ -183,87 +206,28 @@
         give_ref[i] = jnp.where(early, mixed[:, half:], mixed[:, :half])
 
 
-def first_kernel(
-    width, core_ref, order_ref, own_ref, received_ref, tail_ref, up_ref, proj_ref,
-    keep_ref, give_ref, head_ref, context_ref, block_refs, sems,
-):
-    heads, _, value_width = up_ref.shape
-    req_rows = head_ref.shape[0]
-
-    def make_head():
-        refs = (own_ref, received_ref, tail_ref)
-        levels = [
-            jnp.sum(ref[:, width:].astype(jnp.float32), axis=1, keepdims=True) for ref in refs
-        ]
-        top = functools.reduce(jnp.maximum, levels)
-        shares = [jnp.exp2(level - top) for level in levels]
-        total = shares[0] + shares[1] + shares[2]
-        context = sum(
-            ref[:, :width].astype(jnp.float32) * (share / total)
-            for ref, share in zip(refs, shares)
-        )
-        context_ref[...] = context.reshape(req_rows, heads, width)
-        for h in range(heads):
-            head_ref[:, h * value_width : (h + 1) * value_width] = jnp.dot(
-                context_ref[:, h, :].astype(jnp.bfloat16),
-                up_ref[h],
-                preferred_element_type=jnp.float32,
-            ).astype(jnp.bfloat16)
-        return head_ref[...]
-
-    project(
-        core_ref[0], order_ref, None, proj_ref, keep_ref, give_ref, block_refs, sems, make_head
-    )
-
-
-def second_kernel(
-    core_ref, order_ref, head_ref, proj_ref, keep_ref, give_ref, block_refs, sems
-):
-    project(
-        core_ref[0], order_ref, head_ref[...], proj_ref, keep_ref, give_ref, block_refs, sems, None
-    )
-
-
-def finish(args, head, out_proj, value_up, core, order, chips):
+def finish(own, received, tail, value_up, out_proj, core, order):
     heads, width, value_width = value_up.shape
-    depth, columns = out_proj.shape
-    block = columns // chips
-    count = order.shape[0]
+    req_rows = own.shape[0] // heads
     vmem = pl.BlockSpec(memory_space=pltpu.VMEM)
     smem = pl.BlockSpec(memory_space=pltpu.SMEM)
-    req_rows = (args[0].shape[0] // heads) if head is None else head.shape[0]
-    half = jax.ShapeDtypeStruct((count, req_rows, block // 2), jnp.bfloat16)
-    scratch = [
-        pltpu.VMEM((count, depth, block), jnp.bfloat16),
-        pltpu.SemaphoreType.DMA((count,)),
-    ]
-    common = dict(
-        compiler_params=pltpu.CompilerParams(vmem_limit_bytes=VMEM), cost_estimate=COST
-    )
-    anywhere = pl.BlockSpec(memory_space=pl.ANY)
-    if head is None:
-        return pl.pallas_call(
-            functools.partial(first_kernel, width),
-            in_specs=[smem, smem, vmem, vmem, vmem, vmem, anywhere],
-            out_specs=(vmem, vmem, vmem),
-            out_shape=(
-                half,
-                half,
-                jax.ShapeDtypeStruct((req_rows, heads * value_width), jnp.bfloat16),
-            ),
-            scratch_shapes=[pltpu.VMEM((req_rows, heads, width), jnp.float32)] + scratch,
-            name="finish_first",
-            **common,
-        )(core, order, *args, value_up, out_proj)
+    chips = order.shape[0]
+    half = jax.ShapeDtypeStruct((chips, req_rows, out_proj.shape[1] // (2 * chips)), jnp.bfloat16)
     return pl.pallas_call(
-        second_kernel,
-        in_specs=[smem, smem, vmem, anywhere],
+        functools.partial(finish_kernel, width),
+        in_specs=[smem, smem, vmem, vmem, vmem, vmem, pl.BlockSpec(memory_space=pl.ANY)],
         out_specs=(vmem, vmem),
         out_shape=(half, half),
-        scratch_shapes=scratch,
-        name="finish_second",
-        **common,
-    )(core, order, head, out_proj)
+        scratch_shapes=[
+            pltpu.VMEM((req_rows, heads * value_width), jnp.bfloat16),
+            pltpu.VMEM((req_rows, heads, width), jnp.float32),
+            pltpu.VMEM((chips, out_proj.shape[0], out_proj.shape[1] // chips), jnp.bfloat16),
+            pltpu.SemaphoreType.DMA((chips,)),
+        ],
+        compiler_params=pltpu.CompilerParams(vmem_limit_bytes=VMEM),
+        cost_estimate=COST,
+        name="finish",
+    )(core, order, own, received, tail, value_up, out_proj)
 
 
 def on_device(
@@ -347,43 +311,41 @@
     )
 
     go = functools.partial(attend, width=latent_width, exponent_scale=exponent_scale)
-    far = [ring(right[0], "x", 1), ring(left[1], "x", -1)]
     state = go(both, held, None, False)
-
-    state = go(both, right + left, state, False, cost=None)
+    near = [right[0], left[1]]
+    near, state = lax.optimization_barrier((near, state))
+    far = [ring(near[0], "x", 1), ring(near[1], "x", -1)]
+
+    state = go(both, near, state, False)
     joined, state = lax.optimization_barrier((joined, state))
     tail_part = attend_tails(joined, span, length, latent_width, exponent_scale)
     tail_part, state = lax.optimization_barrier((tail_part, state))
+    late = [right[1], left[0]] + far
     tail_part = exchange(tail_part.reshape(devices * slots, heads_here, latent_width + 128))
     tail_part = tail_part[:req_rows].reshape(req_rows * heads_here, latent_width + 128)
 
-    packed_other = go(query_other, far, state, True, second=True, cost=None)
+    packed_other = go(query_other, late, state, True, second=True)
     received = other_core(packed_other)
-    packed_own = go(query_rows, far, state, True, cost=None)
-
-    moves = [(1, by) for by in range(y_size)] + [(0, by) for by in (1, 2, 3, 0)]
+    packed_own = go(query_rows, late, state, True)
+
+    moves = [(by_y, by_high) for by_y in (1, 2, 3, 0) for by_high in range(high_size)]
     order = jnp.stack(
         [
             ((z_high + by_high) % high_size) * y_size + (y_at + by_y) % y_size
-            for by_high, by_y in moves
+            for by_y, by_high in moves
         ]
     ).astype(jnp.int32)
-    run = functools.partial(
-        finish, out_proj=out_proj, value_up=value_up, core=core_at, chips=chips
-    )
-    keep, give, head = run((packed_own, received, tail_part), None, order=order[:y_size])
-    first = (keep, other_core(give))
-    keep, give = run((), head, order=order[y_size:])
-    second = (keep, other_core(give))
-    paired = [
-        (mine[i].astype(jnp.float32) + theirs[i].astype(jnp.float32))
-        for mine, theirs in (first, second)
-        for i in range(y_size)
-    ]
-    total = paired[-1]
-    for (by_high, by_y), value in zip(moves[:-1], paired[:-1]):
-        total += chip_shift(value.astype(jnp.bfloat16), by_high, by_y).astype(jnp.float32)
-    return total.astype(jnp.bfloat16)
+    keep, give = finish(packed_own, received, tail_part, value_up, out_proj, core_at, order)
+    given = other_core(give)
+    sums = [
+        (keep[at : at + high_size].astype(jnp.float32) + given[at : at + high_size].astype(jnp.float32))
+        for at in range(0, chips, high_size)
+    ]
+    total = sums[-1]
+    for by_y, value in zip((1, 2, 3), sums[:-1]):
+        total += ring(value.astype(jnp.bfloat16), "y", by_y).astype(jnp.float32)
+    passed = ring(total[1].astype(jnp.bfloat16), "z_hi", 1)
+    return (total[0] + passed.astype(jnp.float32)).astype(jnp.bfloat16)
 
 
 def solution(mesh):

time: 145 us -> 134 us (0.924)
  starting transfers between devices: 46.2 us -> 40.8 us
  other arithmetic: 13.5 us -> 10.3 us
  Pallas kernels: 45.7 us -> 43 us
    ppermute x7 -> x0, starting transfers between devices: 14.3 us -> none  [chip_shift(): return lax.ppermute(value, ('z_hi', 'y'), pairs)]
    ppermute x9 -> x13, starting transfers between devices: 15.1 us -> 23.6 us  [ring(): lax.ppermute(value, axis, [(i, (i + by) % size) for i in range(size)])]
    ppermute x9 -> x13, waiting for transfers between devices: 14 us -> 19.8 us  [ring(): lax.ppermute(value, axis, [(i, (i + by) % size) for i in range(size)])]
    pallas_call x2 -> x1, Pallas kernels: 12.4 us -> 9.15 us  [finish(): pl.pallas_call(functools.partial(finish_kernel, width), in_specs=[smem, s...]
    all_to_all x2, waiting for transfers between devices: 4.21 us -> 1.08 us  [exchange(): return lax.all_to_all(value, ('z_hi', 'y', 'core'), 0, 0, tiled=True)]
    ppermute x3, waiting for transfers between devices: 11.6 us -> 9.21 us  [z_ring(): return lax.ppermute(value, ('z_lo', 'z_hi'), pairs)]
    ppermute x4 -> x3, waiting for transfers between devices: 0.01 us -> 2.11 us  [other_core(): return lax.ppermute(value, 'core', [(0, 1), (1, 0)])]
    ppermute x7 -> x0, waiting for transfers between devices: 1.98 us -> none  [chip_shift(): return lax.ppermute(value, ('z_hi', 'y'), pairs)]
  transfers between devices with their start and end apart: 25 -> 21, of which waited for: 8 -> 12; matrix products, arithmetic and copies ran while one was open for 9% -> 7% of each run, Pallas kernels for 27% -> 25%
where the time goes in v4:
time: 134 us; the launch traced here: 133 us
  Pallas kernels  43 us (32%)
  starting transfers between devices  40.8 us (30%)
  waiting for transfers between devices  32.3 us (24%)
  other arithmetic  10.3 us (8%)
  local copies, waits for them, and re-layouts  6.19 us (5%)
    pallas_call x4, Pallas kernels, attend(): pl.pallas_call(functools.partial(attend_kernel, first, last, width, expon...  27.7 us
    ppermute x13, starting transfers between devices, ring(): lax.ppermute(value, axis, [(i, (i + by) % size) for i in range(size)])  23.6 us
    ppermute x13, waiting for transfers between devices, ring(): lax.ppermute(value, axis, [(i, (i + by) % size) for i in range(size)])  19.8 us
    all_to_all x2, starting transfers between devices, exchange(): return lax.all_to_all(value, ('z_hi', 'y', 'core'), 0, 0, tiled=True)  10.5 us
    ppermute x3, waiting for transfers between devices, z_ring(): return lax.ppermute(value, ('z_lo', 'z_hi'), pairs)  9.21 us
    pallas_call x1, Pallas kernels, finish(): pl.pallas_call(functools.partial(finish_kernel, width), in_specs=[smem, s...  9.15 us
    pallas_call x1, Pallas kernels, attend_tails(): pl.pallas_call(functools.partial(tail_kernel, span, width, exponent_scale...  6.11 us
    ppermute x3, starting transfers between devices, z_ring(): return lax.ppermute(value, ('z_lo', 'z_hi'), pairs)  5.97 us
  transfers between devices with their start and end apart: 21, of which 12 were waited for; matrix products, arithmetic and copies ran while one was open for 7% of the time, Pallas kernels for 25%

profile of v4, /device:TPU:0, one launch (start us, length us, event | category | flops | bytes accessed | tf_op | source)
XLA Modules:
  0.0 133.0 jit_solution(9509979887670778889)
XLA Ops:
  4.5 2.1 %collective-permute-start.3 = (bf16[64,576]{0,1:T(8,128)(2,1)S(1)}, bf16[64,576]{0,1:T(8,128)(2,1)}, u32[]{:S(2)}, u32[]{:S(2)}) collective-permute-start(bf16[64,576]{0,1:T(8,128)(2,1)S(1)} %copy.20), channel_id=1, source_target_pairs={{0,4},{2,6},{4,0},{6,2},{1,5},{3,7},{5,1},{7,3},{8,12},{10,14},{12... | collective-permute-start | bytes 221192 | tf_op jit(solution)/shard_map/ppermute | solution.py:254
  10.7 1.9 %collective-permute-done.3 = bf16[64,576]{0,1:T(8,128)(2,1)} collective-permute-done((bf16[64,576]{0,1:T(8,128)(2,1)S(1)}, bf16[64,576]{0,1:T(8,128)(2,1)}, u32[]{:S(2)}, u32[]{:S(2)}) %collective-permute-start.3) | collective-permute-done | bytes 73760 | tf_op jit(solution)/shard_map/ppermute | solution.py:254
  13.9 2.0 %collective-permute-start.4 = (bf16[576,256]{1,0:T(8,128)(2,1)S(1)}, bf16[576,256]{1,0:T(8,128)(2,1)S(1)}, u32[]{:S(2)}, u32[]{:S(2)}) collective-permute-start(bf16[576,256]{1,0:T(8,128)(2,1)S(1)} %maximum_bitcast_fusion), channel_id=1, source_target_pairs={{0,16},{16,8},{8,24},{24,0},{1,17},{17,9},{9,25},{25,1},{2,18},{18... | collective-permute-start | bytes 884744 | tf_op jit(solution)/shard_map/ppermute | solution.py:264
  15.9 2.2 %collective-permute-start.5 = (bf16[576,256]{1,0:T(8,128)(2,1)S(1)}, bf16[576,256]{1,0:T(8,128)(2,1)S(1)}, u32[]{:S(2)}, u32[]{:S(2)}) collective-permute-start(bf16[576,256]{1,0:T(8,128)(2,1)S(1)} %maximum_bitcast_fusion), channel_id=1, source_target_pairs={{0,24},{16,0},{8,16},{24,8},{1,25},{17,1},{9,17},{25,9},{2,26},{18... | collective-permute-start | bytes 884744 | tf_op jit(solution)/shard_map/ppermute | solution.py:264
  21.5 3.5 %collective-permute-done.4 = bf16[576,256]{1,0:T(8,128)(2,1)S(1)} collective-permute-done((bf16[576,256]{1,0:T(8,128)(2,1)S(1)}, bf16[576,256]{1,0:T(8,128)(2,1)S(1)}, u32[]{:S(2)}, u32[]{:S(2)}) %collective-permute-start.4) | collective-permute-done | bytes 294944 | tf_op jit(solution)/shard_map/ppermute | solution.py:264
  25.9 3.9 %collective-permute-done.5 = bf16[576,256]{1,0:T(8,128)(2,1)S(1)} collective-permute-done((bf16[576,256]{1,0:T(8,128)(2,1)S(1)}, bf16[576,256]{1,0:T(8,128)(2,1)S(1)}, u32[]{:S(2)}, u32[]{:S(2)}) %collective-permute-start.5) | collective-permute-done | bytes 294944 | tf_op jit(solution)/shard_map/ppermute | solution.py:264
  33.8 4.5 %all-to-all-start = ((bf16[80,24,576]{2,1,0:T(8,128)(2,1)}), bf16[80,24,576]{2,1,0:T(8,128)(2,1)}, u32[]{:S(2)}, u32[]{:S(2)}) async-start(bf16[80,24,576]{2,1,0:T(8,128)(2,1)} %fusion.2), calls=%async_computation | async-start | bytes 4915200 | tf_op jit(solution)/shard_map/all_to_all | solution.py:267
  38.3 2.8 %collective-permute-start.10 = (bf16[576,512]{1,0:T(8,128)(2,1)}, bf16[576,512]{1,0:T(8,128)(2,1)}, u32[]{:S(2)}, u32[]{:S(2)}) collective-permute-start(bf16[576,512]{1,0:T(8,128)(2,1)} %pad_maximum_fusion.3.refs_1_), channel_id=1, source_target_pairs={{0,96},{32,0},{64,32},{96,64},{1,97},{33,1},{65,33},{97,65},{2,98}... | collective-permute-start | bytes 1769480 | tf_op jit(solution)/shard_map/ppermute | solution.py:254
  41.9 2.5 %collective-permute-start.8 = (bf16[576,512]{1,0:T(8,128)(2,1)}, bf16[576,512]{1,0:T(8,128)(2,1)}, u32[]{:S(2)}, u32[]{:S(2)}) collective-permute-start(bf16[576,512]{1,0:T(8,128)(2,1)} %pad_maximum_fusion.2.refs_0_), channel_id=1, source_target_pairs={{0,96},{32,0},{64,32},{96,64},{1,97},{33,1},{65,33},{97,65},{2,98}... | collective-permute-start | bytes 1769480 | tf_op jit(solution)/shard_map/ppermute | solution.py:254
  44.4 6.3 %prefix_attend.4 = (f32[1152,256]{1,0:T(8,128)}, f32[1152,512]{1,0:T(8,128)}) custom-call(bf16[1152,576]{1,0:T(8,128)(2,1)} %pad_maximum_fusion.q_ref, bf16[576,512]{1,0:T(8,128)(2,1)} %pad_maximum_fusion.2.refs_0_, bf16[576,512]{1,0:T(8,128)(2,1)} %pad_maximum_fusion.3.refs_1_), custom_call_target="tpu_custom_call" | custom-call | tf_op jit(solution)/shard_map/prefix_attend/pallas_call | solution.py:113
  50.7 4.4 %collective-permute-done.10.refs_1_ = bf16[576,512]{1,0:T(8,128)(2,1)} collective-permute-done((bf16[576,512]{1,0:T(8,128)(2,1)}, bf16[576,512]{1,0:T(8,128)(2,1)}, u32[]{:S(2)}, u32[]{:S(2)}) %collective-permute-start.10) | collective-permute-done | bytes 589856 | tf_op jit(solution)/shard_map/ppermute | solution.py:254
  55.1 3.7 %collective-permute-done.9.refs_0_ = bf16[576,512]{1,0:T(8,128)(2,1)} collective-permute-done((bf16[576,512]{1,0:T(8,128)(2,1)}, bf16[576,512]{1,0:T(8,128)(2,1)}, u32[]{:S(2)}, u32[]{:S(2)}) %collective-permute-start.9) | collective-permute-done | bytes 589856 | tf_op jit(solution)/shard_map/ppermute | solution.py:254
  58.9 3.2 %collective-permute-start.12 = (bf16[576,512]{1,0:T(8,128)(2,1)}, bf16[576,512]{1,0:T(8,128)(2,1)}, u32[]{:S(2)}, u32[]{:S(2)}) collective-permute-start(bf16[576,512]{1,0:T(8,128)(2,1)} %collective-permute-done.10.refs_1_), channel_id=1, source_target_pairs={{0,96},{32,0},{64,32},{96,64},{1,97},{33,1},{65,33},{97,65},{2,98}... | collective-permute-start | bytes 1769480 | tf_op jit(solution)/shard_map/ppermute | solution.py:254
  62.7 7.6 %prefix_attend.5 = (f32[1152,256]{1,0:T(8,128)}, f32[1152,512]{1,0:T(8,128)}) custom-call(bf16[1152,576]{1,0:T(8,128)(2,1)} %pad_maximum_fusion.q_ref, bf16[576,512]{1,0:T(8,128)(2,1)} %collective-permute-done.9.refs_0_, bf16[576,512]{1,0:T(8,128)(2,1)} %collective-permute-done.10.refs_1_, f32[1152,256]{1,0:T(8,128)} %get-tuple-element.33.refs_2_, ...), custom_call_target="tpu_custom_call" | custom-call | tf_op jit(solution)/shard_map/prefix_attend/pallas_call | solution.py:113
  71.4 6.1 %tail_attend.1 = bf16[16,5,8,640]{3,2,1,0:T(8,128)(2,1)} custom-call(s32[5]{0:T(128)} %pad_dynamic-slice_fusion.length_ref, bf16[16,5,24,576]{3,2,1,0:T(8,128)(2,1)} %bitcast.12.joined_ref), custom_call_target="tpu_custom_call" | custom-call | tf_op jit(solution)/shard_map/tail_attend/pallas_call | solution.py:148
  77.5 6.1 %all-to-all-start.1 = ((bf16[80,8,640]{2,1,0:T(8,128)(2,1)}), bf16[80,8,640]{2,1,0:T(8,128)(2,1)S(1)}, u32[]{:S(2)}, u32[]{:S(2)}) async-start(bf16[80,8,640]{2,1,0:T(8,128)(2,1)} %bitcast.31), calls=%async_computation.1 | async-start | bytes 1638400 | tf_op jit(solution)/shard_map/all_to_all | solution.py:267
  84.4 6.9 %prefix_attend.7 = bf16[576,640]{1,0:T(8,128)(2,1)} custom-call(bf16[576,576]{1,0:T(8,128)(2,1)} %copy-done.2, bf16[576,512]{1,0:T(8,128)(2,1)} %copy-done.3, bf16[576,512]{1,0:T(8,128)(2,1)} %collective-permute-done.8.refs_1_, bf16[576,512]{1,0:T(8,128)(2,1)} %collective-permute-done.11.refs_2_, bf16[576,512]{1,0:T(8,128)(2,1)} %collective-permute-done.12.refs_3_, ...), custom_call_target="tpu_custom_call" | custom-call | tf_op jit(solution)/shard_map/prefix_attend/pallas_call | solution.py:113
  92.3 6.9 %prefix_attend.6.own_ref = bf16[576,640]{1,0:T(8,128)(2,1)} custom-call(bf16[576,576]{1,0:T(8,128)(2,1)} %bitcast.30, bf16[576,512]{1,0:T(8,128)(2,1)} %copy-done.3, bf16[576,512]{1,0:T(8,128)(2,1)} %collective-permute-done.8.refs_1_, bf16[576,512]{1,0:T(8,128)(2,1)} %collective-permute-done.11.refs_2_, bf16[576,512]{1,0:T(8,128)(2,1)} %collective-permute-done.12.refs_3_, ...), custom_call_target="tpu_custom_call" | custom-call | tf_op jit(solution)/shard_map/prefix_attend/pallas_call | solution.py:113
  101.1 9.2 %finish.1 = (bf16[8,72,448]{2,1,0:T(8,128)(2,1)}, bf16[8,72,448]{2,1,0:T(8,128)(2,1)}) custom-call(s32[1]{0:T(128)} %bitcast.core_ref, s32[8]{0:T(128)} %stack.35.order_ref, bf16[576,640]{1,0:T(8,128)(2,1)} %prefix_attend.6.own_ref, bf16[576,640]{1,0:T(8,128)(2,1)} %copy-done.6, bf16[576,640]{1,0:T(8,128)(2,1)} %slice_bitcast_fusion.tail_ref, ...), custom_call_target="tpu_custom_call" | custom-call | tf_op jit(solution)/shard_map/finish/pallas_call | solution.py:216
  110.5 2.1 %collective-permute-done.14 = bf16[8,72,448]{2,1,0:T(8,128)(2,1)S(1)} collective-permute-done((bf16[8,72,448]{2,1,0:T(8,128)(2,1)}, bf16[8,72,448]{2,1,0:T(8,128)(2,1)S(1)}, u32[]{:S(2)}, u32[]{:S(2)}) %collective-permute-start.14) | collective-permute-done | bytes 516128 | tf_op jit(solution)/shard_map/ppermute | solution.py:257
  115.5 2.7 %collective-permute-start.16 = (bf16[2,72,448]{2,1,0:T(8,128)(2,1)S(1)}, bf16[2,72,448]{2,1,0:T(8,128)(2,1)S(1)}, u32[]{:S(2)}, u32[]{:S(2)}) collective-permute-start(bf16[2,72,448]{2,1,0:T(8,128)(2,1)S(1)} %get-tuple-element.47), channel_id=1, source_target_pairs={{0,4},{2,6},{4,0},{6,2},{1,5},{3,7},{5,1},{7,3},{8,12},{10,14},{12... | collective-permute-start | bytes 387080 | tf_op jit(solution)/shard_map/ppermute | solution.py:254
  121.1 4.3 %collective-permute-done.16 = bf16[2,72,448]{2,1,0:T(8,128)(2,1)S(1)} collective-permute-done((bf16[2,72,448]{2,1,0:T(8,128)(2,1)S(1)}, bf16[2,72,448]{2,1,0:T(8,128)(2,1)S(1)}, u32[]{:S(2)}, u32[]{:S(2)}) %collective-permute-start.16) | collective-permute-done | bytes 129056 | tf_op jit(solution)/shard_map/ppermute | solution.py:254
  126.5 3.0 %collective-permute-start.18 = (bf16[72,448]{1,0:T(8,128)(2,1)S(1)}, bf16[72,448]{1,0:T(8,128)(2,1)S(1)}, u32[]{:S(2)}, u32[]{:S(2)}) collective-permute-start(bf16[72,448]{1,0:T(8,128)(2,1)S(1)} %fusion.7), channel_id=1, source_target_pairs={{0,8},{8,0},{1,9},{9,1},{2,10},{10,2},{3,11},{11,3},{4,12},{12,4},... | collective-permute-start | bytes 193544 | tf_op jit(solution)/shard_map/ppermute | solution.py:254
  129.5 2.9 %collective-permute-done.18 = bf16[72,448]{1,0:T(8,128)(2,1)S(1)} collective-permute-done((bf16[72,448]{1,0:T(8,128)(2,1)S(1)}, bf16[72,448]{1,0:T(8,128)(2,1)S(1)}, u32[]{:S(2)}, u32[]{:S(2)}) %collective-permute-start.18) | collective-permute-done | bytes 64544 | tf_op jit(solution)/shard_map/ppermute | solution.py:254
  (63 shorter events, 32.0 us)
Async XLA Ops:
  1.2 8.4 %collective-permute-start.1 = (bf16[64,576]{0,1:T(8,128)(2,1)S(1)}, bf16[64,576]{0,1:T(8,128)(2,1)}, u32[]{:S(2)}, u32[]{:S(2)}) collective-permute-start(bf16[64,576]{0,1:T(8,128)(2,1)S(1)} %copy.20), channel_id=1, source_target_pairs={{0,2},{2,4},{4,6},{6,0},{1,3},{3,5},{5,7},{7,1},{8,10},{10,12},{12... | collective-permute-start | bytes 221192 | tf_op jit(solution)/shard_map/ppermute | solution.py:254
  2.9 7.8 %collective-permute-start.2 = (bf16[64,576]{0,1:T(8,128)(2,1)S(1)}, bf16[64,576]{0,1:T(8,128)(2,1)}, u32[]{:S(2)}, u32[]{:S(2)}) collective-permute-start(bf16[64,576]{0,1:T(8,128)(2,1)S(1)} %copy.20), channel_id=1, source_target_pairs={{0,6},{2,0},{4,2},{6,4},{1,7},{3,1},{5,3},{7,5},{8,14},{10,8},{12,... | collective-permute-start | bytes 221192 | tf_op jit(solution)/shard_map/ppermute | solution.py:254
  4.5 8.2 %collective-permute-start.3 = (bf16[64,576]{0,1:T(8,128)(2,1)S(1)}, bf16[64,576]{0,1:T(8,128)(2,1)}, u32[]{:S(2)}, u32[]{:S(2)}) collective-permute-start(bf16[64,576]{0,1:T(8,128)(2,1)S(1)} %copy.20), channel_id=1, source_target_pairs={{0,4},{2,6},{4,0},{6,2},{1,5},{3,7},{5,1},{7,3},{8,12},{10,14},{12... | collective-permute-start | bytes 221192 | tf_op jit(solution)/shard_map/ppermute | solution.py:254
  9.3 10.5 %copy-start.4 = (bf16[72,16,576]{2,1,0:T(8,128)(2,1)S(1)}, bf16[72,16,576]{2,1,0:T(8,128)(2,1)}, u32[]{:S(2)}) copy-start(bf16[72,16,576]{2,1,0:T(8,128)(2,1)} %param.10) | copy-start | bytes 3981316
  9.5 23.0 %copy-start.1 = (bf16[72,8,576]{2,1,0:T(8,128)(2,1)}, bf16[72,8,576]{2,1,0:T(8,128)(2,1)S(1)}, u32[]{:S(2)}) copy-start(bf16[72,8,576]{2,1,0:T(8,128)(2,1)S(1)} %copy.25) | copy-start | bytes 1990660
  9.5 23.0 %collective-permute-start = (bf16[576,576]{1,0:T(8,128)(2,1)S(1)}, bf16[576,576]{1,0:T(8,128)(2,1)S(1)}, u32[]{:S(2)}, u32[]{:S(2)}) collective-permute-start(bf16[576,576]{1,0:T(8,128)(2,1)S(1)} %bitcast.28), channel_id=1, source_target_pairs={{0,1},{1,0},{2,3},{3,2},{4,5},{5,4},{6,7},{7,6},{8,9},{9,8},{10,11... | collective-permute-start | bytes 1990664 | tf_op jit(solution)/shard_map/ppermute | solution.py:257
  13.9 11.1 %collective-permute-start.4 = (bf16[576,256]{1,0:T(8,128)(2,1)S(1)}, bf16[576,256]{1,0:T(8,128)(2,1)S(1)}, u32[]{:S(2)}, u32[]{:S(2)}) collective-permute-start(bf16[576,256]{1,0:T(8,128)(2,1)S(1)} %maximum_bitcast_fusion), channel_id=1, source_target_pairs={{0,16},{16,8},{8,24},{24,0},{1,17},{17,9},{9,25},{25,1},{2,18},{18... | collective-permute-start | bytes 884744 | tf_op jit(solution)/shard_map/ppermute | solution.py:264
  15.9 13.9 %collective-permute-start.5 = (bf16[576,256]{1,0:T(8,128)(2,1)S(1)}, bf16[576,256]{1,0:T(8,128)(2,1)S(1)}, u32[]{:S(2)}, u32[]{:S(2)}) collective-permute-start(bf16[576,256]{1,0:T(8,128)(2,1)S(1)} %maximum_bitcast_fusion), channel_id=1, source_target_pairs={{0,24},{16,0},{8,16},{24,8},{1,25},{17,1},{9,17},{25,9},{2,26},{18... | collective-permute-start | bytes 884744 | tf_op jit(solution)/shard_map/ppermute | solution.py:264
  18.1 13.6 %collective-permute-start.6 = (bf16[576,256]{1,0:T(8,128)(2,1)S(1)}, bf16[576,256]{1,0:T(8,128)(2,1)S(1)}, u32[]{:S(2)}, u32[]{:S(2)}) collective-permute-start(bf16[576,256]{1,0:T(8,128)(2,1)S(1)} %maximum_bitcast_fusion), channel_id=1, source_target_pairs={{0,8},{16,24},{8,0},{24,16},{1,9},{17,25},{9,1},{25,17},{2,10},{18... | collective-permute-start | bytes 884744 | tf_op jit(solution)/shard_map/ppermute | solution.py:264
  33.8 37.6 %all-to-all-start = ((bf16[80,24,576]{2,1,0:T(8,128)(2,1)}), bf16[80,24,576]{2,1,0:T(8,128)(2,1)}, u32[]{:S(2)}, u32[]{:S(2)}) async-start(bf16[80,24,576]{2,1,0:T(8,128)(2,1)} %fusion.2), calls=%async_computation | async-start | bytes 4915200 | tf_op jit(solution)/shard_map/all_to_all | solution.py:267
  38.3 23.8 %copy-start.7 = (s32[72]{0:T(128)S(1)}, s32[72]{0:T(128)}, u32[]{:S(2)}) copy-start(s32[72]{0:T(128)} %param.11) | copy-start | bytes 868
  38.3 16.8 %collective-permute-start.10 = (bf16[576,512]{1,0:T(8,128)(2,1)}, bf16[576,512]{1,0:T(8,128)(2,1)}, u32[]{:S(2)}, u32[]{:S(2)}) collective-permute-start(bf16[576,512]{1,0:T(8,128)(2,1)} %pad_maximum_fusion.3.refs_1_), channel_id=1, source_target_pairs={{0,96},{32,0},{64,32},{96,64},{1,97},{33,1},{65,33},{97,65},{2,98}... | collective-permute-start | bytes 1769480 | tf_op jit(solution)/shard_map/ppermute | solution.py:254
  41.1 17.7 %collective-permute-start.9 = (bf16[576,512]{1,0:T(8,128)(2,1)}, bf16[576,512]{1,0:T(8,128)(2,1)}, u32[]{:S(2)}, u32[]{:S(2)}) collective-permute-start(bf16[576,512]{1,0:T(8,128)(2,1)} %pad_maximum_fusion.2.refs_0_), channel_id=1, source_target_pairs={{0,32},{32,64},{64,96},{96,0},{1,33},{33,65},{65,97},{97,1},{2,34}... | collective-permute-start | bytes 1769480 | tf_op jit(solution)/shard_map/ppermute | solution.py:254
  41.1 42.4 %collective-permute-start.7 = (bf16[576,512]{1,0:T(8,128)(2,1)}, bf16[576,512]{1,0:T(8,128)(2,1)S(1)}, u32[]{:S(2)}, u32[]{:S(2)}) collective-permute-start(bf16[576,512]{1,0:T(8,128)(2,1)} %pad_maximum_fusion.3.refs_1_), channel_id=1, source_target_pairs={{0,32},{32,64},{64,96},{96,0},{1,33},{33,65},{65,97},{97,1},{2,34}... | collective-permute-start | bytes 1769480 | tf_op jit(solution)/shard_map/ppermute | solution.py:254
  41.9 41.7 %collective-permute-start.8 = (bf16[576,512]{1,0:T(8,128)(2,1)}, bf16[576,512]{1,0:T(8,128)(2,1)}, u32[]{:S(2)}, u32[]{:S(2)}) collective-permute-start(bf16[576,512]{1,0:T(8,128)(2,1)} %pad_maximum_fusion.2.refs_0_), channel_id=1, source_target_pairs={{0,96},{32,0},{64,32},{96,64},{1,97},{33,1},{65,33},{97,65},{2,98}... | collective-permute-start | bytes 1769480 | tf_op jit(solution)/shard_map/ppermute | solution.py:254
  58.9 24.7 %collective-permute-start.11 = (bf16[576,512]{1,0:T(8,128)(2,1)}, bf16[576,512]{1,0:T(8,128)(2,1)}, u32[]{:S(2)}, u32[]{:S(2)}) collective-permute-start(bf16[576,512]{1,0:T(8,128)(2,1)} %collective-permute-done.9.refs_0_), channel_id=1, source_target_pairs={{0,32},{32,64},{64,96},{96,0},{1,33},{33,65},{65,97},{97,1},{2,34}... | collective-permute-start | bytes 1769480 | tf_op jit(solution)/shard_map/ppermute | solution.py:254
  58.9 24.7 %collective-permute-start.12 = (bf16[576,512]{1,0:T(8,128)(2,1)}, bf16[576,512]{1,0:T(8,128)(2,1)}, u32[]{:S(2)}, u32[]{:S(2)}) collective-permute-start(bf16[576,512]{1,0:T(8,128)(2,1)} %collective-permute-done.10.refs_1_), channel_id=1, source_target_pairs={{0,96},{32,0},{64,32},{96,64},{1,97},{33,1},{65,33},{97,65},{2,98}... | collective-permute-start | bytes 1769480 | tf_op jit(solution)/shard_map/ppermute | solution.py:254
  77.5 21.7 %all-to-all-start.1 = ((bf16[80,8,640]{2,1,0:T(8,128)(2,1)}), bf16[80,8,640]{2,1,0:T(8,128)(2,1)S(1)}, u32[]{:S(2)}, u32[]{:S(2)}) async-start(bf16[80,8,640]{2,1,0:T(8,128)(2,1)} %bitcast.31), calls=%async_computation.1 | async-start | bytes 1638400 | tf_op jit(solution)/shard_map/all_to_all | solution.py:267
  91.3 8.9 %collective-permute-start.13 = (bf16[576,640]{1,0:T(8,128)(2,1)}, bf16[576,640]{1,0:T(8,128)(2,1)S(1)}, u32[]{:S(2)}, u32[]{:S(2)}) collective-permute-start(bf16[576,640]{1,0:T(8,128)(2,1)} %prefix_attend.7), channel_id=1, source_target_pairs={{0,1},{1,0},{2,3},{3,2},{4,5},{5,4},{6,7},{7,6},{8,9},{9,8},{10,11... | collective-permute-start | bytes 2211848 | tf_op jit(solution)/shard_map/ppermute | solution.py:257
  110.3 2.3 %collective-permute-start.14 = (bf16[8,72,448]{2,1,0:T(8,128)(2,1)}, bf16[8,72,448]{2,1,0:T(8,128)(2,1)S(1)}, u32[]{:S(2)}, u32[]{:S(2)}) collective-permute-start(bf16[8,72,448]{2,1,0:T(8,128)(2,1)} %get-tuple-element.44), channel_id=1, source_target_pairs={{0,1},{1,0},{2,3},{3,2},{4,5},{5,4},{6,7},{7,6},{8,9},{9,8},{10,11... | collective-permute-start | bytes 1548296 | tf_op jit(solution)/shard_map/ppermute | solution.py:257
  113.8 7.3 %collective-permute-start.15 = (bf16[2,72,448]{2,1,0:T(8,128)(2,1)S(1)}, bf16[2,72,448]{2,1,0:T(8,128)(2,1)S(1)}, u32[]{:S(2)}, u32[]{:S(2)}) collective-permute-start(bf16[2,72,448]{2,1,0:T(8,128)(2,1)S(1)} %get-tuple-element.45), channel_id=1, source_target_pairs={{0,2},{2,4},{4,6},{6,0},{1,3},{3,5},{5,7},{7,1},{8,10},{10,12},{12... | collective-permute-start | bytes 387080 | tf_op jit(solution)/shard_map/ppermute | solution.py:254
  115.5 9.9 %collective-permute-start.16 = (bf16[2,72,448]{2,1,0:T(8,128)(2,1)S(1)}, bf16[2,72,448]{2,1,0:T(8,128)(2,1)S(1)}, u32[]{:S(2)}, u32[]{:S(2)}) collective-permute-start(bf16[2,72,448]{2,1,0:T(8,128)(2,1)S(1)} %get-tuple-element.47), channel_id=1, source_target_pairs={{0,4},{2,6},{4,0},{6,2},{1,5},{3,7},{5,1},{7,3},{8,12},{10,14},{12... | collective-permute-start | bytes 387080 | tf_op jit(solution)/shard_map/ppermute | solution.py:254
  118.2 7.2 %collective-permute-start.17 = (bf16[2,72,448]{2,1,0:T(8,128)(2,1)S(1)}, bf16[2,72,448]{2,1,0:T(8,128)(2,1)S(1)}, u32[]{:S(2)}, u32[]{:S(2)}) collective-permute-start(bf16[2,72,448]{2,1,0:T(8,128)(2,1)S(1)} %get-tuple-element.46), channel_id=1, source_target_pairs={{0,6},{2,0},{4,2},{6,4},{1,7},{3,1},{5,3},{7,5},{8,14},{10,8},{12,... | collective-permute-start | bytes 387080 | tf_op jit(solution)/shard_map/ppermute | solution.py:254
  126.5 5.9 %collective-permute-start.18 = (bf16[72,448]{1,0:T(8,128)(2,1)S(1)}, bf16[72,448]{1,0:T(8,128)(2,1)S(1)}, u32[]{:S(2)}, u32[]{:S(2)}) collective-permute-start(bf16[72,448]{1,0:T(8,128)(2,1)S(1)} %fusion.7), channel_id=1, source_target_pairs={{0,8},{8,0},{1,9},{9,1},{2,10},{10,2},{3,11},{11,3},{4,12},{12,4},... | collective-permute-start | bytes 193544 | tf_op jit(solution)/shard_map/ppermute | solution.py:254
  (5 other events, 20.0 us)

commit v5 on v4

--- a/solution.py
+++ b/solution.py
@@ -178,14 +178,15 @@
     heads, _, value_width = up_ref.shape
     req_rows = head_ref.shape[0]
     refs = (own_ref, received_ref, tail_ref)
+    rows = own_ref.shape[0]
     levels = [
-        jnp.sum(ref[:, width:].astype(jnp.float32), axis=1, keepdims=True) for ref in refs
+        jnp.sum(ref[:rows, width:].astype(jnp.float32), axis=1, keepdims=True) for ref in refs
     ]
     top = functools.reduce(jnp.maximum, levels)
     shares = [jnp.exp2(level - top) for level in levels]
     total = shares[0] + shares[1] + shares[2]
     context = sum(
-        ref[:, :width].astype(jnp.float32) * (share / total)
+        ref[:rows, :width].astype(jnp.float32) * (share / total)
         for ref, share in zip(refs, shares)
     )
     context_ref[...] = context.reshape(req_rows, heads, width)
@@ -284,21 +285,21 @@
     query_full = jnp.concatenate([query_latent, picked[:, :, nope_width:]], axis=2)
     query_rows = query_full.reshape(req_rows * heads_here, features)
 
-    held = jnp.concatenate(
-        [prefix_latent] + [ring(prefix_latent, "y", by) for by in (1, -1, 2)], axis=0
-    ).T
-    shifted = [z_ring(held, by) for by in (1, -1, 2)]
-    held = [
-        jnp.concatenate([held, shifted[0]], axis=1),
-        jnp.concatenate([shifted[1], shifted[2]], axis=1),
-    ]
+    columns = ("z_lo", "z_hi", "y")
+    copies = math.prod(lax.axis_size(name) for name in columns)
+    held = lax.all_to_all(
+        jnp.broadcast_to(prefix_latent[None], (copies, *prefix_latent.shape)), columns, 0, 0
+    )
     joined = jnp.pad(
         jnp.concatenate([tail_latent, query_full], axis=1),
         ((0, slots * devices - req_rows), (0, 0), (0, 0)),
     )
+    query_rows, joined = lax.optimization_barrier((query_rows, joined))
     query_other = other_core(query_rows)
     both = jnp.concatenate([query_rows, query_other], axis=0)
     both, held, joined = lax.optimization_barrier((both, held, joined))
+    held = held.reshape(2, -1, features)
+    held = [held[0].T, held[1].T]
 
     right = [ring(half, "x", 1) for half in held]
     left = [ring(half, "x", -1) for half in held]
@@ -322,7 +323,7 @@
     tail_part, state = lax.optimization_barrier((tail_part, state))
     late = [right[1], left[0]] + far
     tail_part = exchange(tail_part.reshape(devices * slots, heads_here, latent_width + 128))
-    tail_part = tail_part[:req_rows].reshape(req_rows * heads_here, latent_width + 128)
+    tail_part = tail_part.reshape(devices * slots * heads_here, latent_width + 128)
 
     packed_other = go(query_other, late, state, True, second=True)
     received = other_core(packed_other)

time: 134 us -> 131 us (0.978)
  local copies, waits for them, and re-layouts: 6.19 us -> 11 us
  other arithmetic: 10.3 us -> 5.99 us
  starting transfers between devices: 40.8 us -> 38.6 us
    all_to_all x0 -> x1, waiting for transfers between devices: none -> 13.1 us  [on_device(): lax.all_to_all(jnp.broadcast_to(prefix_latent[None], (copies, *prefix_lat...]
    ppermute x3 -> x0, waiting for transfers between devices: 9.21 us -> none  [z_ring(): return lax.ppermute(value, ('z_lo', 'z_hi'), pairs)]
    all_to_all x0 -> x1, starting transfers between devices: none -> 8.31 us  [on_device(): lax.all_to_all(jnp.broadcast_to(prefix_latent[None], (copies, *prefix_lat...]
    ppermute x3 -> x0, starting transfers between devices: 5.97 us -> none  [z_ring(): return lax.ppermute(value, ('z_lo', 'z_hi'), pairs)]
    ppermute x13 -> x10, waiting for transfers between devices: 19.8 us -> 14 us  [ring(): lax.ppermute(value, axis, [(i, (i + by) % size) for i in range(size)])]
    ppermute x13 -> x10, starting transfers between devices: 23.6 us -> 18.2 us  [ring(): lax.ppermute(value, axis, [(i, (i + by) % size) for i in range(size)])]
    broadcast_in_dim x0 -> x1, local copies, waits for them, and re-layouts: none -> 2.25 us  [on_device(): jnp.broadcast_to(prefix_latent[None], (copies, *prefix_latent.shape))]
    ppermute x3, waiting for transfers between devices: 2.11 us -> 4.32 us  [other_core(): return lax.ppermute(value, 'core', [(0, 1), (1, 0)])]
  transfers between devices with their start and end apart: 21 -> 16, of which waited for: 12 -> 10; matrix products, arithmetic and copies ran while one was open for 7% -> 7% of each run, Pallas kernels for 25% -> 26%
where the time goes in v5:
time: 131 us
  Pallas kernels  43.1 us (33%)
  starting transfers between devices  38.6 us (29%)
  waiting for transfers between devices  31.5 us (24%)
  local copies, waits for them, and re-layouts  11 us (8%)
  other arithmetic  5.99 us (5%)
    pallas_call x4, Pallas kernels, attend(): pl.pallas_call(functools.partial(attend_kernel, first, last, width, expon...  27.8 us
    ppermute x10, starting transfers between devices, ring(): lax.ppermute(value, axis, [(i, (i + by) % size) for i in range(size)])  18.2 us
    ppermute x10, waiting for transfers between devices, ring(): lax.ppermute(value, axis, [(i, (i + by) % size) for i in range(size)])  14 us
    all_to_all x1, waiting for transfers between devices, on_device(): lax.all_to_all(jnp.broadcast_to(prefix_latent[None], (copies, *prefix_lat...  13.1 us
    all_to_all x2, starting transfers between devices, exchange(): return lax.all_to_all(value, ('z_hi', 'y', 'core'), 0, 0, tiled=True)  11.5 us
    pallas_call x1, Pallas kernels, finish(): pl.pallas_call(functools.partial(finish_kernel, width), in_specs=[smem, s...  9.18 us
    all_to_all x1, starting transfers between devices, on_device(): lax.all_to_all(jnp.broadcast_to(prefix_latent[None], (copies, *prefix_lat...  8.31 us
    pallas_call x1, Pallas kernels, attend_tails(): pl.pallas_call(functools.partial(tail_kernel, span, width, exponent_scale...  6.15 us
  transfers between devices with their start and end apart: 16, of which 10 were waited for; matrix products, arithmetic and copies ran while one was open for 7% of the time, Pallas kernels for 26%

profile of v5, /device:TPU:0, one launch (start us, length us, event | category | flops | bytes accessed | tf_op | source)
XLA Modules:
  0.0 130.7 jit_solution(12010810535105544155)
XLA Ops:
  0.0 2.2 %broadcast_in_dim.21 = bf16[16,64,576]{2,1,0:T(8,128)(2,1)} broadcast(bf16[64,576]{1,0:T(8,128)(2,1)} %param.9), dimensions={1,2} | broadcast | bytes 1253376 | tf_op jit(solution)/shard_map/broadcast_in_dim | solution.py:291
  2.3 8.3 %all-to-all-start = ((bf16[16,64,576]{2,1,0:T(8,128)(2,1)}), bf16[16,64,576]{2,1,0:T(8,128)(2,1)}, u32[]{:S(2)}, u32[]{:S(2)}) async-start(bf16[16,64,576]{2,1,0:T(8,128)(2,1)} %broadcast_in_dim.21), calls=%async_computation | async-start | bytes 2621440 | tf_op jit(solution)/shard_map/all_to_all | solution.py:290
  13.2 1.7 %fusion.2 = bf16[80,24,576]{2,1,0:T(8,128)(2,1)} fusion(bf16[72,8,576]{2,1,0:T(8,128)(2,1)S(1)} %copy.20, bf16[72,16,576]{2,1,0:T(8,128)(2,1)S(1)} %copy-done.5), kind=kLoop, calls=%fused_computation.4 | loop fusion | flops 7741440 | bytes 4202496 | tf_op jit(solution)/shard_map/concatenate | solution.py:294
  14.8 2.2 %collective-permute-done.q_ref = bf16[576,576]{1,0:T(8,128)(2,1)S(1)} collective-permute-done((bf16[576,576]{1,0:T(8,128)(2,1)S(1)}, bf16[576,576]{1,0:T(8,128)(2,1)S(1)}, u32[]{:S(2)}, u32[]{:S(2)}) %collective-permute-start) | collective-permute-done | bytes 663584 | tf_op jit(solution)/shard_map/ppermute | solution.py:258
  18.4 13.1 %all-to-all-done = bf16[16,64,576]{2,1,0:T(8,128)(2,1)} async-done(((bf16[16,64,576]{2,1,0:T(8,128)(2,1)}), bf16[16,64,576]{2,1,0:T(8,128)(2,1)}, u32[]{:S(2)}, u32[]{:S(2)}) %all-to-all-start) | async-done | bytes 1179680 | tf_op jit(solution)/shard_map/all_to_all | solution.py:290
  31.5 4.5 %all-to-all-start.1 = ((bf16[80,24,576]{2,1,0:T(8,128)(2,1)}), bf16[80,24,576]{2,1,0:T(8,128)(2,1)}, u32[]{:S(2)}, u32[]{:S(2)}) async-start(bf16[80,24,576]{2,1,0:T(8,128)(2,1)} %fusion.2), calls=%async_computation.1 | async-start | bytes 4915200 | tf_op jit(solution)/shard_map/all_to_all | solution.py:268
  41.0 1.7 %collective-permute-start.4 = (bf16[576,512]{1,0:T(8,128)(2,1)}, bf16[576,512]{1,0:T(8,128)(2,1)}, u32[]{:S(2)}, u32[]{:S(2)}) collective-permute-start(bf16[576,512]{1,0:T(8,128)(2,1)} %bitcast.36), channel_id=1, source_target_pairs={{0,96},{32,0},{64,32},{96,64},{1,97},{33,1},{65,33},{97,65},{2,98}... | collective-permute-start | bytes 1769480 | tf_op jit(solution)/shard_map/ppermute | solution.py:255
  43.0 3.0 %collective-permute-start.2 = (bf16[576,512]{1,0:T(8,128)(2,1)}, bf16[576,512]{1,0:T(8,128)(2,1)}, u32[]{:S(2)}, u32[]{:S(2)}) collective-permute-start(bf16[576,512]{1,0:T(8,128)(2,1)} %bitcast.14.refs_0_), channel_id=1, source_target_pairs={{0,96},{32,0},{64,32},{96,64},{1,97},{33,1},{65,33},{97,65},{2,98}... | collective-permute-start | bytes 1769480 | tf_op jit(solution)/shard_map/ppermute | solution.py:255
  46.0 6.3 %prefix_attend.4 = (f32[1152,256]{1,0:T(8,128)}, f32[1152,512]{1,0:T(8,128)}) custom-call(bf16[1152,576]{1,0:T(8,128)(2,1)} %pad_maximum_fusion.q_ref, bf16[576,512]{1,0:T(8,128)(2,1)} %bitcast.14.refs_0_, bf16[576,512]{1,0:T(8,128)(2,1)} %bitcast.38), custom_call_target="tpu_custom_call" | custom-call | tf_op jit(solution)/shard_map/prefix_attend/pallas_call | solution.py:113
  52.2 4.9 %collective-permute-done.3.refs_0_ = bf16[576,512]{1,0:T(8,128)(2,1)} collective-permute-done((bf16[576,512]{1,0:T(8,128)(2,1)}, bf16[576,512]{1,0:T(8,128)(2,1)}, u32[]{:S(2)}, u32[]{:S(2)}) %collective-permute-start.3) | collective-permute-done | bytes 589856 | tf_op jit(solution)/shard_map/ppermute | solution.py:255
  57.5 1.5 %collective-permute-start.5 = (bf16[576,512]{1,0:T(8,128)(2,1)}, bf16[576,512]{1,0:T(8,128)(2,1)}, u32[]{:S(2)}, u32[]{:S(2)}) collective-permute-start(bf16[576,512]{1,0:T(8,128)(2,1)} %collective-permute-done.3.refs_0_), channel_id=1, source_target_pairs={{0,32},{32,64},{64,96},{96,0},{1,33},{33,65},{65,97},{97,1},{2,34}... | collective-permute-start | bytes 1769480 | tf_op jit(solution)/shard_map/ppermute | solution.py:255
  59.0 1.7 %collective-permute-start.6 = (bf16[576,512]{1,0:T(8,128)(2,1)}, bf16[576,512]{1,0:T(8,128)(2,1)}, u32[]{:S(2)}, u32[]{:S(2)}) collective-permute-start(bf16[576,512]{1,0:T(8,128)(2,1)} %collective-permute-done.4.refs_1_), channel_id=1, source_target_pairs={{0,96},{32,0},{64,32},{96,64},{1,97},{33,1},{65,33},{97,65},{2,98}... | collective-permute-start | bytes 1769480 | tf_op jit(solution)/shard_map/ppermute | solution.py:255
  61.3 7.6 %prefix_attend.5 = (f32[1152,256]{1,0:T(8,128)}, f32[1152,512]{1,0:T(8,128)}) custom-call(bf16[1152,576]{1,0:T(8,128)(2,1)} %pad_maximum_fusion.q_ref, bf16[576,512]{1,0:T(8,128)(2,1)} %collective-permute-done.3.refs_0_, bf16[576,512]{1,0:T(8,128)(2,1)} %collective-permute-done.4.refs_1_, f32[1152,256]{1,0:T(8,128)} %get-tuple-element.35.refs_2_, ...), custom_call_target="tpu_custom_call" | custom-call | tf_op jit(solution)/shard_map/prefix_attend/pallas_call | solution.py:113
  69.0 6.1 %tail_attend.1 = bf16[16,5,8,640]{3,2,1,0:T(8,128)(2,1)} custom-call(s32[5]{0:T(128)} %pad_dynamic-slice_fusion.length_ref, bf16[16,5,24,576]{3,2,1,0:T(8,128)(2,1)} %bitcast.15.joined_ref), custom_call_target="tpu_custom_call" | custom-call | tf_op jit(solution)/shard_map/tail_attend/pallas_call | solution.py:148
  75.2 7.1 %all-to-all-start.2 = ((bf16[80,8,640]{2,1,0:T(8,128)(2,1)}), bf16[80,8,640]{2,1,0:T(8,128)(2,1)S(1)}, u32[]{:S(2)}, u32[]{:S(2)}) async-start(bf16[80,8,640]{2,1,0:T(8,128)(2,1)} %bitcast.32), calls=%async_computation.2 | async-start | bytes 1638400 | tf_op jit(solution)/shard_map/all_to_all | solution.py:268
  83.1 6.9 %prefix_attend.7 = bf16[576,640]{1,0:T(8,128)(2,1)} custom-call(bf16[576,576]{1,0:T(8,128)(2,1)} %copy-done.3, bf16[576,512]{1,0:T(8,128)(2,1)} %copy-done.4, bf16[576,512]{1,0:T(8,128)(2,1)} %collective-permute-done.2.refs_1_, bf16[576,512]{1,0:T(8,128)(2,1)} %collective-permute-done.5.refs_2_, bf16[576,512]{1,0:T(8,128)(2,1)} %collective-permute-done.6.refs_3_, ...), custom_call_target="tpu_custom_call" | custom-call | tf_op jit(solution)/shard_map/prefix_attend/pallas_call | solution.py:113
  91.0 6.9 %prefix_attend.6.own_ref = bf16[576,640]{1,0:T(8,128)(2,1)} custom-call(bf16[576,576]{1,0:T(8,128)(2,1)} %bitcast.31, bf16[576,512]{1,0:T(8,128)(2,1)} %copy-done.4, bf16[576,512]{1,0:T(8,128)(2,1)} %collective-permute-done.2.refs_1_, bf16[576,512]{1,0:T(8,128)(2,1)} %collective-permute-done.5.refs_2_, bf16[576,512]{1,0:T(8,128)(2,1)} %collective-permute-done.6.refs_3_, ...), custom_call_target="tpu_custom_call" | custom-call | tf_op jit(solution)/shard_map/prefix_attend/pallas_call | solution.py:113
  99.1 9.2 %finish.1 = (bf16[8,72,448]{2,1,0:T(8,128)(2,1)}, bf16[8,72,448]{2,1,0:T(8,128)(2,1)}) custom-call(s32[1]{0:T(128)} %bitcast.core_ref, s32[8]{0:T(128)} %stack.35.order_ref, bf16[576,640]{1,0:T(8,128)(2,1)} %prefix_attend.6.own_ref, bf16[576,640]{1,0:T(8,128)(2,1)} %copy-done.7, bf16[640,640]{1,0:T(8,128)(2,1)} %bitcast.33, bf16[8,512,128]{2,1,0:T(8,128)(2,1)} %up_ref.1, ...), custom_call_target="tpu_custom_call" | custom-call | tf_op jit(solution)/shard_map/finish/pallas_call | solution.py:217
  108.5 2.1 %collective-permute-done.8 = bf16[8,72,448]{2,1,0:T(8,128)(2,1)S(1)} collective-permute-done((bf16[8,72,448]{2,1,0:T(8,128)(2,1)}, bf16[8,72,448]{2,1,0:T(8,128)(2,1)S(1)}, u32[]{:S(2)}, u32[]{:S(2)}) %collective-permute-start.8) | collective-permute-done | bytes 516128 | tf_op jit(solution)/shard_map/ppermute | solution.py:258
  111.7 3.3 %collective-permute-start.10 = (bf16[2,72,448]{2,1,0:T(8,128)(2,1)S(1)}, bf16[2,72,448]{2,1,0:T(8,128)(2,1)S(1)}, u32[]{:S(2)}, u32[]{:S(2)}) collective-permute-start(bf16[2,72,448]{2,1,0:T(8,128)(2,1)S(1)} %get-tuple-element.51), channel_id=1, source_target_pairs={{0,4},{2,6},{4,0},{6,2},{1,5},{3,7},{5,1},{7,3},{8,12},{10,14},{12... | collective-permute-start | bytes 387080 | tf_op jit(solution)/shard_map/ppermute | solution.py:255
  117.0 3.0 %collective-permute-done.10 = bf16[2,72,448]{2,1,0:T(8,128)(2,1)S(1)} collective-permute-done((bf16[2,72,448]{2,1,0:T(8,128)(2,1)S(1)}, bf16[2,72,448]{2,1,0:T(8,128)(2,1)S(1)}, u32[]{:S(2)}, u32[]{:S(2)}) %collective-permute-start.10) | collective-permute-done | bytes 129056 | tf_op jit(solution)/shard_map/ppermute | solution.py:255
  120.0 2.8 %collective-permute-done.11 = bf16[2,72,448]{2,1,0:T(8,128)(2,1)S(1)} collective-permute-done((bf16[2,72,448]{2,1,0:T(8,128)(2,1)S(1)}, bf16[2,72,448]{2,1,0:T(8,128)(2,1)S(1)}, u32[]{:S(2)}, u32[]{:S(2)}) %collective-permute-start.11) | collective-permute-done | bytes 129056 | tf_op jit(solution)/shard_map/ppermute | solution.py:255
  124.1 3.2 %collective-permute-start.12 = (bf16[72,448]{1,0:T(8,128)(2,1)S(1)}, bf16[72,448]{1,0:T(8,128)(2,1)S(1)}, u32[]{:S(2)}, u32[]{:S(2)}) collective-permute-start(bf16[72,448]{1,0:T(8,128)(2,1)S(1)} %fusion.7), channel_id=1, source_target_pairs={{0,8},{8,0},{1,9},{9,1},{2,10},{10,2},{3,11},{11,3},{4,12},{12,4},... | collective-permute-start | bytes 193544 | tf_op jit(solution)/shard_map/ppermute | solution.py:255
  127.2 2.8 %collective-permute-done.12 = bf16[72,448]{1,0:T(8,128)(2,1)S(1)} collective-permute-done((bf16[72,448]{1,0:T(8,128)(2,1)S(1)}, bf16[72,448]{1,0:T(8,128)(2,1)S(1)}, u32[]{:S(2)}, u32[]{:S(2)}) %collective-permute-start.12) | collective-permute-done | bytes 64544 | tf_op jit(solution)/shard_map/ppermute | solution.py:255
  (56 shorter events, 18.3 us)
Async XLA Ops:
  0.0 10.6 %copy-start = (bf16[576,1536]{1,0:T(8,128)(2,1)S(1)}, bf16[576,1536]{1,0:T(8,128)(2,1)}, u32[]{:S(2)}) copy-start(bf16[576,1536]{1,0:T(8,128)(2,1)} %param.8) | copy-start | bytes 5308420
  0.0 10.6 %copy-start.8 = (s32[72]{0:T(128)S(1)}, s32[72]{0:T(128)}, u32[]{:S(2)}) copy-start(s32[72]{0:T(128)} %param.12) | copy-start | bytes 868
  2.3 9.5 %copy-start.6 = (bf16[8,128,512]{2,1,0:T(8,128)(2,1)S(1)}, bf16[8,128,512]{2,1,0:T(8,128)(2,1)}, u32[]{:S(2)}) copy-start(bf16[8,128,512]{2,1,0:T(8,128)(2,1)} %param.13) | copy-start | bytes 3145732
  2.3 29.2 %all-to-all-start = ((bf16[16,64,576]{2,1,0:T(8,128)(2,1)}), bf16[16,64,576]{2,1,0:T(8,128)(2,1)}, u32[]{:S(2)}, u32[]{:S(2)}) async-start(bf16[16,64,576]{2,1,0:T(8,128)(2,1)} %broadcast_in_dim.21), calls=%async_computation | async-start | bytes 2621440 | tf_op jit(solution)/shard_map/all_to_all | solution.py:290
  11.8 1.4 %copy-start.5 = (bf16[72,16,576]{2,1,0:T(8,128)(2,1)S(1)}, bf16[72,16,576]{2,1,0:T(8,128)(2,1)}, u32[]{:S(2)}) copy-start(bf16[72,16,576]{2,1,0:T(8,128)(2,1)} %param.10) | copy-start | bytes 3981316
  13.2 5.2 %copy-start.1 = (bf16[72,8,576]{2,1,0:T(8,128)(2,1)}, bf16[72,8,576]{2,1,0:T(8,128)(2,1)S(1)}, u32[]{:S(2)}) copy-start(bf16[72,8,576]{2,1,0:T(8,128)(2,1)S(1)} %copy.20) | copy-start | bytes 1990660
  14.8 2.2 %collective-permute-start = (bf16[576,576]{1,0:T(8,128)(2,1)S(1)}, bf16[576,576]{1,0:T(8,128)(2,1)S(1)}, u32[]{:S(2)}, u32[]{:S(2)}) collective-permute-start(bf16[576,576]{1,0:T(8,128)(2,1)S(1)} %bitcast.29), channel_id=1, source_target_pairs={{0,1},{1,0},{2,3},{3,2},{4,5},{5,4},{6,7},{7,6},{8,9},{9,8},{10,11... | collective-permute-start | bytes 1990664 | tf_op jit(solution)/shard_map/ppermute | solution.py:258
  17.0 14.4 %copy-start.3 = (bf16[576,576]{1,0:T(8,128)(2,1)}, bf16[576,576]{1,0:T(8,128)(2,1)S(1)}, u32[]{:S(2)}) copy-start(bf16[576,576]{1,0:T(8,128)(2,1)S(1)} %collective-permute-done.q_ref) | copy-start | bytes 1990660
  31.5 37.6 %all-to-all-start.1 = ((bf16[80,24,576]{2,1,0:T(8,128)(2,1)}), bf16[80,24,576]{2,1,0:T(8,128)(2,1)}, u32[]{:S(2)}, u32[]{:S(2)}) async-start(bf16[80,24,576]{2,1,0:T(8,128)(2,1)} %fusion.2), calls=%async_computation.1 | async-start | bytes 4915200 | tf_op jit(solution)/shard_map/all_to_all | solution.py:268
  37.3 23.4 %copy-start.9 = (s32[72]{0:T(128)S(1)}, s32[72]{0:T(128)}, u32[]{:S(2)}) copy-start(s32[72]{0:T(128)} %param.11) | copy-start | bytes 868
  39.5 17.7 %collective-permute-start.3 = (bf16[576,512]{1,0:T(8,128)(2,1)}, bf16[576,512]{1,0:T(8,128)(2,1)}, u32[]{:S(2)}, u32[]{:S(2)}) collective-permute-start(bf16[576,512]{1,0:T(8,128)(2,1)} %bitcast.14.refs_0_), channel_id=1, source_target_pairs={{0,32},{32,64},{64,96},{96,0},{1,33},{33,65},{65,97},{97,1},{2,34}... | collective-permute-start | bytes 1769480 | tf_op jit(solution)/shard_map/ppermute | solution.py:255
  41.0 16.5 %collective-permute-start.4 = (bf16[576,512]{1,0:T(8,128)(2,1)}, bf16[576,512]{1,0:T(8,128)(2,1)}, u32[]{:S(2)}, u32[]{:S(2)}) collective-permute-start(bf16[576,512]{1,0:T(8,128)(2,1)} %bitcast.36), channel_id=1, source_target_pairs={{0,96},{32,0},{64,32},{96,64},{1,97},{33,1},{65,33},{97,65},{2,98}... | collective-permute-start | bytes 1769480 | tf_op jit(solution)/shard_map/ppermute | solution.py:255
  42.7 39.5 %collective-permute-start.1 = (bf16[576,512]{1,0:T(8,128)(2,1)}, bf16[576,512]{1,0:T(8,128)(2,1)S(1)}, u32[]{:S(2)}, u32[]{:S(2)}) collective-permute-start(bf16[576,512]{1,0:T(8,128)(2,1)} %bitcast.37), channel_id=1, source_target_pairs={{0,32},{32,64},{64,96},{96,0},{1,33},{33,65},{65,97},{97,1},{2,34}... | collective-permute-start | bytes 1769480 | tf_op jit(solution)/shard_map/ppermute | solution.py:255
  43.0 39.3 %collective-permute-start.2 = (bf16[576,512]{1,0:T(8,128)(2,1)}, bf16[576,512]{1,0:T(8,128)(2,1)}, u32[]{:S(2)}, u32[]{:S(2)}) collective-permute-start(bf16[576,512]{1,0:T(8,128)(2,1)} %bitcast.14.refs_0_), channel_id=1, source_target_pairs={{0,96},{32,0},{64,32},{96,64},{1,97},{33,1},{65,33},{97,65},{2,98}... | collective-permute-start | bytes 1769480 | tf_op jit(solution)/shard_map/ppermute | solution.py:255
  57.5 24.8 %collective-permute-start.5 = (bf16[576,512]{1,0:T(8,128)(2,1)}, bf16[576,512]{1,0:T(8,128)(2,1)}, u32[]{:S(2)}, u32[]{:S(2)}) collective-permute-start(bf16[576,512]{1,0:T(8,128)(2,1)} %collective-permute-done.3.refs_0_), channel_id=1, source_target_pairs={{0,32},{32,64},{64,96},{96,0},{1,33},{33,65},{65,97},{97,1},{2,34}... | collective-permute-start | bytes 1769480 | tf_op jit(solution)/shard_map/ppermute | solution.py:255
  59.0 23.3 %collective-permute-start.6 = (bf16[576,512]{1,0:T(8,128)(2,1)}, bf16[576,512]{1,0:T(8,128)(2,1)}, u32[]{:S(2)}, u32[]{:S(2)}) collective-permute-start(bf16[576,512]{1,0:T(8,128)(2,1)} %collective-permute-done.4.refs_1_), channel_id=1, source_target_pairs={{0,96},{32,0},{64,32},{96,64},{1,97},{33,1},{65,33},{97,65},{2,98}... | collective-permute-start | bytes 1769480 | tf_op jit(solution)/shard_map/ppermute | solution.py:255
  75.2 22.8 %all-to-all-start.2 = ((bf16[80,8,640]{2,1,0:T(8,128)(2,1)}), bf16[80,8,640]{2,1,0:T(8,128)(2,1)S(1)}, u32[]{:S(2)}, u32[]{:S(2)}) async-start(bf16[80,8,640]{2,1,0:T(8,128)(2,1)} %bitcast.32), calls=%async_computation.2 | async-start | bytes 1638400 | tf_op jit(solution)/shard_map/all_to_all | solution.py:268
  90.0 8.0 %collective-permute-start.7 = (bf16[576,640]{1,0:T(8,128)(2,1)}, bf16[576,640]{1,0:T(8,128)(2,1)S(1)}, u32[]{:S(2)}, u32[]{:S(2)}) collective-permute-start(bf16[576,640]{1,0:T(8,128)(2,1)} %prefix_attend.7), channel_id=1, source_target_pairs={{0,1},{1,0},{2,3},{3,2},{4,5},{5,4},{6,7},{7,6},{8,9},{9,8},{10,11... | collective-permute-start | bytes 2211848 | tf_op jit(solution)/shard_map/ppermute | solution.py:258
  98.0 1.1 copy-start.2
  108.3 2.3 %collective-permute-start.8 = (bf16[8,72,448]{2,1,0:T(8,128)(2,1)}, bf16[8,72,448]{2,1,0:T(8,128)(2,1)S(1)}, u32[]{:S(2)}, u32[]{:S(2)}) collective-permute-start(bf16[8,72,448]{2,1,0:T(8,128)(2,1)} %get-tuple-element.46), channel_id=1, source_target_pairs={{0,1},{1,0},{2,3},{3,2},{4,5},{5,4},{6,7},{7,6},{8,9},{9,8},{10,11... | collective-permute-start | bytes 1548296 | tf_op jit(solution)/shard_map/ppermute | solution.py:258
  111.7 8.3 %collective-permute-start.10 = (bf16[2,72,448]{2,1,0:T(8,128)(2,1)S(1)}, bf16[2,72,448]{2,1,0:T(8,128)(2,1)S(1)}, u32[]{:S(2)}, u32[]{:S(2)}) collective-permute-start(bf16[2,72,448]{2,1,0:T(8,128)(2,1)S(1)} %get-tuple-element.51), channel_id=1, source_target_pairs={{0,4},{2,6},{4,0},{6,2},{1,5},{3,7},{5,1},{7,3},{8,12},{10,14},{12... | collective-permute-start | bytes 387080 | tf_op jit(solution)/shard_map/ppermute | solution.py:255
  115.0 7.8 %collective-permute-start.11 = (bf16[2,72,448]{2,1,0:T(8,128)(2,1)S(1)}, bf16[2,72,448]{2,1,0:T(8,128)(2,1)S(1)}, u32[]{:S(2)}, u32[]{:S(2)}) collective-permute-start(bf16[2,72,448]{2,1,0:T(8,128)(2,1)S(1)} %get-tuple-element.50), channel_id=1, source_target_pairs={{0,6},{2,0},{4,2},{6,4},{1,7},{3,1},{5,3},{7,5},{8,14},{10,8},{12,... | collective-permute-start | bytes 387080 | tf_op jit(solution)/shard_map/ppermute | solution.py:255
  116.2 6.9 %collective-permute-start.9 = (bf16[2,72,448]{2,1,0:T(8,128)(2,1)S(1)}, bf16[2,72,448]{2,1,0:T(8,128)(2,1)S(1)}, u32[]{:S(2)}, u32[]{:S(2)}) collective-permute-start(bf16[2,72,448]{2,1,0:T(8,128)(2,1)S(1)} %get-tuple-element.49), channel_id=1, source_target_pairs={{0,2},{2,4},{4,6},{6,0},{1,3},{3,5},{5,7},{7,1},{8,10},{10,12},{12... | collective-permute-start | bytes 387080 | tf_op jit(solution)/shard_map/ppermute | solution.py:255
  124.1 5.9 %collective-permute-start.12 = (bf16[72,448]{1,0:T(8,128)(2,1)S(1)}, bf16[72,448]{1,0:T(8,128)(2,1)S(1)}, u32[]{:S(2)}, u32[]{:S(2)}) collective-permute-start(bf16[72,448]{1,0:T(8,128)(2,1)S(1)} %fusion.7), channel_id=1, source_target_pairs={{0,8},{8,0},{1,9},{9,1},{2,10},{10,2},{3,11},{11,3},{4,12},{12,4},... | collective-permute-start | bytes 193544 | tf_op jit(solution)/shard_map/ppermute | solution.py:255
  (2 other events, 1.8 us)

commit v6 on v5

--- a/solution.py
+++ b/solution.py
@@ -123,33 +123,34 @@
 
 
 def tail_kernel(span, width, exponent_scale, length_ref, joined_ref, out_ref):
-    sources, _, tall, features = joined_ref.shape
+    sources, slots, tall, features = joined_ref.shape
     heads = tall - span
-    keys = joined_ref[:, 0, :span].reshape(sources * span, features)
-    q = joined_ref[:, 0, span:].reshape(sources * heads, features)
-    s = lax.dot_general(q, keys, (((1,), (1,)), ((), ())), preferred_element_type=jnp.float32)
-    usable = lax.broadcasted_iota(jnp.int32, s.shape, 1) < length_ref[pl.program_id(0)]
-    s = jnp.where(usable, s, -1e30)
-    highest = jnp.max(s, axis=1, keepdims=True)
-    w = jnp.where(usable, jnp.exp2((s - highest) * exponent_scale), 0.0)
-    weight_sum = jnp.sum(w, axis=1, keepdims=True)
-    acc = jnp.dot(w.astype(jnp.bfloat16), keys[:, :width], preferred_element_type=jnp.float32)
-    context, level = pack(acc, weight_sum, highest, exponent_scale)
-    out_ref[:, 0, :, :width] = context.reshape(sources, heads, width)
-    out_ref[:, 0, :, width:] = level.reshape(sources, heads, 128)
+    for slot in range(slots):
+        keys = joined_ref[:, slot, :span].reshape(sources * span, features)
+        q = joined_ref[:, slot, span:].reshape(sources * heads, features)
+        s = lax.dot_general(q, keys, (((1,), (1,)), ((), ())), preferred_element_type=jnp.float32)
+        usable = lax.broadcasted_iota(jnp.int32, s.shape, 1) < length_ref[slot]
+        s = jnp.where(usable, s, -1e30)
+        highest = jnp.max(s, axis=1, keepdims=True)
+        w = jnp.where(usable, jnp.exp2((s - highest) * exponent_scale), 0.0)
+        weight_sum = jnp.sum(w, axis=1, keepdims=True)
+        acc = jnp.dot(w.astype(jnp.bfloat16), keys[:, :width], preferred_element_type=jnp.float32)
+        context, level = pack(acc, weight_sum, highest, exponent_scale)
+        out_ref[:, slot, :, :width] = context.reshape(sources, heads, width)
+        out_ref[:, slot, :, width:] = level.reshape(sources, heads, 128)
 
 
 def attend_tails(joined, span, length, width, exponent_scale):
     sources, slots, tall, features = joined.shape
     heads = tall - span
     block = lambda last2, last1: pl.BlockSpec(
-        (sources, 1, last2, last1), lambda i, *_: (0, i, 0, 0)
+        (sources, slots, last2, last1), lambda i, *_: (0, 0, 0, 0)
     )
     return pl.pallas_call(
         functools.partial(tail_kernel, span, width, exponent_scale),
         grid_spec=pltpu.PrefetchScalarGridSpec(
             num_scalar_prefetch=1,
-            grid=(slots,),
+            grid=(1,),
             in_specs=[block(tall, features)],
             out_specs=block(heads, width + 128),
         ),

time: 131 us -> 131 us (level)
  transfers between devices with their start and end apart: 16 -> 16, of which waited for: 10 -> 11; matrix products, arithmetic and copies ran while one was open for 7% -> 7% of each run, Pallas kernels for 26% -> 26%
where the time goes in v6:
time: 131 us; the launch traced here: 130 us
  Pallas kernels  42.4 us (32%)
  starting transfers between devices  38.6 us (29%)
  waiting for transfers between devices  31.6 us (24%)
  local copies, waits for them, and re-layouts  10.9 us (8%)
  other arithmetic  5.99 us (5%)
    pallas_call x4, Pallas kernels, attend(): pl.pallas_call(functools.partial(attend_kernel, first, last, width, expon...  27.8 us
    ppermute x10, starting transfers between devices, ring(): lax.ppermute(value, axis, [(i, (i + by) % size) for i in range(size)])  18.2 us
    ppermute x10, waiting for transfers between devices, ring(): lax.ppermute(value, axis, [(i, (i + by) % size) for i in range(size)])  14.2 us
    all_to_all x1, waiting for transfers between devices, on_device(): lax.all_to_all(jnp.broadcast_to(prefix_latent[None], (copies, *prefix_lat...  13.1 us
    all_to_all x2, starting transfers between devices, exchange(): return lax.all_to_all(value, ('z_hi', 'y', 'core'), 0, 0, tiled=True)  11.5 us
    pallas_call x1, Pallas kernels, finish(): pl.pallas_call(functools.partial(finish_kernel, width), in_specs=[smem, s...  9.18 us
    all_to_all x1, starting transfers between devices, on_device(): lax.all_to_all(jnp.broadcast_to(prefix_latent[None], (copies, *prefix_lat...  8.31 us
    pallas_call x1, Pallas kernels, attend_tails(): pl.pallas_call(functools.partial(tail_kernel, span, width, exponent_scale...  5.5 us
  transfers between devices with their start and end apart: 16, of which 11 were waited for; matrix products, arithmetic and copies ran while one was open for 7% of the time, Pallas kernels for 26%

profile of v6, /device:TPU:0, one launch (start us, length us, event | category | flops | bytes accessed | tf_op | source)
XLA Modules:
  0.0 130.0 jit_solution(11808608057352462607)
XLA Ops:
  0.0 2.2 %broadcast_in_dim.21 = bf16[16,64,576]{2,1,0:T(8,128)(2,1)} broadcast(bf16[64,576]{1,0:T(8,128)(2,1)} %param.9), dimensions={1,2} | broadcast | bytes 1253376 | tf_op jit(solution)/shard_map/broadcast_in_dim | solution.py:292
  2.3 8.3 %all-to-all-start = ((bf16[16,64,576]{2,1,0:T(8,128)(2,1)}), bf16[16,64,576]{2,1,0:T(8,128)(2,1)}, u32[]{:S(2)}, u32[]{:S(2)}) async-start(bf16[16,64,576]{2,1,0:T(8,128)(2,1)} %broadcast_in_dim.21), calls=%async_computation | async-start | bytes 2621440 | tf_op jit(solution)/shard_map/all_to_all | solution.py:291
  13.2 1.7 %fusion.2 = bf16[80,24,576]{2,1,0:T(8,128)(2,1)} fusion(bf16[72,8,576]{2,1,0:T(8,128)(2,1)S(1)} %copy.20, bf16[72,16,576]{2,1,0:T(8,128)(2,1)S(1)} %copy-done.5), kind=kLoop, calls=%fused_computation.4 | loop fusion | flops 7741440 | bytes 4202496 | tf_op jit(solution)/shard_map/concatenate | solution.py:295
  14.8 2.2 %collective-permute-done.q_ref = bf16[576,576]{1,0:T(8,128)(2,1)S(1)} collective-permute-done((bf16[576,576]{1,0:T(8,128)(2,1)S(1)}, bf16[576,576]{1,0:T(8,128)(2,1)S(1)}, u32[]{:S(2)}, u32[]{:S(2)}) %collective-permute-start) | collective-permute-done | bytes 663584 | tf_op jit(solution)/shard_map/ppermute | solution.py:259
  18.4 13.1 %all-to-all-done = bf16[16,64,576]{2,1,0:T(8,128)(2,1)} async-done(((bf16[16,64,576]{2,1,0:T(8,128)(2,1)}), bf16[16,64,576]{2,1,0:T(8,128)(2,1)}, u32[]{:S(2)}, u32[]{:S(2)}) %all-to-all-start) | async-done | bytes 1179680 | tf_op jit(solution)/shard_map/all_to_all | solution.py:291
  31.5 4.5 %all-to-all-start.1 = ((bf16[80,24,576]{2,1,0:T(8,128)(2,1)}), bf16[80,24,576]{2,1,0:T(8,128)(2,1)}, u32[]{:S(2)}, u32[]{:S(2)}) async-start(bf16[80,24,576]{2,1,0:T(8,128)(2,1)} %fusion.2), calls=%async_computation.1 | async-start | bytes 4915200 | tf_op jit(solution)/shard_map/all_to_all | solution.py:269
  39.5 1.5 %collective-permute-start.3 = (bf16[576,512]{1,0:T(8,128)(2,1)}, bf16[576,512]{1,0:T(8,128)(2,1)}, u32[]{:S(2)}, u32[]{:S(2)}) collective-permute-start(bf16[576,512]{1,0:T(8,128)(2,1)} %bitcast.14.refs_0_), channel_id=1, source_target_pairs={{0,32},{32,64},{64,96},{96,0},{1,33},{33,65},{65,97},{97,1},{2,34}... | collective-permute-start | bytes 1769480 | tf_op jit(solution)/shard_map/ppermute | solution.py:256
  41.0 1.7 %collective-permute-start.4 = (bf16[576,512]{1,0:T(8,128)(2,1)}, bf16[576,512]{1,0:T(8,128)(2,1)}, u32[]{:S(2)}, u32[]{:S(2)}) collective-permute-start(bf16[576,512]{1,0:T(8,128)(2,1)} %bitcast.36), channel_id=1, source_target_pairs={{0,96},{32,0},{64,32},{96,64},{1,97},{33,1},{65,33},{97,65},{2,98}... | collective-permute-start | bytes 1769480 | tf_op jit(solution)/shard_map/ppermute | solution.py:256
  43.0 3.0 %collective-permute-start.2 = (bf16[576,512]{1,0:T(8,128)(2,1)}, bf16[576,512]{1,0:T(8,128)(2,1)}, u32[]{:S(2)}, u32[]{:S(2)}) collective-permute-start(bf16[576,512]{1,0:T(8,128)(2,1)} %bitcast.14.refs_0_), channel_id=1, source_target_pairs={{0,96},{32,0},{64,32},{96,64},{1,97},{33,1},{65,33},{97,65},{2,98}... | collective-permute-start | bytes 1769480 | tf_op jit(solution)/shard_map/ppermute | solution.py:256
  46.0 6.3 %prefix_attend.4 = (f32[1152,256]{1,0:T(8,128)}, f32[1152,512]{1,0:T(8,128)}) custom-call(bf16[1152,576]{1,0:T(8,128)(2,1)} %pad_maximum_fusion.q_ref, bf16[576,512]{1,0:T(8,128)(2,1)} %bitcast.14.refs_0_, bf16[576,512]{1,0:T(8,128)(2,1)} %bitcast.38), custom_call_target="tpu_custom_call" | custom-call | tf_op jit(solution)/shard_map/prefix_attend/pallas_call | solution.py:113
  52.2 4.9 %collective-permute-done.3.refs_0_ = bf16[576,512]{1,0:T(8,128)(2,1)} collective-permute-done((bf16[576,512]{1,0:T(8,128)(2,1)}, bf16[576,512]{1,0:T(8,128)(2,1)}, u32[]{:S(2)}, u32[]{:S(2)}) %collective-permute-start.3) | collective-permute-done | bytes 589856 | tf_op jit(solution)/shard_map/ppermute | solution.py:256
  59.0 1.7 %collective-permute-start.6 = (bf16[576,512]{1,0:T(8,128)(2,1)}, bf16[576,512]{1,0:T(8,128)(2,1)}, u32[]{:S(2)}, u32[]{:S(2)}) collective-permute-start(bf16[576,512]{1,0:T(8,128)(2,1)} %collective-permute-done.4.refs_1_), channel_id=1, source_target_pairs={{0,96},{32,0},{64,32},{96,64},{1,97},{33,1},{65,33},{97,65},{2,98}... | collective-permute-start | bytes 1769480 | tf_op jit(solution)/shard_map/ppermute | solution.py:256
  61.3 7.6 %prefix_attend.5 = (f32[1152,256]{1,0:T(8,128)}, f32[1152,512]{1,0:T(8,128)}) custom-call(bf16[1152,576]{1,0:T(8,128)(2,1)} %pad_maximum_fusion.q_ref, bf16[576,512]{1,0:T(8,128)(2,1)} %collective-permute-done.3.refs_0_, bf16[576,512]{1,0:T(8,128)(2,1)} %collective-permute-done.4.refs_1_, f32[1152,256]{1,0:T(8,128)} %get-tuple-element.35.refs_2_, ...), custom_call_target="tpu_custom_call" | custom-call | tf_op jit(solution)/shard_map/prefix_attend/pallas_call | solution.py:113
  69.0 5.5 %tail_attend.1 = bf16[16,5,8,640]{3,2,1,0:T(8,128)(2,1)} custom-call(s32[5]{0:T(128)} %pad_dynamic-slice_fusion.length_ref, bf16[16,5,24,576]{3,2,1,0:T(8,128)(2,1)} %bitcast.15.joined_ref), custom_call_target="tpu_custom_call" | custom-call | tf_op jit(solution)/shard_map/tail_attend/pallas_call | solution.py:149
  74.5 7.1 %all-to-all-start.2 = ((bf16[80,8,640]{2,1,0:T(8,128)(2,1)}), bf16[80,8,640]{2,1,0:T(8,128)(2,1)S(1)}, u32[]{:S(2)}, u32[]{:S(2)}) async-start(bf16[80,8,640]{2,1,0:T(8,128)(2,1)} %bitcast.32), calls=%async_computation.2 | async-start | bytes 1638400 | tf_op jit(solution)/shard_map/all_to_all | solution.py:269
  82.5 6.9 %prefix_attend.7 = bf16[576,640]{1,0:T(8,128)(2,1)} custom-call(bf16[576,576]{1,0:T(8,128)(2,1)} %copy-done.3, bf16[576,512]{1,0:T(8,128)(2,1)} %copy-done.4, bf16[576,512]{1,0:T(8,128)(2,1)} %collective-permute-done.2.refs_1_, bf16[576,512]{1,0:T(8,128)(2,1)} %collective-permute-done.5.refs_2_, bf16[576,512]{1,0:T(8,128)(2,1)} %collective-permute-done.6.refs_3_, ...), custom_call_target="tpu_custom_call" | custom-call | tf_op jit(solution)/shard_map/prefix_attend/pallas_call | solution.py:113
  90.4 6.9 %prefix_attend.6.own_ref = bf16[576,640]{1,0:T(8,128)(2,1)} custom-call(bf16[576,576]{1,0:T(8,128)(2,1)} %bitcast.31, bf16[576,512]{1,0:T(8,128)(2,1)} %copy-done.4, bf16[576,512]{1,0:T(8,128)(2,1)} %collective-permute-done.2.refs_1_, bf16[576,512]{1,0:T(8,128)(2,1)} %collective-permute-done.5.refs_2_, bf16[576,512]{1,0:T(8,128)(2,1)} %collective-permute-done.6.refs_3_, ...), custom_call_target="tpu_custom_call" | custom-call | tf_op jit(solution)/shard_map/prefix_attend/pallas_call | solution.py:113
  98.4 9.2 %finish.1 = (bf16[8,72,448]{2,1,0:T(8,128)(2,1)}, bf16[8,72,448]{2,1,0:T(8,128)(2,1)}) custom-call(s32[1]{0:T(128)} %bitcast.core_ref, s32[8]{0:T(128)} %stack.35.order_ref, bf16[576,640]{1,0:T(8,128)(2,1)} %prefix_attend.6.own_ref, bf16[576,640]{1,0:T(8,128)(2,1)} %copy-done.7, bf16[640,640]{1,0:T(8,128)(2,1)} %bitcast.33, bf16[8,512,128]{2,1,0:T(8,128)(2,1)} %up_ref.1, ...), custom_call_target="tpu_custom_call" | custom-call | tf_op jit(solution)/shard_map/finish/pallas_call | solution.py:218
  107.8 2.1 %collective-permute-done.8 = bf16[8,72,448]{2,1,0:T(8,128)(2,1)S(1)} collective-permute-done((bf16[8,72,448]{2,1,0:T(8,128)(2,1)}, bf16[8,72,448]{2,1,0:T(8,128)(2,1)S(1)}, u32[]{:S(2)}, u32[]{:S(2)}) %collective-permute-start.8) | collective-permute-done | bytes 516128 | tf_op jit(solution)/shard_map/ppermute | solution.py:259
  111.1 3.3 %collective-permute-start.10 = (bf16[2,72,448]{2,1,0:T(8,128)(2,1)S(1)}, bf16[2,72,448]{2,1,0:T(8,128)(2,1)S(1)}, u32[]{:S(2)}, u32[]{:S(2)}) collective-permute-start(bf16[2,72,448]{2,1,0:T(8,128)(2,1)S(1)} %get-tuple-element.51), channel_id=1, source_target_pairs={{0,4},{2,6},{4,0},{6,2},{1,5},{3,7},{5,1},{7,3},{8,12},{10,14},{12... | collective-permute-start | bytes 387080 | tf_op jit(solution)/shard_map/ppermute | solution.py:256
  116.4 3.0 %collective-permute-done.10 = bf16[2,72,448]{2,1,0:T(8,128)(2,1)S(1)} collective-permute-done((bf16[2,72,448]{2,1,0:T(8,128)(2,1)S(1)}, bf16[2,72,448]{2,1,0:T(8,128)(2,1)S(1)}, u32[]{:S(2)}, u32[]{:S(2)}) %collective-permute-start.10) | collective-permute-done | bytes 129056 | tf_op jit(solution)/shard_map/ppermute | solution.py:256
  119.3 2.8 %collective-permute-done.11 = bf16[2,72,448]{2,1,0:T(8,128)(2,1)S(1)} collective-permute-done((bf16[2,72,448]{2,1,0:T(8,128)(2,1)S(1)}, bf16[2,72,448]{2,1,0:T(8,128)(2,1)S(1)}, u32[]{:S(2)}, u32[]{:S(2)}) %collective-permute-start.11) | collective-permute-done | bytes 129056 | tf_op jit(solution)/shard_map/ppermute | solution.py:256
  123.4 3.2 %collective-permute-start.12 = (bf16[72,448]{1,0:T(8,128)(2,1)S(1)}, bf16[72,448]{1,0:T(8,128)(2,1)S(1)}, u32[]{:S(2)}, u32[]{:S(2)}) collective-permute-start(bf16[72,448]{1,0:T(8,128)(2,1)S(1)} %fusion.7), channel_id=1, source_target_pairs={{0,8},{8,0},{1,9},{9,1},{2,10},{10,2},{3,11},{11,3},{4,12},{12,4},... | collective-permute-start | bytes 193544 | tf_op jit(solution)/shard_map/ppermute | solution.py:256
  126.6 2.8 %collective-permute-done.12 = bf16[72,448]{1,0:T(8,128)(2,1)S(1)} collective-permute-done((bf16[72,448]{1,0:T(8,128)(2,1)S(1)}, bf16[72,448]{1,0:T(8,128)(2,1)S(1)}, u32[]{:S(2)}, u32[]{:S(2)}) %collective-permute-start.12) | collective-permute-done | bytes 64544 | tf_op jit(solution)/shard_map/ppermute | solution.py:256
  (56 shorter events, 18.3 us)
Async XLA Ops:
  0.0 10.6 %copy-start = (bf16[576,1536]{1,0:T(8,128)(2,1)S(1)}, bf16[576,1536]{1,0:T(8,128)(2,1)}, u32[]{:S(2)}) copy-start(bf16[576,1536]{1,0:T(8,128)(2,1)} %param.8) | copy-start | bytes 5308420
  0.0 10.6 %copy-start.8 = (s32[72]{0:T(128)S(1)}, s32[72]{0:T(128)}, u32[]{:S(2)}) copy-start(s32[72]{0:T(128)} %param.12) | copy-start | bytes 868
  2.3 9.5 %copy-start.6 = (bf16[8,128,512]{2,1,0:T(8,128)(2,1)S(1)}, bf16[8,128,512]{2,1,0:T(8,128)(2,1)}, u32[]{:S(2)}) copy-start(bf16[8,128,512]{2,1,0:T(8,128)(2,1)} %param.13) | copy-start | bytes 3145732
  2.3 29.2 %all-to-all-start = ((bf16[16,64,576]{2,1,0:T(8,128)(2,1)}), bf16[16,64,576]{2,1,0:T(8,128)(2,1)}, u32[]{:S(2)}, u32[]{:S(2)}) async-start(bf16[16,64,576]{2,1,0:T(8,128)(2,1)} %broadcast_in_dim.21), calls=%async_computation | async-start | bytes 2621440 | tf_op jit(solution)/shard_map/all_to_all | solution.py:291
  11.8 1.4 %copy-start.5 = (bf16[72,16,576]{2,1,0:T(8,128)(2,1)S(1)}, bf16[72,16,576]{2,1,0:T(8,128)(2,1)}, u32[]{:S(2)}) copy-start(bf16[72,16,576]{2,1,0:T(8,128)(2,1)} %param.10) | copy-start | bytes 3981316
  13.2 5.2 %copy-start.1 = (bf16[72,8,576]{2,1,0:T(8,128)(2,1)}, bf16[72,8,576]{2,1,0:T(8,128)(2,1)S(1)}, u32[]{:S(2)}) copy-start(bf16[72,8,576]{2,1,0:T(8,128)(2,1)S(1)} %copy.20) | copy-start | bytes 1990660
  14.8 2.2 %collective-permute-start = (bf16[576,576]{1,0:T(8,128)(2,1)S(1)}, bf16[576,576]{1,0:T(8,128)(2,1)S(1)}, u32[]{:S(2)}, u32[]{:S(2)}) collective-permute-start(bf16[576,576]{1,0:T(8,128)(2,1)S(1)} %bitcast.29), channel_id=1, source_target_pairs={{0,1},{1,0},{2,3},{3,2},{4,5},{5,4},{6,7},{7,6},{8,9},{9,8},{10,11... | collective-permute-start | bytes 1990664 | tf_op jit(solution)/shard_map/ppermute | solution.py:259
  17.0 14.4 %copy-start.3 = (bf16[576,576]{1,0:T(8,128)(2,1)}, bf16[576,576]{1,0:T(8,128)(2,1)S(1)}, u32[]{:S(2)}) copy-start(bf16[576,576]{1,0:T(8,128)(2,1)S(1)} %collective-permute-done.q_ref) | copy-start | bytes 1990660
  31.5 37.6 %all-to-all-start.1 = ((bf16[80,24,576]{2,1,0:T(8,128)(2,1)}), bf16[80,24,576]{2,1,0:T(8,128)(2,1)}, u32[]{:S(2)}, u32[]{:S(2)}) async-start(bf16[80,24,576]{2,1,0:T(8,128)(2,1)} %fusion.2), calls=%async_computation.1 | async-start | bytes 4915200 | tf_op jit(solution)/shard_map/all_to_all | solution.py:269
  37.3 23.4 %copy-start.9 = (s32[72]{0:T(128)S(1)}, s32[72]{0:T(128)}, u32[]{:S(2)}) copy-start(s32[72]{0:T(128)} %param.11) | copy-start | bytes 868
  39.5 17.7 %collective-permute-start.3 = (bf16[576,512]{1,0:T(8,128)(2,1)}, bf16[576,512]{1,0:T(8,128)(2,1)}, u32[]{:S(2)}, u32[]{:S(2)}) collective-permute-start(bf16[576,512]{1,0:T(8,128)(2,1)} %bitcast.14.refs_0_), channel_id=1, source_target_pairs={{0,32},{32,64},{64,96},{96,0},{1,33},{33,65},{65,97},{97,1},{2,34}... | collective-permute-start | bytes 1769480 | tf_op jit(solution)/shard_map/ppermute | solution.py:256
  41.0 16.5 %collective-permute-start.4 = (bf16[576,512]{1,0:T(8,128)(2,1)}, bf16[576,512]{1,0:T(8,128)(2,1)}, u32[]{:S(2)}, u32[]{:S(2)}) collective-permute-start(bf16[576,512]{1,0:T(8,128)(2,1)} %bitcast.36), channel_id=1, source_target_pairs={{0,96},{32,0},{64,32},{96,64},{1,97},{33,1},{65,33},{97,65},{2,98}... | collective-permute-start | bytes 1769480 | tf_op jit(solution)/shard_map/ppermute | solution.py:256
  42.7 38.9 %collective-permute-start.1 = (bf16[576,512]{1,0:T(8,128)(2,1)}, bf16[576,512]{1,0:T(8,128)(2,1)S(1)}, u32[]{:S(2)}, u32[]{:S(2)}) collective-permute-start(bf16[576,512]{1,0:T(8,128)(2,1)} %bitcast.37), channel_id=1, source_target_pairs={{0,32},{32,64},{64,96},{96,0},{1,33},{33,65},{65,97},{97,1},{2,34}... | collective-permute-start | bytes 1769480 | tf_op jit(solution)/shard_map/ppermute | solution.py:256
  43.0 38.6 %collective-permute-start.2 = (bf16[576,512]{1,0:T(8,128)(2,1)}, bf16[576,512]{1,0:T(8,128)(2,1)}, u32[]{:S(2)}, u32[]{:S(2)}) collective-permute-start(bf16[576,512]{1,0:T(8,128)(2,1)} %bitcast.14.refs_0_), channel_id=1, source_target_pairs={{0,96},{32,0},{64,32},{96,64},{1,97},{33,1},{65,33},{97,65},{2,98}... | collective-permute-start | bytes 1769480 | tf_op jit(solution)/shard_map/ppermute | solution.py:256
  57.5 24.3 %collective-permute-start.5 = (bf16[576,512]{1,0:T(8,128)(2,1)}, bf16[576,512]{1,0:T(8,128)(2,1)}, u32[]{:S(2)}, u32[]{:S(2)}) collective-permute-start(bf16[576,512]{1,0:T(8,128)(2,1)} %collective-permute-done.3.refs_0_), channel_id=1, source_target_pairs={{0,32},{32,64},{64,96},{96,0},{1,33},{33,65},{65,97},{97,1},{2,34}... | collective-permute-start | bytes 1769480 | tf_op jit(solution)/shard_map/ppermute | solution.py:256
  59.0 22.8 %collective-permute-start.6 = (bf16[576,512]{1,0:T(8,128)(2,1)}, bf16[576,512]{1,0:T(8,128)(2,1)}, u32[]{:S(2)}, u32[]{:S(2)}) collective-permute-start(bf16[576,512]{1,0:T(8,128)(2,1)} %collective-permute-done.4.refs_1_), channel_id=1, source_target_pairs={{0,96},{32,0},{64,32},{96,64},{1,97},{33,1},{65,33},{97,65},{2,98}... | collective-permute-start | bytes 1769480 | tf_op jit(solution)/shard_map/ppermute | solution.py:256
  74.5 22.8 %all-to-all-start.2 = ((bf16[80,8,640]{2,1,0:T(8,128)(2,1)}), bf16[80,8,640]{2,1,0:T(8,128)(2,1)S(1)}, u32[]{:S(2)}, u32[]{:S(2)}) async-start(bf16[80,8,640]{2,1,0:T(8,128)(2,1)} %bitcast.32), calls=%async_computation.2 | async-start | bytes 1638400 | tf_op jit(solution)/shard_map/all_to_all | solution.py:269
  89.4 8.0 %collective-permute-start.7 = (bf16[576,640]{1,0:T(8,128)(2,1)}, bf16[576,640]{1,0:T(8,128)(2,1)S(1)}, u32[]{:S(2)}, u32[]{:S(2)}) collective-permute-start(bf16[576,640]{1,0:T(8,128)(2,1)} %prefix_attend.7), channel_id=1, source_target_pairs={{0,1},{1,0},{2,3},{3,2},{4,5},{5,4},{6,7},{7,6},{8,9},{9,8},{10,11... | collective-permute-start | bytes 2211848 | tf_op jit(solution)/shard_map/ppermute | solution.py:259
  97.3 1.1 copy-start.2
  107.6 2.3 %collective-permute-start.8 = (bf16[8,72,448]{2,1,0:T(8,128)(2,1)}, bf16[8,72,448]{2,1,0:T(8,128)(2,1)S(1)}, u32[]{:S(2)}, u32[]{:S(2)}) collective-permute-start(bf16[8,72,448]{2,1,0:T(8,128)(2,1)} %get-tuple-element.46), channel_id=1, source_target_pairs={{0,1},{1,0},{2,3},{3,2},{4,5},{5,4},{6,7},{7,6},{8,9},{9,8},{10,11... | collective-permute-start | bytes 1548296 | tf_op jit(solution)/shard_map/ppermute | solution.py:259
  111.1 8.3 %collective-permute-start.10 = (bf16[2,72,448]{2,1,0:T(8,128)(2,1)S(1)}, bf16[2,72,448]{2,1,0:T(8,128)(2,1)S(1)}, u32[]{:S(2)}, u32[]{:S(2)}) collective-permute-start(bf16[2,72,448]{2,1,0:T(8,128)(2,1)S(1)} %get-tuple-element.51), channel_id=1, source_target_pairs={{0,4},{2,6},{4,0},{6,2},{1,5},{3,7},{5,1},{7,3},{8,12},{10,14},{12... | collective-permute-start | bytes 387080 | tf_op jit(solution)/shard_map/ppermute | solution.py:256
  114.4 7.8 %collective-permute-start.11 = (bf16[2,72,448]{2,1,0:T(8,128)(2,1)S(1)}, bf16[2,72,448]{2,1,0:T(8,128)(2,1)S(1)}, u32[]{:S(2)}, u32[]{:S(2)}) collective-permute-start(bf16[2,72,448]{2,1,0:T(8,128)(2,1)S(1)} %get-tuple-element.50), channel_id=1, source_target_pairs={{0,6},{2,0},{4,2},{6,4},{1,7},{3,1},{5,3},{7,5},{8,14},{10,8},{12,... | collective-permute-start | bytes 387080 | tf_op jit(solution)/shard_map/ppermute | solution.py:256
  115.5 6.9 %collective-permute-start.9 = (bf16[2,72,448]{2,1,0:T(8,128)(2,1)S(1)}, bf16[2,72,448]{2,1,0:T(8,128)(2,1)S(1)}, u32[]{:S(2)}, u32[]{:S(2)}) collective-permute-start(bf16[2,72,448]{2,1,0:T(8,128)(2,1)S(1)} %get-tuple-element.49), channel_id=1, source_target_pairs={{0,2},{2,4},{4,6},{6,0},{1,3},{3,5},{5,7},{7,1},{8,10},{10,12},{12... | collective-permute-start | bytes 387080 | tf_op jit(solution)/shard_map/ppermute | solution.py:256
  123.4 5.9 %collective-permute-start.12 = (bf16[72,448]{1,0:T(8,128)(2,1)S(1)}, bf16[72,448]{1,0:T(8,128)(2,1)S(1)}, u32[]{:S(2)}, u32[]{:S(2)}) collective-permute-start(bf16[72,448]{1,0:T(8,128)(2,1)S(1)} %fusion.7), channel_id=1, source_target_pairs={{0,8},{8,0},{1,9},{9,1},{2,10},{10,2},{3,11},{11,3},{4,12},{12,4},... | collective-permute-start | bytes 193544 | tf_op jit(solution)/shard_map/ppermute | solution.py:256
  (2 other events, 1.8 us)
